TPU v7x, 32 devices: a whole 2x2x4 slice. The times are simulated.
32 devices in a mesh: dp: 4 (over x, core), ctx: 4 (over z), rep: 2 (over y).
Axes of the slice: x: 2, y: 2, z: 4, core: 2. Of those that a mesh axis runs over, the one named last changes fastest.
Arguments:
- inputs: bfloat16 [4, 1024, 4096], P('dp', ('ctx', 'rep')), may hold values from -6 to 6
- queries: bfloat16 [4, 1024, 2048], P('dp', ('ctx', 'rep')), may hold values from -24 to 24
- keys: bfloat16 [4, 1024, 512], P('dp', ('ctx', 'rep')), may hold values from -24 to 24
- values: bfloat16 [4, 1024, 512], P('dp', ('ctx', 'rep')), may hold values from -6 to 6
- grad_out: bfloat16 [4, 1024, 2048], P('dp', ('ctx', 'rep')), may hold values from -0.125 to 0.125
- doc_ids: int32 [4, 1024], P('dp', ('ctx', 'rep')), may hold values from 0 to 31, never falling along the last dimension, each value on 1 to 128 neighbouring positions
- plan: int32 [4, 32], P('dp', ('ctx', 'rep')), may hold values from 0 to 3, as said below
Outputs:
- placed_out: bfloat16 [4, 1024, 2048], P('dp', ('ctx', 'rep'))
- weight_grad: float32 [4096, 512], P('ctx')
Inputs may be any that keep to these rules, and one draw needn't show every extreme that they name: `doc_ids`: ids never fall along a micro-batch; a document holds at most 128 positions. `plan`: for one sequence shard, the 4 blocks of a micro-batch go to 4 different micro-batches (itself possibly), and every micro-batch receives exactly one block of each local block index.
All inputs are finite; a program needn't handle non-finite values.
Results may differ from a plain program's by a relative error of at most 0.017.
Values may be sent and summed in bfloat16 or wider, within the bound.
No kernel may reach another device: no remote copies, remote signals or barrier semaphores. Data moves between devices by JAX's collectives and lax.ppermute only.
A program may use at most 64 MiB of HBM per device.

v0:
```python
import math

import jax
import jax.numpy as jnp
from jax import lax
from jax.sharding import PartitionSpec as P

HEAD_DIM = 128
KV_HEADS = 4
GROUP = 4


def from_behind(value, axis, by):
    devices = lax.axis_size(axis)
    pairs = [(i, i + by) for i in range(devices) if 0 <= i + by < devices]
    return lax.ppermute(value, axis, pairs)


def block_attention(query_rows, key_rows, query_docs, key_docs, query_pos, key_pos):
    count_q = query_rows.shape[0]
    count_k = key_rows.shape[0]
    queries4 = query_rows.reshape(count_q, KV_HEADS, GROUP, HEAD_DIM)
    keys3 = key_rows.reshape(count_k, KV_HEADS, HEAD_DIM)
    scores = jnp.einsum("tgrd,ugd->grtu", queries4, keys3, preferred_element_type=jnp.float32) * (
        1.0 / math.sqrt(HEAD_DIM)
    )
    allowed = (query_docs[:, None] == key_docs[None, :]) & (key_pos[None, :] <= query_pos[:, None])
    scores = jnp.where(allowed, scores, -jnp.inf)
    row_max = jnp.max(scores, axis=-1, keepdims=True)
    exponent = jnp.exp(scores - row_max)
    row_sum = jnp.sum(exponent, axis=-1, keepdims=True)
    probabilities = (exponent / row_sum).astype(jnp.bfloat16)
    return (probabilities, row_max, row_sum)


def local(inputs, queries, keys, values, grad_out, doc_ids, plan):
    token_count = inputs.shape[1]
    q_width = queries.shape[2]
    kv_width = keys.shape[2]
    input_rows = inputs[0]
    query_rows = queries[0]
    key_rows = keys[0]
    value_rows = values[0]
    grad_rows = grad_out[0]
    row_docs = doc_ids[0]
    shard_index = lax.axis_index(("ctx", "rep"))
    query_pos = shard_index * token_count + jnp.arange(token_count, dtype=jnp.int32)
    prior_keys, prior_values, prior_docs = from_behind(
        (key_rows, value_rows, row_docs + 1), ("ctx", "rep"), 1
    )
    keys_all = jnp.concatenate([prior_keys, key_rows], 0)
    values_all = jnp.concatenate([prior_values, value_rows], 0)
    docs_all = jnp.concatenate([prior_docs - 1, row_docs], 0)
    pos_all = jnp.concatenate([query_pos - token_count, query_pos], 0)
    probabilities, row_max, row_sum = block_attention(
        query_rows, keys_all, row_docs, docs_all, query_pos, pos_all
    )
    values3 = values_all.reshape(2 * token_count, KV_HEADS, HEAD_DIM)
    attended = jnp.einsum(
        "grtu,ugd->tgrd", probabilities, values3, preferred_element_type=jnp.float32
    ).astype(jnp.bfloat16)
    attended = attended.reshape(token_count, q_width)
    owner_count = lax.axis_size("dp")
    block_count = plan.shape[1]
    block_rows = token_count // block_count
    targets = plan[0]
    owner_index = jnp.arange(owner_count, dtype=jnp.int32)
    chosen = owner_index[:, None] == targets[None, :]
    pieces = attended.reshape(block_count, block_rows, q_width)
    outgoing = jnp.einsum(
        "pi,ibf->pbf", chosen.astype(jnp.bfloat16), pieces, preferred_element_type=jnp.float32
    ).astype(jnp.bfloat16)
    block_labels = jnp.sum(
        chosen.astype(jnp.int32) * (jnp.arange(block_count, dtype=jnp.int32)[None, :] + 1),
        axis=1,
        keepdims=True,
    )
    arrived, arrived_labels = (
        lax.all_to_all(outgoing, "dp", split_axis=0, concat_axis=0, tiled=True),
        lax.all_to_all(block_labels, "dp", split_axis=0, concat_axis=0, tiled=True),
    )
    matched = arrived_labels[:, 0][None, :] == jnp.arange(block_count, dtype=jnp.int32)[:, None] + 1
    placed = jnp.einsum(
        "ip,pbf->ibf", matched.astype(jnp.bfloat16), arrived, preferred_element_type=jnp.float32
    ).astype(jnp.bfloat16)
    placed = placed.reshape(1, token_count, q_width)
    grads4 = grad_rows.reshape(token_count, KV_HEADS, GROUP, HEAD_DIM)
    value_grad = jnp.einsum(
        "grtu,tgrd->ugd", probabilities, grads4, preferred_element_type=jnp.float32
    )
    value_grad = value_grad.reshape(2 * token_count, kv_width)
    returned = from_behind(
        value_grad[:token_count].astype(jnp.bfloat16), ("ctx", "rep"), -1
    ).astype(jnp.float32)
    grad_values = (value_grad[token_count:] + returned).astype(jnp.bfloat16)
    partial_grad = lax.psum_scatter(
        jnp.einsum("tc,tf->cf", input_rows, grad_values, preferred_element_type=jnp.float32).astype(
            jnp.bfloat16
        ),
        "ctx",
        scatter_dimension=0,
        tiled=True,
    ).astype(jnp.float32)
    weight_grad = lax.psum(partial_grad, ("dp", "rep"))
    return (placed, weight_grad)


def solution(mesh):
    in_specs = (
        P("dp", ("ctx", "rep"), None),
        P("dp", ("ctx", "rep"), None),
        P("dp", ("ctx", "rep"), None),
        P("dp", ("ctx", "rep"), None),
        P("dp", ("ctx", "rep"), None),
        P("dp", ("ctx", "rep")),
        P("dp", ("ctx", "rep")),
    )
    out_specs = (P("dp", ("ctx", "rep"), None), P("ctx", None))
    return jax.shard_map(local, mesh=mesh, in_specs=in_specs, out_specs=out_specs, check_vma=False)
```

profile of v0, /device:TPU:0, one launch (start us, length us, event | category | flops | bytes accessed | tf_op | source)
XLA Modules:
  0.0 208.9 jit_solution(2452693672353760981)
XLA Ops:
  7.2 0.7 broadcast_add_fusion.2
  8.0 4.9 %collective-permute-start.1 = (s32[128]{0:T(128)S(1)}, s32[128]{0:T(128)S(1)}, u32[]{:S(2)}, u32[]{:S(2)}) collective-permute-start(s32[128]{0:T(128)S(1)} %broadcast_add_fusion.2), channel_id=1, source_target_pairs={{0,1},{1,2},{2,3},{3,4},{4,5},{5,6},{6,7},{8,9},{9,10},{10,11},{11... | collective-permute-start | bytes 1544 | tf_op jit(solution)/shard_map/ppermute | solution.py:16
  12.8 1.0 copy.49
  13.9 3.4 %collective-permute-start.2 = (bf16[128,512]{0,1:T(8,128)(2,1)S(1)}, bf16[128,512]{0,1:T(8,128)(2,1)S(1)}, u32[]{:S(2)}, u32[]{:S(2)}) collective-permute-start(bf16[128,512]{0,1:T(8,128)(2,1)S(1)} %bitcast.64), channel_id=1, source_target_pairs={{0,1},{1,2},{2,3},{3,4},{4,5},{5,6},{6,7},{8,9},{9,10},{10,11},{11... | collective-permute-start | bytes 393224 | tf_op jit(solution)/shard_map/ppermute | solution.py:16
  17.5 1.4 reshape_squeeze.6
  18.9 1.3 copy.68
  20.6 2.1 %fusion.36 = (f32[4,4,128]{2,1,0:T(4,128)S(1)}, f32[4,4,128,256]{2,3,1,0:T(8,128)}) fusion(pred[128,256]{0,1:T(8,128)(4,1)S(1)} %compare_and_fusion, bf16[128,4,4,128]{3,2,1,0:T(4,128)(2,1)S(1)} %reshape_squeeze.6, bf16[128,4,128]{2,0,1:T(8,128)(2,1)S(1)} %copy.52, bf16[128,4,128]{2,0,1:T(8,128)(2,1)S(1)} %copy.51), kind=kOutput, calls=%fused_computation.50 | convolution fusion | flops 136839424 | bytes 2924544 | tf_op jit(solution)/shard_map/sub | solution.py:30
  22.7 2.1 convolution_bitcast_fusion
  24.8 1.3 collective-permute-start.3
  26.1 5.5 %collective-permute-done.3 = bf16[128,512]{0,1:T(8,128)(2,1)S(1)} collective-permute-done((bf16[128,512]{0,1:T(8,128)(2,1)S(1)}, bf16[128,512]{0,1:T(8,128)(2,1)S(1)}, u32[]{:S(2)}, u32[]{:S(2)}) %collective-permute-start.3) | collective-permute-done | bytes 131104 | tf_op jit(solution)/shard_map/ppermute | solution.py:16
  31.7 3.2 %fusion.1 = bf16[4096,512]{0,1:T(8,128)(2,1)} fusion(bf16[128,512]{0,1:T(8,128)(2,1)S(1)} %fusion.16, bf16[1,128,4096]{2,1,0:T(8,128)(2,1)S(1)} %copy-done), kind=kOutput, calls=%fused_computation.2 | convolution fusion | flops 538968064 | bytes 5373952 | tf_op jit(solution)/shard_map/tc,tf->cf/dot_general | solution.py:97
  34.9 0.9 copy-done.1
  35.8 4.6 %collective-permute-start = (bf16[128,512]{1,0:T(8,128)(2,1)S(1)}, bf16[128,512]{1,0:T(8,128)(2,1)S(1)}, u32[]{:S(2)}, u32[]{:S(2)}) collective-permute-start(bf16[128,512]{1,0:T(8,128)(2,1)S(1)} %bitcast.66), channel_id=1, source_target_pairs={{0,1},{1,2},{2,3},{3,4},{4,5},{5,6},{6,7},{8,9},{9,10},{10,11},{11... | collective-permute-start | bytes 393224 | tf_op jit(solution)/shard_map/ppermute | solution.py:16
  40.5 0.7 copy.46
  41.2 3.2 %all-to-all-start = ((s32[4,1,1]{2,1,0:T(1,128)}), s32[4,1,1]{2,1,0:T(1,128)S(1)}, u32[]{:S(2)}, u32[]{:S(2)}) async-start(s32[4,1,1]{2,1,0:T(1,128)} %copy.46), calls=%async_computation | async-start | bytes 4096 | tf_op jit(solution)/shard_map/all_to_all | solution.py:80
  44.6 1.9 fusion.3
  47.9 1.1 copy.57
  49.0 3.5 %all-to-all-start.1 = ((bf16[4,32,2048]{2,1,0:T(8,128)(2,1)}), bf16[4,32,2048]{2,1,0:T(8,128)(2,1)S(1)}, u32[]{:S(2)}, u32[]{:S(2)}) async-start(bf16[4,32,2048]{2,1,0:T(8,128)(2,1)} %copy.57), calls=%async_computation.1 | async-start | bytes 1048576 | tf_op jit(solution)/shard_map/all_to_all | solution.py:79
  52.6 8.7 %all-to-all-done.1 = bf16[4,32,2048]{2,1,0:T(8,128)(2,1)S(1)} async-done(((bf16[4,32,2048]{2,1,0:T(8,128)(2,1)}), bf16[4,32,2048]{2,1,0:T(8,128)(2,1)S(1)}, u32[]{:S(2)}, u32[]{:S(2)}) %all-to-all-start.1) | async-done | bytes 524320 | tf_op jit(solution)/shard_map/all_to_all | solution.py:79
  61.3 0.5 convolution_convert_fusion.1
  61.9 1.1 copy.59
  62.9 50.4 %reduce-scatter.2.cloned.1.call-done = bf16[1024,512]{0,1:T(8,128)(2,1)} async-done(((bf16[4096,512]{0,1:T(8,128)(2,1)}), bf16[1024,512]{0,1:T(8,128)(2,1)}) %reduce-scatter.2.cloned.1.call-update) | async-done | bytes 1048592 | tf_op jit(solution)/shard_map/reduce_scatter | solution.py:96
  113.3 86.9 %all-reduce.1 = f32[1024,512]{0,1:T(8,128)S(1)} all-reduce(bf16[1024,512]{0,1:T(8,128)(2,1)} %reduce-scatter.2.cloned.1.call-done), channel_id=1, replica_groups=mesh['dp'=4,'ctx'=4,'rep'=2] {'dp','rep'}, use_global_device_ids=true, to_apply=%region_4.5 | all-reduce | flops 524288 | bytes 3145728 | tf_op jit(solution)/shard_map/psum | solution.py:104
  200.2 1.8 copy.62
  (32 shorter events, 2.4 us)
Async XLA Ops:
  7.2 24.5 %copy-start = (bf16[1,128,4096]{2,1,0:T(8,128)(2,1)S(1)}, bf16[1,128,4096]{2,1,0:T(8,128)(2,1)}, u32[]{:S(2)}) copy-start(bf16[1,128,4096]{2,1,0:T(8,128)(2,1)} %param.7) | copy-start | bytes 3145732
  7.2 13.1 %copy-start.2 = (s32[1,128]{1,0:T(1,128)S(1)}, s32[1,128]{1,0:T(1,128)}, u32[]{:S(2)}) copy-start(s32[1,128]{1,0:T(1,128)} %param.12) | copy-start | bytes 1540
  7.2 106.1 %reduce-scatter.2.cloned.1.call-start = ((), (), s32[]{:S(2)}) async-start(), calls=%async_computation.3 | async-start | bytes 5242880 | tf_op jit(solution)/shard_map/reduce_scatter | solution.py:96
  8.0 12.3 %collective-permute-start.1 = (s32[128]{0:T(128)S(1)}, s32[128]{0:T(128)S(1)}, u32[]{:S(2)}, u32[]{:S(2)}) collective-permute-start(s32[128]{0:T(128)S(1)} %broadcast_add_fusion.2), channel_id=1, source_target_pairs={{0,1},{1,2},{2,3},{3,4},{4,5},{5,6},{6,7},{8,9},{9,10},{10,11},{11... | collective-permute-start | bytes 1544 | tf_op jit(solution)/shard_map/ppermute | solution.py:16
  13.9 6.5 %collective-permute-start.2 = (bf16[128,512]{0,1:T(8,128)(2,1)S(1)}, bf16[128,512]{0,1:T(8,128)(2,1)S(1)}, u32[]{:S(2)}, u32[]{:S(2)}) collective-permute-start(bf16[128,512]{0,1:T(8,128)(2,1)S(1)} %bitcast.64), channel_id=1, source_target_pairs={{0,1},{1,2},{2,3},{3,4},{4,5},{5,6},{6,7},{8,9},{9,10},{10,11},{11... | collective-permute-start | bytes 393224 | tf_op jit(solution)/shard_map/ppermute | solution.py:16
  24.8 6.9 %collective-permute-start.3 = (bf16[128,512]{0,1:T(8,128)(2,1)S(1)}, bf16[128,512]{0,1:T(8,128)(2,1)S(1)}, u32[]{:S(2)}, u32[]{:S(2)}) collective-permute-start(bf16[128,512]{0,1:T(8,128)(2,1)S(1)} %bitcast.69), channel_id=1, source_target_pairs={{1,0},{2,1},{3,2},{4,3},{5,4},{6,5},{7,6},{9,8},{10,9},{11,10},{12... | collective-permute-start | bytes 393224 | tf_op jit(solution)/shard_map/ppermute | solution.py:16
  34.8 0.9 copy-start.1
  34.8 5.6 %copy-start.3 = (s32[1,4]{1,0:T(1,128)S(1)}, s32[1,4]{1,0:T(1,128)}, u32[]{:S(2)}) copy-start(s32[1,4]{1,0:T(1,128)} %param.13) | copy-start | bytes 52
  35.8 8.8 %collective-permute-start = (bf16[128,512]{1,0:T(8,128)(2,1)S(1)}, bf16[128,512]{1,0:T(8,128)(2,1)S(1)}, u32[]{:S(2)}, u32[]{:S(2)}) collective-permute-start(bf16[128,512]{1,0:T(8,128)(2,1)S(1)} %bitcast.66), channel_id=1, source_target_pairs={{0,1},{1,2},{2,3},{3,4},{4,5},{5,6},{6,7},{8,9},{9,10},{10,11},{11... | collective-permute-start | bytes 393224 | tf_op jit(solution)/shard_map/ppermute | solution.py:16
  41.2 7.8 %all-to-all-start = ((s32[4,1,1]{2,1,0:T(1,128)}), s32[4,1,1]{2,1,0:T(1,128)S(1)}, u32[]{:S(2)}, u32[]{:S(2)}) async-start(s32[4,1,1]{2,1,0:T(1,128)} %copy.46), calls=%async_computation | async-start | bytes 4096 | tf_op jit(solution)/shard_map/all_to_all | solution.py:80
  49.0 12.3 %all-to-all-start.1 = ((bf16[4,32,2048]{2,1,0:T(8,128)(2,1)}), bf16[4,32,2048]{2,1,0:T(8,128)(2,1)S(1)}, u32[]{:S(2)}, u32[]{:S(2)}) async-start(bf16[4,32,2048]{2,1,0:T(8,128)(2,1)} %copy.57), calls=%async_computation.1 | async-start | bytes 1048576 | tf_op jit(solution)/shard_map/all_to_all | solution.py:79
Sparse Core Ops, SparseCore 0:
  35.0 78.2 reduce-scatter.1
where the time goes:
time: 209 us
  blocking collectives  86.9 us (42%)
  waiting for transfers between devices  64.6 us (31%)
  starting transfers between devices  20.9 us (10%)
  between operations  14.3 us (7%)
  local copies, waits for them, and re-layouts  10.6 us (5%)
  matrix products  10.3 us (5%)
    psum x1, blocking collectives, local(): weight_grad = lax.psum(partial_grad, ('dp', 'rep'))  86.9 us
    reduce_scatter x1, waiting for transfers between devices, local(): lax.psum_scatter(jnp.einsum('tc,tf->cf', input_rows, grad_values, preferr...  50.4 us
    ppermute x4, starting transfers between devices, from_behind(): return lax.ppermute(value, axis, pairs)  14.2 us
    all_to_all x1, waiting for transfers between devices, local(): lax.all_to_all(outgoing, 'dp', split_axis=0, concat_axis=0, tiled=True)  8.65 us
    ppermute x4, waiting for transfers between devices, from_behind(): return lax.ppermute(value, axis, pairs)  5.54 us
  transfers between devices with their start and end apart: 7, of which 3 were waited for; matrix products, arithmetic and copies ran while one was open for 5% of the time, Pallas kernels for 0%

commit v1 on v0

v1 whole, which is shorter than its diff:
```python
import functools
import math

import jax
import jax.numpy as jnp
from jax import lax
from jax.experimental import pallas as pl
from jax.experimental.pallas import tpu as pltpu
from jax.sharding import PartitionSpec as P

HEAD_DIM = 128
KV_HEADS = 4
GROUP = 4
CORES = 2
LANES = 128
LABEL_ROWS = 16
DOC_BASE = 128
MASKED = -1e30
BF16 = jnp.bfloat16
F32 = jnp.float32


def from_behind(value, axis, by):
    devices = lax.axis_size(axis)
    pairs = [(i, i + by) for i in range(devices) if 0 <= i + by < devices]
    return lax.ppermute(value, axis, pairs)


def swap(value, axis, mask):
    devices = lax.axis_size(axis)
    return lax.ppermute(value, axis, [(i, i ^ mask) for i in range(devices)])


def vmem():
    return pl.BlockSpec(memory_space=pltpu.VMEM)


def smem():
    return pl.BlockSpec(memory_space=pltpu.SMEM)


def call(body, outs, ins, flops=0, limit=None):
    count = sum(math.prod(a.shape) * a.dtype.itemsize for a in (*ins, *outs))
    return pl.pallas_call(
        body,
        out_shape=outs,
        in_specs=[smem() if a.dtype == jnp.int32 and a.ndim == 1 else vmem() for a in ins],
        out_specs=[vmem() for _ in outs],
        cost_estimate=pl.CostEstimate(flops=flops, bytes_accessed=count, transcendentals=0),
        compiler_params=pltpu.CompilerParams(vmem_limit_bytes=limit or 32 * 2**20),
    )(*ins)


def shape(*dims, dtype=BF16):
    return jax.ShapeDtypeStruct(dims, dtype)


def dot(a, b, dims):
    return lax.dot_general(a, b, (dims, ((), ())), preferred_element_type=F32)


def doc_message(key_rows, row_docs):
    tokens, width = key_rows.shape
    plus = row_docs + 1
    row = jnp.concatenate([plus % DOC_BASE, plus // DOC_BASE]).astype(BF16)
    row = jnp.pad(row, (0, width - 2 * tokens))
    return jnp.concatenate([key_rows, jnp.broadcast_to(row[None, :], (LABEL_ROWS, width))], 0)


def column_of(row, eye):
    return jnp.sum(jnp.where(eye, row, 0.0), axis=1, keepdims=True)


def probs_body(q_ref, k_ref, prior_ref, doc_ref, g_ref, pt_ref, back_ref, own_ref):
    tokens = k_ref.shape[0]
    u = lax.broadcasted_iota(jnp.int32, (tokens, tokens), 0)
    t = lax.broadcasted_iota(jnp.int32, (tokens, tokens), 1)
    eye = u == t
    own_docs = doc_ref[...].astype(F32)
    codes = prior_ref[tokens : tokens + LABEL_ROWS, : 2 * tokens].astype(F32)[0:1]
    prior_docs = codes[:, :tokens] + DOC_BASE * codes[:, tokens:] - 1.0
    prior_ok = column_of(prior_docs, eye) == own_docs
    own_ok = (column_of(own_docs, eye) == own_docs) & (u <= t)
    prior_ok = jnp.concatenate([prior_ok] * GROUP, 1)
    own_ok = jnp.concatenate([own_ok] * GROUP, 1)
    scale = 1.0 / math.sqrt(HEAD_DIM)
    for g in range(KV_HEADS):
        heads = [slice((g * GROUP + r) * HEAD_DIM, (g * GROUP + r + 1) * HEAD_DIM) for r in range(GROUP)]
        col = slice(g * HEAD_DIM, (g + 1) * HEAD_DIM)
        q4 = jnp.concatenate([q_ref[:, h] for h in heads], 0)
        g4 = jnp.concatenate([g_ref[:, h] for h in heads], 0)
        sp = jnp.where(prior_ok, dot(prior_ref[:tokens, col], q4, ((1,), (1,))), MASKED)
        so = jnp.where(own_ok, dot(k_ref[:, col], q4, ((1,), (1,))), MASKED)
        top = jnp.maximum(jnp.max(sp, 0, keepdims=True), jnp.max(so, 0, keepdims=True))
        ep = jnp.exp((sp - top) * scale)
        eo = jnp.exp((so - top) * scale)
        inv = 1.0 / (jnp.sum(ep, 0, keepdims=True) + jnp.sum(eo, 0, keepdims=True))
        pp = (ep * inv).astype(BF16)
        po = (eo * inv).astype(BF16)
        pt_ref[g, :tokens, :] = pp
        pt_ref[g, tokens:, :] = po
        back_ref[:, col] = dot(pp, g4, ((1,), (0,))).astype(BF16)
        own_ref[:, col] = dot(po, g4, ((1,), (0,)))


def attend_body(blocks, pt_ref, v_ref, prior_ref, plan_ref, idx_ref, out_ref):
    tokens = v_ref.shape[0]
    rows = tokens // blocks
    owners = out_ref.shape[0]
    data = KV_HEADS * GROUP * rows
    me = idx_ref[0]
    for p in range(owners):
        if owners > blocks:
            out_ref[p, :, :] = jnp.zeros(out_ref.shape[1:], BF16)
    slots = [plan_ref[j] ^ me for j in range(blocks)]
    for j in range(blocks):
        out_ref[slots[j], data:, :] = jnp.full((LABEL_ROWS, LANES), j + 1, F32).astype(BF16)
    for g in range(KV_HEADS):
        col = slice(g * HEAD_DIM, (g + 1) * HEAD_DIM)
        att = dot(pt_ref[g, :tokens, :], prior_ref[:, col], ((0,), (0,)))
        att = (att + dot(pt_ref[g, tokens:, :], v_ref[:, col], ((0,), (0,)))).astype(BF16)
        for r in range(GROUP):
            first = (g * GROUP + r) * rows
            for j in range(blocks):
                at = r * tokens + j * rows
                out_ref[slots[j], first : first + rows, :] = att[at : at + rows]


def place_body(blocks, *refs):
    *arrived, out_ref = refs
    rows = out_ref.shape[0] // blocks
    heads = out_ref.shape[1] // LANES
    for a in arrived:
        label = jnp.max(a[heads * rows : heads * rows + LABEL_ROWS, :].astype(F32)).astype(jnp.int32)

        @pl.when(label > 0)
        def _():
            first = pl.multiple_of((label - 1) * rows, rows)
            for h in range(heads):
                out_ref[pl.ds(first, rows), h * LANES : (h + 1) * LANES] = a[h * rows : (h + 1) * rows, :]


def split_body(owners, chips, idx_ref, in_ref, *outs):
    tokens, width = in_ref.shape
    sub = width // (owners * chips)
    q, z = idx_ref[2], idx_ref[3]
    for k in range(chips):
        for m in range(owners):
            first = pl.multiple_of(((z ^ m) * chips + (q ^ k)) * sub, sub)
            outs[k][m * sub : (m + 1) * sub, :] = in_ref[:, pl.ds(first, sub)].T


def halves_body(idx_ref, own_ref, ret_ref, mine_ref, other_ref):
    half = mine_ref.shape[1]
    c = idx_ref[1]
    for ref, core in ((mine_ref, c), (other_ref, 1 - c)):
        at = pl.ds(pl.multiple_of(core * half, half), half)
        ref[...] = (own_ref[:, at] + ret_ref[:, at].astype(F32)).astype(BF16)


def product_body(owners, chips, *refs):
    a, b, h = refs[:chips], refs[chips : 2 * chips], refs[2 * chips : 3 * chips]
    outs = refs[3 * chips :]
    sub = outs[0].shape[0]
    for m in range(owners):
        rows = slice(m * sub, (m + 1) * sub)
        total = None
        for k in range(chips):
            part = dot(jnp.concatenate([a[k][rows, :], b[k][rows, :]], 1), h[k][...], ((1,), (0,)))
            total = part if total is None else total + part
        outs[m][...] = total.astype(outs[m].dtype)


def sum_body(*refs):
    *terms, out_ref = refs
    total = terms[0][...]
    for term in terms[1:]:
        total = total + term[...].astype(F32)
    out_ref[...] = total.astype(BF16)


def spread_body(chips, idx_ref, *refs):
    mine, other, out_ref = refs[:chips], refs[chips : 2 * chips], refs[2 * chips]
    sub, half = mine[0].shape
    c, q = idx_ref[1], idx_ref[2]
    for k in range(chips):
        rows = pl.ds(pl.multiple_of((q ^ k) * sub, sub), sub)
        for ref, core in ((mine[k], c), (other[k], 1 - c)):
            out_ref[rows, pl.ds(pl.multiple_of(core * half, half), half)] = ref[...].astype(F32)


def weight_by_planes(input_rows, grad_parts, idx):
    owners = lax.axis_size("ctx")
    reps = lax.axis_size("rep")
    plane = ("dp", "rep")
    chips = lax.axis_size(plane) // CORES
    tokens, width = input_rows.shape
    sub = width // (owners * chips)
    masks = [(k // reps) * CORES * reps + k % reps for k in range(chips)]
    pieces = call(
        functools.partial(split_body, owners, chips),
        [shape(owners * sub, tokens)] * chips,
        [idx, input_rows],
    )
    mine_in = [pieces[0]] + [swap(pieces[k], plane, masks[k]) for k in range(1, chips)]
    other_in = [swap(p, "dp", 1) for p in mine_in]
    own_grad, returned = grad_parts()
    kv_width = own_grad.shape[1]
    half = kv_width // CORES
    mine, other = call(halves_body, [shape(tokens, half)] * 2, [idx, own_grad, returned])
    both = jnp.concatenate([mine, swap(other, "dp", 1)], 0)
    grads = [both] + [swap(both, plane, masks[k]) for k in range(1, chips)]
    partial = call(
        functools.partial(product_body, owners, chips),
        [shape(sub, half, dtype=F32)] + [shape(sub, half)] * (owners - 1),
        [*mine_in, *other_in, *grads],
        flops=2 * owners * sub * half * CORES * tokens * chips,
    )
    arrived = [swap(partial[m], "ctx", m) for m in range(1, owners)]
    (total,) = call(sum_body, [shape(sub, half)], [partial[0], *arrived])
    mine_out = [total] + [swap(total, plane, masks[k]) for k in range(1, chips)]
    other_out = [swap(p, "dp", 1) for p in mine_out]
    (result,) = call(
        functools.partial(spread_body, chips),
        [shape(chips * sub, kv_width, dtype=F32)],
        [idx, *mine_out, *other_out],
    )
    return result


def weight_by_collectives(input_rows, grad_parts):
    own_grad, returned = grad_parts()
    grad_values = (own_grad + returned.astype(F32)).astype(BF16)
    term = jnp.einsum("tc,tf->cf", input_rows, grad_values, preferred_element_type=F32).astype(BF16)
    part = lax.psum_scatter(term, "ctx", scatter_dimension=0, tiled=True).astype(F32)
    return lax.psum(part, ("dp", "rep"))


def local(inputs, queries, keys, values, grad_out, doc_ids, plan):
    tokens = inputs.shape[1]
    q_width = queries.shape[2]
    kv_width = keys.shape[2]
    shards = ("ctx", "rep")
    owners = lax.axis_size("dp")
    reps = lax.axis_size("rep")
    blocks = plan.shape[1]
    dp = lax.axis_index("dp")
    idx = jnp.stack(
        [dp, dp % CORES, (dp // CORES) * reps + lax.axis_index("rep"), lax.axis_index("ctx")]
    ).astype(jnp.int32)

    prior_keys = from_behind(doc_message(keys[0], doc_ids[0]), shards, 1)
    prior_values = from_behind(values[0], shards, 1)
    probs, back, own_grad = call(
        probs_body,
        [shape(KV_HEADS, 2 * tokens, GROUP * tokens), shape(tokens, kv_width), shape(tokens, kv_width, dtype=F32)],
        [queries[0], keys[0], prior_keys, doc_ids, grad_out[0]],
        flops=8 * tokens * tokens * q_width,
    )

    rows = tokens // blocks
    (outgoing,) = call(
        functools.partial(attend_body, blocks),
        [shape(owners, (q_width // LANES) * rows + LABEL_ROWS, LANES)],
        [probs, values[0], prior_values, plan[0], idx],
        flops=4 * tokens * tokens * q_width,
    )
    arrived = [outgoing[0]] + [swap(outgoing[m], "dp", m) for m in range(1, owners)]
    (placed,) = call(functools.partial(place_body, blocks), [shape(tokens, q_width)], arrived)

    def grad_parts():
        return own_grad, from_behind(back, shards, -1)

    sub = inputs.shape[2] // (lax.axis_size("ctx") * owners // CORES * reps)
    if sub % LANES == 0:
        weight_grad = weight_by_planes(inputs[0], grad_parts, idx)
    else:
        weight_grad = weight_by_collectives(inputs[0], grad_parts)
    return (placed[None], weight_grad)


def solution(mesh):
    rows = P("dp", ("ctx", "rep"), None)
    ids = P("dp", ("ctx", "rep"))
    return jax.shard_map(
        local,
        mesh=mesh,
        in_specs=(rows, rows, rows, rows, rows, ids, ids),
        out_specs=(rows, P("ctx", None)),
        check_vma=False,
    )
```

time: 209 us -> 72.3 us (0.35)
  blocking collectives: 86.9 us -> 0 us
  waiting for transfers between devices: 64.6 us -> 22.3 us
  between operations: 14.3 us -> 0.82 us
  starting transfers between devices: 20.9 us -> 33.1 us
  matrix products: 10.3 us -> 0 us
  Pallas kernels: 0 us -> 8.32 us
  local copies, waits for them, and re-layouts: 10.6 us -> 4.93 us
    psum x1 -> x0, blocking collectives: 86.9 us -> none  [local(): weight_grad = lax.psum(partial_grad, ('dp', 'rep'))]
    reduce_scatter x1 -> x0, waiting for transfers between devices: 50.4 us -> none  [local(): lax.psum_scatter(jnp.einsum('tc,tf->cf', input_rows, grad_values, preferr...]
    ppermute x0 -> x24, starting transfers between devices: none -> 25 us  [swap(): return lax.ppermute(value, axis, [(i, i ^ mask) for i in range(devices)])]
    ppermute x0 -> x24, waiting for transfers between devices: none -> 16.7 us  [swap(): return lax.ppermute(value, axis, [(i, i ^ mask) for i in range(devices)])]
    all_to_all x2 -> x0, waiting for transfers between devices: 8.65 us -> none  [the longest x1 8.65 us: local(): lax.all_to_all(outgoing, 'dp', split_axis=0, concat_axis=0, tiled=True)]
    pallas_call x0 -> x8, Pallas kernels: none -> 8.32 us  [call(): pl.pallas_call(body, out_shape=outs, in_specs=[smem() if a.dtype == jnp.i...]
    dot_general x5 -> x0, matrix products: 8.2 us -> none  [the longest x1 3.17 us: local(): jnp.einsum('tc,tf->cf', input_rows, grad_values, preferred_element_type=j...]
    all_to_all x2 -> x0, starting transfers between devices: 6.67 us -> none  [the longest x1 3.48 us: local(): lax.all_to_all(outgoing, 'dp', split_axis=0, concat_axis=0, tiled=True)]
  transfers between devices with their start and end apart: 7 -> 27, of which waited for: 3 -> 8; matrix products, arithmetic and copies ran while one was open for 5% -> 0% of each run, Pallas kernels for 0% -> 8%
where the time goes in v1:
time: 72.3 us; the launch traced here: 71.9 us
  starting transfers between devices  33.1 us (46%)
  waiting for transfers between devices  22.3 us (31%)
  Pallas kernels  8.32 us (12%)
  local copies, waits for them, and re-layouts  4.93 us (7%)
  other arithmetic  2.37 us (3%)
  between operations  0.82 us (1%)
    ppermute x24, starting transfers between devices, swap(): return lax.ppermute(value, axis, [(i, i ^ mask) for i in range(devices)])  25 us
    ppermute x24, waiting for transfers between devices, swap(): return lax.ppermute(value, axis, [(i, i ^ mask) for i in range(devices)])  16.7 us
    pallas_call x8, Pallas kernels, call(): pl.pallas_call(body, out_shape=outs, in_specs=[smem() if a.dtype == jnp.i...  8.32 us
    ppermute x3, starting transfers between devices, from_behind(): return lax.ppermute(value, axis, pairs)  8.1 us
    ppermute x3, waiting for transfers between devices, from_behind(): return lax.ppermute(value, axis, pairs)  5.57 us
    unnamed x15, local copies, waits for them, and re-layouts  4.88 us
  transfers between devices with their start and end apart: 27, of which 8 were waited for; matrix products, arithmetic and copies ran while one was open for 0% of the time, Pallas kernels for 8%

profile of v1, /device:TPU:0, one launch (start us, length us, event | category | flops | bytes accessed | tf_op | source)
XLA Modules:
  0.0 71.9 jit_solution(9841960482848887014)
XLA Ops:
  3.0 4.9 %collective-permute-start = (bf16[144,512]{1,0:T(8,128)(2,1)S(1)}, bf16[144,512]{1,0:T(8,128)(2,1)S(1)}, u32[]{:S(2)}, u32[]{:S(2)}) collective-permute-start(bf16[144,512]{1,0:T(8,128)(2,1)S(1)} %pad_maximum_fusion), channel_id=1, source_target_pairs={{0,1},{1,2},{2,3},{3,4},{4,5},{5,6},{6,7},{8,9},{9,10},{10,11},{11... | collective-permute-start | bytes 442376 | tf_op jit(solution)/shard_map/ppermute | solution.py:26
  10.0 1.6 %collective-permute-start.5 = (bf16[1024,128]{1,0:T(8,128)(2,1)S(1)}, bf16[1024,128]{1,0:T(8,128)(2,1)S(1)}, u32[]{:S(2)}, u32[]{:S(2)}) collective-permute-start(bf16[1024,128]{1,0:T(8,128)(2,1)S(1)} %get-tuple-element.17), channel_id=1, source_target_pairs={{0,1},{1,0},{8,9},{9,8},{16,17},{17,16},{24,25},{25,24},{2,3},{3,2... | collective-permute-start | bytes 786440 | tf_op jit(solution)/shard_map/ppermute | solution.py:31
  15.3 1.7 %shard_map.86 = (bf16[4,256,512]{2,1,0:T(8,128)(2,1)S(1)}, bf16[128,512]{1,0:T(8,128)(2,1)S(1)}, f32[128,512]{1,0:T(8,128)S(1)}) custom-call(bf16[128,2048]{1,0:T(8,128)(2,1)S(1)} %bitcast.34, bf16[128,512]{1,0:T(8,128)(2,1)S(1)} %bitcast.37, bf16[144,512]{1,0:T(8,128)(2,1)S(1)} %collective-permute-done.prior_ref, s32[1,128]{1,0:T(1,128)S(1)} %copy-done.5, ...), custom_call_target="tpu_custom_call" | custom-call | flops 268435456 | bytes 2769408 | tf_op jit(solution)/shard_map/pallas_call | solution.py:44
  17.0 1.3 %collective-permute-start.12 = (bf16[128,512]{1,0:T(8,128)(2,1)S(1)}, bf16[128,512]{1,0:T(8,128)(2,1)S(1)}, u32[]{:S(2)}, u32[]{:S(2)}) collective-permute-start(bf16[128,512]{1,0:T(8,128)(2,1)S(1)} %get-tuple-element.21), channel_id=1, source_target_pairs={{1,0},{2,1},{3,2},{4,3},{5,4},{6,5},{7,6},{9,8},{10,9},{11,10},{12... | collective-permute-start | bytes 393224 | tf_op jit(solution)/shard_map/ppermute | solution.py:26
  18.3 1.5 %collective-permute-start.6 = (bf16[1024,128]{1,0:T(8,128)(2,1)S(1)}, bf16[1024,128]{1,0:T(8,128)(2,1)S(1)}, u32[]{:S(2)}, u32[]{:S(2)}) collective-permute-start(bf16[1024,128]{1,0:T(8,128)(2,1)S(1)} %get-tuple-element.18), channel_id=1, source_target_pairs={{0,16},{1,17},{8,24},{9,25},{16,0},{17,1},{24,8},{25,9},{2,18},{3,... | collective-permute-start | bytes 786440 | tf_op jit(solution)/shard_map/ppermute | solution.py:31
  19.8 2.6 %collective-permute-start.7 = (bf16[1024,128]{1,0:T(8,128)(2,1)S(1)}, bf16[1024,128]{1,0:T(8,128)(2,1)S(1)}, u32[]{:S(2)}, u32[]{:S(2)}) collective-permute-start(bf16[1024,128]{1,0:T(8,128)(2,1)S(1)} %get-tuple-element.19), channel_id=1, source_target_pairs={{0,17},{1,16},{8,25},{9,24},{16,1},{17,0},{24,9},{25,8},{2,19},{3,... | collective-permute-start | bytes 786440 | tf_op jit(solution)/shard_map/ppermute | solution.py:31
  22.5 1.9 %collective-permute-start.1 = (bf16[128,512]{1,0:T(8,128)(2,1)S(1)}, bf16[128,512]{1,0:T(8,128)(2,1)S(1)}, u32[]{:S(2)}, u32[]{:S(2)}) collective-permute-start(bf16[128,512]{1,0:T(8,128)(2,1)S(1)} %bitcast.38), channel_id=1, source_target_pairs={{0,1},{1,2},{2,3},{3,4},{4,5},{5,6},{6,7},{8,9},{9,10},{10,11},{11... | collective-permute-start | bytes 393224 | tf_op jit(solution)/shard_map/ppermute | solution.py:26
  26.9 5.6 %collective-permute-done.1.prior_ref = bf16[128,512]{1,0:T(8,128)(2,1)S(1)} collective-permute-done((bf16[128,512]{1,0:T(8,128)(2,1)S(1)}, bf16[128,512]{1,0:T(8,128)(2,1)S(1)}, u32[]{:S(2)}, u32[]{:S(2)}) %collective-permute-start.1) | collective-permute-done | bytes 131104 | tf_op jit(solution)/shard_map/ppermute | solution.py:26
  32.5 2.5 %collective-permute-start.14 = (bf16[256,256]{1,0:T(8,128)(2,1)S(1)}, bf16[256,256]{1,0:T(8,128)(2,1)S(1)}, u32[]{:S(2)}, u32[]{:S(2)}) collective-permute-start(bf16[256,256]{1,0:T(8,128)(2,1)S(1)} %constant_dynamic-update-slice_fusion.refs_8_), channel_id=1, source_target_pairs={{0,1},{1,0},{8,9},{9,8},{16,17},{17,16},{24,25},{25,24},{2,3},{3,2... | collective-permute-start | bytes 393224 | tf_op jit(solution)/shard_map/ppermute | solution.py:31
  35.5 1.4 %collective-permute-start.15 = (bf16[256,256]{1,0:T(8,128)(2,1)S(1)}, bf16[256,256]{1,0:T(8,128)(2,1)S(1)}, u32[]{:S(2)}, u32[]{:S(2)}) collective-permute-start(bf16[256,256]{1,0:T(8,128)(2,1)S(1)} %constant_dynamic-update-slice_fusion.refs_8_), channel_id=1, source_target_pairs={{0,16},{1,17},{8,24},{9,25},{16,0},{17,1},{24,8},{25,9},{2,18},{3,... | collective-permute-start | bytes 393224 | tf_op jit(solution)/shard_map/ppermute | solution.py:31
  36.9 1.6 %collective-permute-done.14.refs_9_ = bf16[256,256]{1,0:T(8,128)(2,1)S(1)} collective-permute-done((bf16[256,256]{1,0:T(8,128)(2,1)S(1)}, bf16[256,256]{1,0:T(8,128)(2,1)S(1)}, u32[]{:S(2)}, u32[]{:S(2)}) %collective-permute-start.14) | collective-permute-done | bytes 131104 | tf_op jit(solution)/shard_map/ppermute | solution.py:31
  38.5 2.6 %collective-permute-start.16 = (bf16[256,256]{1,0:T(8,128)(2,1)S(1)}, bf16[256,256]{1,0:T(8,128)(2,1)S(1)}, u32[]{:S(2)}, u32[]{:S(2)}) collective-permute-start(bf16[256,256]{1,0:T(8,128)(2,1)S(1)} %constant_dynamic-update-slice_fusion.refs_8_), channel_id=1, source_target_pairs={{0,17},{1,16},{8,25},{9,24},{16,1},{17,0},{24,9},{25,8},{2,19},{3,... | collective-permute-start | bytes 393224 | tf_op jit(solution)/shard_map/ppermute | solution.py:31
  42.2 2.2 %collective-permute-done.16.refs_11_ = bf16[256,256]{1,0:T(8,128)(2,1)S(1)} collective-permute-done((bf16[256,256]{1,0:T(8,128)(2,1)S(1)}, bf16[256,256]{1,0:T(8,128)(2,1)S(1)}, u32[]{:S(2)}, u32[]{:S(2)}) %collective-permute-start.16) | collective-permute-done | bytes 131104 | tf_op jit(solution)/shard_map/ppermute | solution.py:31
  45.1 1.6 %collective-permute-start.17 = (bf16[256,256]{1,0:T(8,128)(2,1)S(1)}, bf16[256,256]{1,0:T(8,128)(2,1)S(1)}, u32[]{:S(2)}, u32[]{:S(2)}) collective-permute-start(bf16[256,256]{1,0:T(8,128)(2,1)S(1)} %get-tuple-element.25), channel_id=1, source_target_pairs={{0,2},{2,0},{4,6},{6,4},{1,3},{3,1},{5,7},{7,5},{8,10},{10,8},{12,... | collective-permute-start | bytes 393224 | tf_op jit(solution)/shard_map/ppermute | solution.py:31
  46.7 2.6 %collective-permute-start.18 = (bf16[256,256]{1,0:T(8,128)(2,1)S(1)}, bf16[256,256]{1,0:T(8,128)(2,1)S(1)}, u32[]{:S(2)}, u32[]{:S(2)}) collective-permute-start(bf16[256,256]{1,0:T(8,128)(2,1)S(1)} %get-tuple-element.26), channel_id=1, source_target_pairs={{0,4},{2,6},{4,0},{6,2},{1,5},{3,7},{5,1},{7,3},{8,12},{10,14},{12... | collective-permute-start | bytes 393224 | tf_op jit(solution)/shard_map/ppermute | solution.py:31
  49.7 1.5 %collective-permute-start.3 = (bf16[528,128]{1,0:T(8,128)(2,1)S(1)}, bf16[528,128]{1,0:T(8,128)(2,1)S(1)}, u32[]{:S(2)}, u32[]{:S(2)}) collective-permute-start(bf16[528,128]{1,0:T(8,128)(2,1)S(1)} %get-tuple-element.31), channel_id=1, source_target_pairs={{0,16},{8,24},{16,0},{24,8},{1,17},{9,25},{17,1},{25,9},{2,18},{10... | collective-permute-start | bytes 405512 | tf_op jit(solution)/shard_map/ppermute | solution.py:31
  51.2 6.4 %collective-permute-done.18.refs_2_ = bf16[256,256]{1,0:T(8,128)(2,1)S(1)} collective-permute-done((bf16[256,256]{1,0:T(8,128)(2,1)S(1)}, bf16[256,256]{1,0:T(8,128)(2,1)S(1)}, u32[]{:S(2)}, u32[]{:S(2)}) %collective-permute-start.18) | collective-permute-done | bytes 131104 | tf_op jit(solution)/shard_map/ppermute | solution.py:31
  57.6 2.1 %collective-permute-start.20 = (bf16[256,256]{1,0:T(8,128)(2,1)S(1)}, bf16[256,256]{1,0:T(8,128)(2,1)S(1)}, u32[]{:S(2)}, u32[]{:S(2)}) collective-permute-start(bf16[256,256]{1,0:T(8,128)(2,1)S(1)} %shard_map.92.refs_0_), channel_id=1, source_target_pairs={{0,1},{1,0},{8,9},{9,8},{16,17},{17,16},{24,25},{25,24},{2,3},{3,2... | collective-permute-start | bytes 393224 | tf_op jit(solution)/shard_map/ppermute | solution.py:31
  59.7 1.5 %collective-permute-start.21 = (bf16[256,256]{1,0:T(8,128)(2,1)S(1)}, bf16[256,256]{1,0:T(8,128)(2,1)S(1)}, u32[]{:S(2)}, u32[]{:S(2)}) collective-permute-start(bf16[256,256]{1,0:T(8,128)(2,1)S(1)} %shard_map.92.refs_0_), channel_id=1, source_target_pairs={{0,16},{1,17},{8,24},{9,25},{16,0},{17,1},{24,8},{25,9},{2,18},{3,... | collective-permute-start | bytes 393224 | tf_op jit(solution)/shard_map/ppermute | solution.py:31
  61.3 1.6 %collective-permute-start.23 = (bf16[256,256]{1,0:T(8,128)(2,1)S(1)}, bf16[256,256]{1,0:T(8,128)(2,1)S(1)}, u32[]{:S(2)}, u32[]{:S(2)}) collective-permute-start(bf16[256,256]{1,0:T(8,128)(2,1)S(1)} %shard_map.92.refs_0_), channel_id=1, source_target_pairs={{0,8},{8,0},{16,24},{24,16},{1,9},{9,1},{17,25},{25,17},{2,10},{10... | collective-permute-start | bytes 393224 | tf_op jit(solution)/shard_map/ppermute | solution.py:31
  63.0 2.1 %collective-permute-done.21.refs_2_ = bf16[256,256]{1,0:T(8,128)(2,1)S(1)} collective-permute-done((bf16[256,256]{1,0:T(8,128)(2,1)S(1)}, bf16[256,256]{1,0:T(8,128)(2,1)S(1)}, u32[]{:S(2)}, u32[]{:S(2)}) %collective-permute-start.21) | collective-permute-done | bytes 131104 | tf_op jit(solution)/shard_map/ppermute | solution.py:31
  65.1 3.4 %collective-permute-done.22.refs_3_ = bf16[256,256]{1,0:T(8,128)(2,1)S(1)} collective-permute-done((bf16[256,256]{1,0:T(8,128)(2,1)S(1)}, bf16[256,256]{1,0:T(8,128)(2,1)S(1)}, u32[]{:S(2)}, u32[]{:S(2)}) %collective-permute-start.22) | collective-permute-done | bytes 131104 | tf_op jit(solution)/shard_map/ppermute | solution.py:31
  68.5 1.4 %shard_map.88 = bf16[128,2048]{1,0:T(8,128)(2,1)} custom-call(bf16[528,128]{1,0:T(8,128)(2,1)S(1)} %get-tuple-element.33.refs_0_, bf16[528,128]{1,0:T(8,128)(2,1)S(1)} %collective-permute-done.2.refs_1_, bf16[528,128]{1,0:T(8,128)(2,1)S(1)} %collective-permute-done.3.refs_2_, bf16[528,128]{1,0:T(8,128)(2,1)S(1)} %collective-permute-done.4.refs_3_), custom_call_target="tpu_custom_call" | custom-call | bytes 1064960 | tf_op jit(solution)/shard_map/pallas_call | solution.py:44
  69.9 2.0 %shard_map.93 = f32[1024,512]{1,0:T(8,128)} custom-call(s32[4]{0:T(128)S(1)} %pad_add_fusion.idx_ref, bf16[256,256]{1,0:T(8,128)(2,1)S(1)} %shard_map.92.refs_0_, bf16[256,256]{1,0:T(8,128)(2,1)S(1)} %collective-permute-done.20.refs_1_, bf16[256,256]{1,0:T(8,128)(2,1)S(1)} %collective-permute-done.21.refs_2_, ...), custom_call_target="tpu_custom_call" | custom-call | bytes 3145744 | tf_op jit(solution)/shard_map/pallas_call | solution.py:44
  (61 shorter events, 13.6 us)
Async XLA Ops:
  3.0 8.7 %collective-permute-start = (bf16[144,512]{1,0:T(8,128)(2,1)S(1)}, bf16[144,512]{1,0:T(8,128)(2,1)S(1)}, u32[]{:S(2)}, u32[]{:S(2)}) collective-permute-start(bf16[144,512]{1,0:T(8,128)(2,1)S(1)} %pad_maximum_fusion), channel_id=1, source_target_pairs={{0,1},{1,2},{2,3},{3,4},{4,5},{5,6},{6,7},{8,9},{9,10},{10,11},{11... | collective-permute-start | bytes 442376 | tf_op jit(solution)/shard_map/ppermute | solution.py:26
  10.0 15.0 %collective-permute-start.5 = (bf16[1024,128]{1,0:T(8,128)(2,1)S(1)}, bf16[1024,128]{1,0:T(8,128)(2,1)S(1)}, u32[]{:S(2)}, u32[]{:S(2)}) collective-permute-start(bf16[1024,128]{1,0:T(8,128)(2,1)S(1)} %get-tuple-element.17), channel_id=1, source_target_pairs={{0,1},{1,0},{8,9},{9,8},{16,17},{17,16},{24,25},{25,24},{2,3},{3,2... | collective-permute-start | bytes 786440 | tf_op jit(solution)/shard_map/ppermute | solution.py:31
  17.0 7.4 %collective-permute-start.12 = (bf16[128,512]{1,0:T(8,128)(2,1)S(1)}, bf16[128,512]{1,0:T(8,128)(2,1)S(1)}, u32[]{:S(2)}, u32[]{:S(2)}) collective-permute-start(bf16[128,512]{1,0:T(8,128)(2,1)S(1)} %get-tuple-element.21), channel_id=1, source_target_pairs={{1,0},{2,1},{3,2},{4,3},{5,4},{6,5},{7,6},{9,8},{10,9},{11,10},{12... | collective-permute-start | bytes 393224 | tf_op jit(solution)/shard_map/ppermute | solution.py:26
  18.3 16.7 %collective-permute-start.6 = (bf16[1024,128]{1,0:T(8,128)(2,1)S(1)}, bf16[1024,128]{1,0:T(8,128)(2,1)S(1)}, u32[]{:S(2)}, u32[]{:S(2)}) collective-permute-start(bf16[1024,128]{1,0:T(8,128)(2,1)S(1)} %get-tuple-element.18), channel_id=1, source_target_pairs={{0,16},{1,17},{8,24},{9,25},{16,0},{17,1},{24,8},{25,9},{2,18},{3,... | collective-permute-start | bytes 786440 | tf_op jit(solution)/shard_map/ppermute | solution.py:31
  19.8 15.1 %collective-permute-start.7 = (bf16[1024,128]{1,0:T(8,128)(2,1)S(1)}, bf16[1024,128]{1,0:T(8,128)(2,1)S(1)}, u32[]{:S(2)}, u32[]{:S(2)}) collective-permute-start(bf16[1024,128]{1,0:T(8,128)(2,1)S(1)} %get-tuple-element.19), channel_id=1, source_target_pairs={{0,17},{1,16},{8,25},{9,24},{16,1},{17,0},{24,9},{25,8},{2,19},{3,... | collective-permute-start | bytes 786440 | tf_op jit(solution)/shard_map/ppermute | solution.py:31
  22.5 10.0 %collective-permute-start.1 = (bf16[128,512]{1,0:T(8,128)(2,1)S(1)}, bf16[128,512]{1,0:T(8,128)(2,1)S(1)}, u32[]{:S(2)}, u32[]{:S(2)}) collective-permute-start(bf16[128,512]{1,0:T(8,128)(2,1)S(1)} %bitcast.38), channel_id=1, source_target_pairs={{0,1},{1,2},{2,3},{3,4},{4,5},{5,6},{6,7},{8,9},{9,10},{10,11},{11... | collective-permute-start | bytes 393224 | tf_op jit(solution)/shard_map/ppermute | solution.py:26
  24.4 11.1 %collective-permute-start.8 = (bf16[1024,128]{1,0:T(8,128)(2,1)S(1)}, bf16[1024,128]{1,0:T(8,128)(2,1)S(1)}, u32[]{:S(2)}, u32[]{:S(2)}) collective-permute-start(bf16[1024,128]{1,0:T(8,128)(2,1)S(1)} %get-tuple-element.16.refs_0_), channel_id=1, source_target_pairs={{0,8},{8,0},{16,24},{24,16},{1,9},{9,1},{17,25},{25,17},{2,10},{10... | collective-permute-start | bytes 786440 | tf_op jit(solution)/shard_map/ppermute | solution.py:31
  26.5 17.8 %collective-permute-start.9 = (bf16[1024,128]{1,0:T(8,128)(2,1)S(1)}, bf16[1024,128]{1,0:T(8,128)(2,1)S(1)}, u32[]{:S(2)}, u32[]{:S(2)}) collective-permute-start(bf16[1024,128]{1,0:T(8,128)(2,1)S(1)} %collective-permute-done.5.refs_1_), channel_id=1, source_target_pairs={{0,8},{8,0},{16,24},{24,16},{1,9},{9,1},{17,25},{25,17},{2,10},{10... | collective-permute-start | bytes 786440 | tf_op jit(solution)/shard_map/ppermute | solution.py:31
  32.5 6.0 %collective-permute-start.14 = (bf16[256,256]{1,0:T(8,128)(2,1)S(1)}, bf16[256,256]{1,0:T(8,128)(2,1)S(1)}, u32[]{:S(2)}, u32[]{:S(2)}) collective-permute-start(bf16[256,256]{1,0:T(8,128)(2,1)S(1)} %constant_dynamic-update-slice_fusion.refs_8_), channel_id=1, source_target_pairs={{0,1},{1,0},{8,9},{9,8},{16,17},{17,16},{24,25},{25,24},{2,3},{3,2... | collective-permute-start | bytes 393224 | tf_op jit(solution)/shard_map/ppermute | solution.py:31
  34.9 9.4 %collective-permute-start.10 = (bf16[1024,128]{1,0:T(8,128)(2,1)S(1)}, bf16[1024,128]{1,0:T(8,128)(2,1)S(1)}, u32[]{:S(2)}, u32[]{:S(2)}) collective-permute-start(bf16[1024,128]{1,0:T(8,128)(2,1)S(1)} %collective-permute-done.6.refs_2_), channel_id=1, source_target_pairs={{0,8},{8,0},{16,24},{24,16},{1,9},{9,1},{17,25},{25,17},{2,10},{10... | collective-permute-start | bytes 786440 | tf_op jit(solution)/shard_map/ppermute | solution.py:31
  35.0 9.4 %collective-permute-start.11 = (bf16[1024,128]{1,0:T(8,128)(2,1)S(1)}, bf16[1024,128]{1,0:T(8,128)(2,1)S(1)}, u32[]{:S(2)}, u32[]{:S(2)}) collective-permute-start(bf16[1024,128]{1,0:T(8,128)(2,1)S(1)} %collective-permute-done.7.refs_3_), channel_id=1, source_target_pairs={{0,8},{8,0},{16,24},{24,16},{1,9},{9,1},{17,25},{25,17},{2,10},{10... | collective-permute-start | bytes 786440 | tf_op jit(solution)/shard_map/ppermute | solution.py:31
  35.5 6.7 %collective-permute-start.15 = (bf16[256,256]{1,0:T(8,128)(2,1)S(1)}, bf16[256,256]{1,0:T(8,128)(2,1)S(1)}, u32[]{:S(2)}, u32[]{:S(2)}) collective-permute-start(bf16[256,256]{1,0:T(8,128)(2,1)S(1)} %constant_dynamic-update-slice_fusion.refs_8_), channel_id=1, source_target_pairs={{0,16},{1,17},{8,24},{9,25},{16,0},{17,1},{24,8},{25,9},{2,18},{3,... | collective-permute-start | bytes 393224 | tf_op jit(solution)/shard_map/ppermute | solution.py:31
  38.5 5.9 %collective-permute-start.16 = (bf16[256,256]{1,0:T(8,128)(2,1)S(1)}, bf16[256,256]{1,0:T(8,128)(2,1)S(1)}, u32[]{:S(2)}, u32[]{:S(2)}) collective-permute-start(bf16[256,256]{1,0:T(8,128)(2,1)S(1)} %constant_dynamic-update-slice_fusion.refs_8_), channel_id=1, source_target_pairs={{0,17},{1,16},{8,25},{9,24},{16,1},{17,0},{24,9},{25,8},{2,19},{3,... | collective-permute-start | bytes 393224 | tf_op jit(solution)/shard_map/ppermute | solution.py:31
  45.1 6.1 %collective-permute-start.17 = (bf16[256,256]{1,0:T(8,128)(2,1)S(1)}, bf16[256,256]{1,0:T(8,128)(2,1)S(1)}, u32[]{:S(2)}, u32[]{:S(2)}) collective-permute-start(bf16[256,256]{1,0:T(8,128)(2,1)S(1)} %get-tuple-element.25), channel_id=1, source_target_pairs={{0,2},{2,0},{4,6},{6,4},{1,3},{3,1},{5,7},{7,5},{8,10},{10,8},{12,... | collective-permute-start | bytes 393224 | tf_op jit(solution)/shard_map/ppermute | solution.py:31
  46.7 10.9 %collective-permute-start.18 = (bf16[256,256]{1,0:T(8,128)(2,1)S(1)}, bf16[256,256]{1,0:T(8,128)(2,1)S(1)}, u32[]{:S(2)}, u32[]{:S(2)}) collective-permute-start(bf16[256,256]{1,0:T(8,128)(2,1)S(1)} %get-tuple-element.26), channel_id=1, source_target_pairs={{0,4},{2,6},{4,0},{6,2},{1,5},{3,7},{5,1},{7,3},{8,12},{10,14},{12... | collective-permute-start | bytes 393224 | tf_op jit(solution)/shard_map/ppermute | solution.py:31
  49.3 8.3 %collective-permute-start.19 = (bf16[256,256]{1,0:T(8,128)(2,1)S(1)}, bf16[256,256]{1,0:T(8,128)(2,1)S(1)}, u32[]{:S(2)}, u32[]{:S(2)}) collective-permute-start(bf16[256,256]{1,0:T(8,128)(2,1)S(1)} %get-tuple-element.27), channel_id=1, source_target_pairs={{0,6},{2,4},{4,2},{6,0},{1,7},{3,5},{5,3},{7,1},{8,14},{10,12},{12... | collective-permute-start | bytes 393224 | tf_op jit(solution)/shard_map/ppermute | solution.py:31
  49.6 11.7 %collective-permute-start.2 = (bf16[528,128]{1,0:T(8,128)(2,1)S(1)}, bf16[528,128]{1,0:T(8,128)(2,1)S(1)}, u32[]{:S(2)}, u32[]{:S(2)}) collective-permute-start(bf16[528,128]{1,0:T(8,128)(2,1)S(1)} %get-tuple-element.32), channel_id=1, source_target_pairs={{0,8},{8,0},{16,24},{24,16},{1,9},{9,1},{17,25},{25,17},{2,10},{10... | collective-permute-start | bytes 405512 | tf_op jit(solution)/shard_map/ppermute | solution.py:31
  49.7 11.6 %collective-permute-start.3 = (bf16[528,128]{1,0:T(8,128)(2,1)S(1)}, bf16[528,128]{1,0:T(8,128)(2,1)S(1)}, u32[]{:S(2)}, u32[]{:S(2)}) collective-permute-start(bf16[528,128]{1,0:T(8,128)(2,1)S(1)} %get-tuple-element.31), channel_id=1, source_target_pairs={{0,16},{8,24},{16,0},{24,8},{1,17},{9,25},{17,1},{25,9},{2,18},{10... | collective-permute-start | bytes 405512 | tf_op jit(solution)/shard_map/ppermute | solution.py:31
  57.6 5.4 %collective-permute-start.20 = (bf16[256,256]{1,0:T(8,128)(2,1)S(1)}, bf16[256,256]{1,0:T(8,128)(2,1)S(1)}, u32[]{:S(2)}, u32[]{:S(2)}) collective-permute-start(bf16[256,256]{1,0:T(8,128)(2,1)S(1)} %shard_map.92.refs_0_), channel_id=1, source_target_pairs={{0,1},{1,0},{8,9},{9,8},{16,17},{17,16},{24,25},{25,24},{2,3},{3,2... | collective-permute-start | bytes 393224 | tf_op jit(solution)/shard_map/ppermute | solution.py:31
  59.7 5.4 %collective-permute-start.21 = (bf16[256,256]{1,0:T(8,128)(2,1)S(1)}, bf16[256,256]{1,0:T(8,128)(2,1)S(1)}, u32[]{:S(2)}, u32[]{:S(2)}) collective-permute-start(bf16[256,256]{1,0:T(8,128)(2,1)S(1)} %shard_map.92.refs_0_), channel_id=1, source_target_pairs={{0,16},{1,17},{8,24},{9,25},{16,0},{17,1},{24,8},{25,9},{2,18},{3,... | collective-permute-start | bytes 393224 | tf_op jit(solution)/shard_map/ppermute | solution.py:31
  61.2 7.3 %collective-permute-start.22 = (bf16[256,256]{1,0:T(8,128)(2,1)S(1)}, bf16[256,256]{1,0:T(8,128)(2,1)S(1)}, u32[]{:S(2)}, u32[]{:S(2)}) collective-permute-start(bf16[256,256]{1,0:T(8,128)(2,1)S(1)} %shard_map.92.refs_0_), channel_id=1, source_target_pairs={{0,17},{1,16},{8,25},{9,24},{16,1},{17,0},{24,9},{25,8},{2,19},{3,... | collective-permute-start | bytes 393224 | tf_op jit(solution)/shard_map/ppermute | solution.py:31
  61.2 7.2 %collective-permute-start.4 = (bf16[528,128]{1,0:T(8,128)(2,1)S(1)}, bf16[528,128]{1,0:T(8,128)(2,1)S(1)}, u32[]{:S(2)}, u32[]{:S(2)}) collective-permute-start(bf16[528,128]{1,0:T(8,128)(2,1)S(1)} %get-tuple-element.30), channel_id=1, source_target_pairs={{0,24},{8,16},{16,8},{24,0},{1,25},{9,17},{17,9},{25,1},{2,26},{10... | collective-permute-start | bytes 405512 | tf_op jit(solution)/shard_map/ppermute | solution.py:31
  61.3 8.6 %collective-permute-start.23 = (bf16[256,256]{1,0:T(8,128)(2,1)S(1)}, bf16[256,256]{1,0:T(8,128)(2,1)S(1)}, u32[]{:S(2)}, u32[]{:S(2)}) collective-permute-start(bf16[256,256]{1,0:T(8,128)(2,1)S(1)} %shard_map.92.refs_0_), channel_id=1, source_target_pairs={{0,8},{8,0},{16,24},{24,16},{1,9},{9,1},{17,25},{25,17},{2,10},{10... | collective-permute-start | bytes 393224 | tf_op jit(solution)/shard_map/ppermute | solution.py:31
  63.0 6.8 %collective-permute-start.24 = (bf16[256,256]{1,0:T(8,128)(2,1)S(1)}, bf16[256,256]{1,0:T(8,128)(2,1)S(1)}, u32[]{:S(2)}, u32[]{:S(2)}) collective-permute-start(bf16[256,256]{1,0:T(8,128)(2,1)S(1)} %collective-permute-done.20.refs_1_), channel_id=1, source_target_pairs={{0,8},{8,0},{16,24},{24,16},{1,9},{9,1},{17,25},{25,17},{2,10},{10... | collective-permute-start | bytes 393224 | tf_op jit(solution)/shard_map/ppermute | solution.py:31
  (10 other events, 74.8 us)

commit v2 on v1

v2 whole, which is shorter than its diff:
```python
import functools
import math

import jax
import jax.numpy as jnp
from jax import lax
from jax.experimental import pallas as pl
from jax.experimental.pallas import tpu as pltpu
from jax.sharding import PartitionSpec as P

HEAD_DIM = 128
KV_HEADS = 4
GROUP = 4
CORES = 2
LANES = 128
LABEL_ROWS = 16
DOC_BASE = 128
MASKED = -1e30
BF16 = jnp.bfloat16
F32 = jnp.float32


def from_behind(value, axis, by):
    devices = lax.axis_size(axis)
    pairs = [(i, i + by) for i in range(devices) if 0 <= i + by < devices]
    return lax.ppermute(value, axis, pairs)


def swap(value, axis, mask):
    devices = lax.axis_size(axis)
    return lax.ppermute(value, axis, [(i, i ^ mask) for i in range(devices)])


def vmem():
    return pl.BlockSpec(memory_space=pltpu.VMEM)


def smem():
    return pl.BlockSpec(memory_space=pltpu.SMEM)


def call(body, outs, ins, weight=0, deps=(), hbm_in=(), hbm_out=(), scratch=()):
    space = pl.BlockSpec(memory_space=pltpu.HBM)
    ins_at = [smem() if a.dtype == jnp.int32 and a.ndim == 1 else vmem() for a in ins]
    ins_at = [space if i in hbm_in else at for i, at in enumerate(ins_at)]
    skip = len(deps)
    ins = [pltpu.with_memory_space_constraint(a, pltpu.HBM) if i in hbm_in else a for i, a in enumerate(ins)]
    return pl.pallas_call(
        lambda *refs: body(*refs[skip:]),
        out_shape=outs,
        in_specs=[space] * skip + ins_at,
        out_specs=[space if i in hbm_out else vmem() for i in range(len(outs))],
        scratch_shapes=list(scratch),
        cost_estimate=pl.CostEstimate(flops=weight * 10**9, bytes_accessed=0, transcendentals=0),
        compiler_params=pltpu.CompilerParams(vmem_limit_bytes=32 * 2**20),
    )(*deps, *ins)


def shape(*dims, dtype=BF16):
    return jax.ShapeDtypeStruct(dims, dtype)


def dot(a, b, dims):
    return lax.dot_general(a, b, (dims, ((), ())), preferred_element_type=F32)


def message_body(key_hbm, value_hbm, doc_hbm, out_ref, doc_ref, sems):
    tokens, width = key_hbm.shape
    copies = [
        pltpu.make_async_copy(ref, out_ref.at[pl.ds(i * tokens, tokens)], sems.at[i])
        for i, ref in enumerate((key_hbm, value_hbm))
    ]
    copies.append(pltpu.make_async_copy(doc_hbm, doc_ref, sems.at[2]))
    for copy in copies:
        copy.start()
    copies.pop().wait()
    plus = doc_ref[...] + 1
    high = plus // DOC_BASE
    digits = jnp.concatenate([plus - high * DOC_BASE, high], 1).astype(F32)
    digits = jnp.broadcast_to(digits, (LABEL_ROWS, 2 * tokens)).astype(BF16)
    out_ref[2 * tokens :, : 2 * tokens] = digits
    if width > 2 * tokens:
        out_ref[2 * tokens :, 2 * tokens :] = jnp.zeros((LABEL_ROWS, width - 2 * tokens), BF16)
    for copy in copies:
        copy.wait()


def docs_of(message_ref, tokens):
    codes = message_ref[2 * tokens :, : 2 * tokens].astype(F32)[0:1]
    return codes[:, :tokens] + DOC_BASE * codes[:, tokens:] - 1.0


def column_of(row, eye):
    return jnp.sum(jnp.where(eye, row, 0.0), axis=1, keepdims=True)


def probs_body(q_ref, g_ref, k_ref, prior_ref, pt_ref, back_ref, own_ref):
    tokens = q_ref.shape[0]
    u = lax.broadcasted_iota(jnp.int32, (tokens, tokens), 0)
    t = lax.broadcasted_iota(jnp.int32, (tokens, tokens), 1)
    eye = u == t
    own_docs = docs_of(k_ref, tokens)
    prior_ok = column_of(docs_of(prior_ref, tokens), eye) == own_docs
    own_ok = (column_of(own_docs, eye) == own_docs) & (u <= t)
    prior_ok = jnp.concatenate([prior_ok] * GROUP, 1)
    own_ok = jnp.concatenate([own_ok] * GROUP, 1)
    scale = 1.0 / math.sqrt(HEAD_DIM)
    for g in range(KV_HEADS):
        heads = [slice((g * GROUP + r) * HEAD_DIM, (g * GROUP + r + 1) * HEAD_DIM) for r in range(GROUP)]
        col = slice(g * HEAD_DIM, (g + 1) * HEAD_DIM)
        q4 = jnp.concatenate([q_ref[:, h] for h in heads], 0)
        g4 = jnp.concatenate([g_ref[:, h] for h in heads], 0)
        sp = jnp.where(prior_ok, dot(prior_ref[:tokens, col], q4, ((1,), (1,))), MASKED)
        so = jnp.where(own_ok, dot(k_ref[:tokens, col], q4, ((1,), (1,))), MASKED)
        top = jnp.maximum(jnp.max(sp, 0, keepdims=True), jnp.max(so, 0, keepdims=True))
        ep = jnp.exp((sp - top) * scale)
        eo = jnp.exp((so - top) * scale)
        inv = 1.0 / (jnp.sum(ep, 0, keepdims=True) + jnp.sum(eo, 0, keepdims=True))
        pp = (ep * inv).astype(BF16)
        po = (eo * inv).astype(BF16)
        pt_ref[g, :tokens, :] = pp
        pt_ref[g, tokens:, :] = po
        back_ref[:, col] = dot(pp, g4, ((1,), (0,))).astype(BF16)
        own_ref[:, col] = dot(po, g4, ((1,), (0,)))


def attend_body(blocks, pt_ref, message_ref, prior_ref, plan_ref, idx_ref, out_ref):
    tokens = pt_ref.shape[1] // 2
    rows = tokens // blocks
    owners = out_ref.shape[0]
    data = KV_HEADS * GROUP * rows
    me = idx_ref[0]
    if owners > blocks:
        out_ref[...] = jnp.zeros(out_ref.shape, BF16)
    slots = [plan_ref[j] ^ me for j in range(blocks)]
    for j in range(blocks):
        out_ref[slots[j], data:, :] = jnp.full((LABEL_ROWS, LANES), j + 1, F32).astype(BF16)
    for g in range(KV_HEADS):
        col = slice(g * HEAD_DIM, (g + 1) * HEAD_DIM)
        att = dot(pt_ref[g, :tokens, :], prior_ref[tokens : 2 * tokens, col], ((0,), (0,)))
        att = att + dot(pt_ref[g, tokens:, :], message_ref[tokens : 2 * tokens, col], ((0,), (0,)))
        att = att.astype(BF16)
        for r in range(GROUP):
            first = (g * GROUP + r) * rows
            for j in range(blocks):
                at = r * tokens + j * rows
                out_ref[slots[j], first : first + rows, :] = att[at : at + rows]


def place_body(blocks, *refs):
    *arrived, out_hbm, wide_ref, sems = refs
    rows = out_hbm.shape[0] // blocks
    heads = out_hbm.shape[1] // LANES
    labels = [jnp.max(a[heads * rows :, :].astype(F32)).astype(jnp.int32) for a in arrived]
    copies = []
    for i, a in enumerate(arrived):
        first = pl.multiple_of(jnp.maximum(labels[i] - 1, 0) * rows, rows)
        copies.append(pltpu.make_async_copy(wide_ref.at[i], out_hbm.at[pl.ds(first, rows)], sems.at[i]))

        @pl.when(labels[i] > 0)
        def _():
            for h in range(heads):
                wide_ref[i, :, h * LANES : (h + 1) * LANES] = a[h * rows : (h + 1) * rows, :]
            copies[i].start()

    for i, copy in enumerate(copies):

        @pl.when(labels[i] > 0)
        def _():
            copy.wait()


def split_body(reduced, places, idx_ref, in_hbm, q_hbm, g_hbm, *refs):
    spread = len(places)
    outs, (q_ref, g_ref, in_ref, sems) = refs[:spread], refs[spread:]
    copies = [
        pltpu.make_async_copy(src, dst, sems.at[i])
        for i, (src, dst) in enumerate(((in_hbm, in_ref), (q_hbm, q_ref), (g_hbm, g_ref)))
    ]
    for copy in copies:
        copy.start()
    sub = in_ref.shape[1] // (spread * len(reduced))
    x, y, z = idx_ref[2], idx_ref[3], idx_ref[4]
    reps, chips = idx_ref[5], idx_ref[6]
    copies[0].wait()
    for k, (kx, kz, ky) in enumerate(places):
        for m, (mx, mz, my) in enumerate(reduced):
            first = (z ^ kz ^ mz) * chips + (x ^ kx ^ mx) * reps + (y ^ ky ^ my)
            first = pl.multiple_of(first * sub, sub)
            outs[k][m * sub : (m + 1) * sub, :] = in_ref[:, pl.ds(first, sub)].T
    copies[1].wait()
    copies[2].wait()


def both_body(own_ref, ret_ref, out_ref):
    out_ref[...] = (own_ref[...] + ret_ref[...].astype(F32)).astype(BF16)


def product_body(cross, idx_ref, *refs):
    *ins, out_ref = refs
    count = len(ins) // 2
    half = out_ref.shape[1]
    core = idx_ref[1] ^ 1 if cross else idx_ref[1]
    cols = pl.ds(pl.multiple_of(core * half, half), half)
    a = jnp.concatenate([ref[...] for ref in ins[:count]], 1)
    b = jnp.concatenate([ref[:, cols] for ref in ins[count:]], 0)
    out_ref[...] = dot(a, b, ((1,), (0,))).astype(out_ref.dtype)


def add_body(own_ref, cross_ref, *outs):
    sub = outs[0].shape[0]
    for m, out in enumerate(outs):
        rows = slice(m * sub, (m + 1) * sub)
        out[...] = (own_ref[rows, :] + cross_ref[rows, :].astype(F32)).astype(out.dtype)


def sum_body(*refs):
    *terms, out_ref = refs
    total = terms[0][...]
    for term in terms[1:]:
        total = total + term[...].astype(F32)
    out_ref[...] = total.astype(BF16)


def spread_body(chips, idx_ref, *refs):
    mine, other, (out_hbm, wide_ref, sems) = refs[:chips], refs[chips : 2 * chips], refs[2 * chips :]
    sub, half = mine[0].shape
    c, q = idx_ref[1], idx_ref[2] * idx_ref[5] + idx_ref[3]
    copies = []
    for k in range(chips):
        rows = pl.ds(pl.multiple_of((q ^ k) * sub, sub), sub)
        for i, (ref, core) in enumerate(((mine[k], c), (other[k], 1 - c))):
            at = 2 * k + i
            wide_ref[at] = ref[...].astype(F32)
            to = out_hbm.at[rows, pl.ds(pl.multiple_of(core * half, half), half)]
            copies.append(pltpu.make_async_copy(wide_ref.at[at], to, sems.at[at]))
            copies[-1].start()
    for copy in copies:
        copy.wait()


def weight_by_collectives(input_rows, grad_parts):
    own_grad, returned = grad_parts()
    grad_values = (own_grad + returned.astype(F32)).astype(BF16)
    term = jnp.einsum("tc,tf->cf", input_rows, grad_values, preferred_element_type=F32).astype(BF16)
    part = lax.psum_scatter(term, "ctx", scatter_dimension=0, tiled=True).astype(F32)
    return lax.psum(part, ("dp", "rep"))


def weight_by_collectives(input_rows, own_grad, returned):
    grad_values = (own_grad + returned.astype(F32)).astype(BF16)
    term = jnp.einsum("tc,tf->cf", input_rows, grad_values, preferred_element_type=F32).astype(BF16)
    part = lax.psum_scatter(term, "ctx", scatter_dimension=0, tiled=True).astype(F32)
    return lax.psum(part, ("dp", "rep"))


def local(inputs, queries, keys, values, grad_out, doc_ids, plan):
    tokens, width = inputs.shape[1:]
    q_width = queries.shape[2]
    kv_width = keys.shape[2]
    half = kv_width // CORES
    shards = ("ctx", "rep")
    micro, owners, reps = (lax.axis_size(axis) for axis in ("dp", "ctx", "rep"))
    chips = micro // CORES * reps
    blocks = plan.shape[1]
    rows = tokens // blocks
    dp, ctx, rep = (lax.axis_index(axis) for axis in ("dp", "ctx", "rep"))
    idx = jnp.stack([dp, dp % CORES, dp // CORES, rep, ctx, reps, chips]).astype(jnp.int32)

    places = [(kx, 0, ky) for kx in range(micro // CORES) for ky in range(reps)]
    reduced = [(0, mz, 0) for mz in range(owners)]
    every = ("dp", "ctx", "rep")

    def away(value, x, z, y):
        return swap(value, every, (x * CORES * owners + z) * reps + y)

    sub = width // (len(places) * len(reduced))
    by_chips = sub % LANES == 0

    (message,) = call(
        message_body,
        [shape(2 * tokens + LABEL_ROWS, kv_width)],
        [keys[0], values[0], doc_ids],
        hbm_in=(0, 1, 2),
        scratch=[pltpu.VMEM(doc_ids.shape, jnp.int32), pltpu.SemaphoreType.DMA((3,))],
    )
    prior = from_behind(message, shards, 1)

    if by_chips:
        *pieces, q_rows, g_rows = call(
            functools.partial(split_body, reduced, places),
            [shape(len(reduced) * sub, tokens)] * len(places) + [shape(tokens, q_width)] * 2,
            [idx, inputs[0], queries[0], grad_out[0]],
            hbm_in=(1, 2, 3),
            scratch=[pltpu.VMEM((tokens, width), BF16), pltpu.SemaphoreType.DMA((3,))],
        )

        def gather(value_of):
            return [value_of(0)] + [away(value_of(k), *place) for k, place in enumerate(places) if k]

        mine_in = gather(lambda k: pieces[k])
    else:
        q_rows, g_rows = queries[0], grad_out[0]

    probs, back, own = call(
        probs_body,
        [
            shape(KV_HEADS, 2 * tokens, GROUP * tokens),
            shape(tokens, kv_width),
            shape(tokens, kv_width, dtype=F32),
        ],
        [q_rows, g_rows, message, prior],
        weight=100,
    )
    returned = from_behind(back, shards, -1)
    if by_chips:
        (grad_values,) = call(both_body, [shape(tokens, kv_width)], [own, returned])
        grads = gather(lambda k: grad_values)
        factors = [idx, *mine_in, *grads]
        (cross,) = call(functools.partial(product_body, True), [shape(len(reduced) * sub, half)], factors)
        (kept,) = call(
            functools.partial(product_body, False), [shape(len(reduced) * sub, half, dtype=F32)], factors, weight=3
        )
        partial = call(
            add_body,
            [shape(sub, half, dtype=F32)] + [shape(sub, half)] * (len(reduced) - 1),
            [kept, swap(cross, "dp", 1)],
        )
        arrived = [away(partial[m], *place) for m, place in enumerate(reduced) if m]

    (outgoing,) = call(
        functools.partial(attend_body, blocks),
        [shape(micro, (q_width // LANES) * rows + LABEL_ROWS, LANES)],
        [probs, message, prior, plan[0], idx],
        weight=100,
        deps=[partial[0]] if by_chips else [],
    )
    arrived_out = [outgoing[0]] + [swap(outgoing[m], "dp", m) for m in range(1, micro)]

    (placed,) = call(
        functools.partial(place_body, blocks),
        [shape(tokens, q_width)],
        arrived_out,
        hbm_out=(0,),
        scratch=[pltpu.VMEM((micro, rows, q_width), BF16), pltpu.SemaphoreType.DMA((micro,))],
    )
    if by_chips:
        (total,) = call(sum_body, [shape(sub, half)], [partial[0], *arrived], deps=[outgoing])
        mine_out = [total] + [away(total, k // reps, 0, k % reps) for k in range(1, chips)]
        other_out = [swap(p, "dp", 1) for p in mine_out]
        (weight_grad,) = call(
            functools.partial(spread_body, chips),
            [shape(chips * sub, kv_width, dtype=F32)],
            [idx, *mine_out, *other_out],
            hbm_out=(0,),
            scratch=[pltpu.VMEM((2 * chips, sub, half), F32), pltpu.SemaphoreType.DMA((2 * chips,))],
        )
    else:
        weight_grad = weight_by_collectives(inputs[0], own, returned)
    return (placed[None], weight_grad)


def solution(mesh):
    rows = P("dp", ("ctx", "rep"), None)
    ids = P("dp", ("ctx", "rep"))
    return jax.shard_map(
        local,
        mesh=mesh,
        in_specs=(rows, rows, rows, rows, rows, ids, ids),
        out_specs=(rows, P("ctx", None)),
        check_vma=False,
    )
```

time: 72.3 us -> 66 us (0.913)
  starting transfers between devices: 33.1 us -> 28.2 us
  local copies, waits for them, and re-layouts: 4.93 us -> 0.13 us
  waiting for transfers between devices: 22.3 us -> 25.6 us
  Pallas kernels: 8.32 us -> 10.9 us
  other arithmetic: 2.37 us -> 0 us
    unnamed x15 -> x2, local copies, waits for them, and re-layouts: 4.88 us -> 0.01 us
    ppermute x24 -> x20, waiting for transfers between devices: 16.7 us -> 20.4 us  [swap(): return lax.ppermute(value, axis, [(i, i ^ mask) for i in range(devices)])]
    ppermute x24 -> x20, starting transfers between devices: 25 us -> 22.1 us  [swap(): return lax.ppermute(value, axis, [(i, i ^ mask) for i in range(devices)])]
    pallas_call x8 -> x11, Pallas kernels: 8.32 us -> 10.9 us  [call(): pl.pallas_call(lambda *refs: body(*refs[skip:]), out_shape=outs, in_specs...]
    ppermute x3 -> x2, starting transfers between devices: 8.1 us -> 6.18 us  [from_behind(): return lax.ppermute(value, axis, pairs)]
    another operation x3 -> x0, other arithmetic: 1.45 us -> none
    concatenate x2 -> x0, other arithmetic: 0.93 us -> none  [the longest x1 0.92 us: doc_message(): jnp.concatenate([key_rows, jnp.broadcast_to(row[None, :], (LABEL_ROWS, wi...]
    ppermute x3 -> x2, waiting for transfers between devices: 5.57 us -> 5.22 us  [from_behind(): return lax.ppermute(value, axis, pairs)]
  transfers between devices with their start and end apart: 27 -> 22, of which waited for: 8 -> 12; matrix products, arithmetic and copies ran while one was open for 0% -> 0% of each run, Pallas kernels for 8% -> 10%
where the time goes in v2:
time: 66 us; the launch traced here: 65.6 us
  starting transfers between devices  28.2 us (43%)
  waiting for transfers between devices  25.6 us (39%)
  Pallas kernels  10.9 us (17%)
  between operations  0.8 us (1%)
    ppermute x20, starting transfers between devices, swap(): return lax.ppermute(value, axis, [(i, i ^ mask) for i in range(devices)])  22.1 us
    ppermute x20, waiting for transfers between devices, swap(): return lax.ppermute(value, axis, [(i, i ^ mask) for i in range(devices)])  20.4 us
    pallas_call x11, Pallas kernels, call(): pl.pallas_call(lambda *refs: body(*refs[skip:]), out_shape=outs, in_specs...  10.9 us
    ppermute x2, starting transfers between devices, from_behind(): return lax.ppermute(value, axis, pairs)  6.18 us
    ppermute x2, waiting for transfers between devices, from_behind(): return lax.ppermute(value, axis, pairs)  5.22 us
  transfers between devices with their start and end apart: 22, of which 12 were waited for; matrix products, arithmetic and copies ran while one was open for 0% of the time, Pallas kernels for 10%

profile of v2, /device:TPU:0, one launch (start us, length us, event | category | flops | bytes accessed | tf_op | source)
XLA Modules:
  0.0 65.6 jit_solution(6157731804381178608)
XLA Ops:
  0.6 1.0 %shard_map.87.refs_2_ = bf16[272,512]{1,0:T(8,128)(2,1)S(1)} custom-call(bf16[128,512]{1,0:T(8,128)(2,1)} %bitcast.25, bf16[128,512]{1,0:T(8,128)(2,1)} %bitcast.26, s32[1,128]{1,0:T(1,128)} %refs_2_.1), custom_call_target="tpu_custom_call" | custom-call | tf_op jit(solution)/shard_map/pallas_call | solution.py:48
  1.6 4.9 %collective-permute-start.3 = (bf16[272,512]{1,0:T(8,128)(2,1)S(1)}, bf16[272,512]{1,0:T(8,128)(2,1)S(1)}, u32[]{:S(2)}, u32[]{:S(2)}) collective-permute-start(bf16[272,512]{1,0:T(8,128)(2,1)S(1)} %shard_map.87.refs_2_), channel_id=1, source_target_pairs={{0,1},{1,2},{2,3},{3,4},{4,5},{5,6},{6,7},{8,9},{9,10},{10,11},{11... | collective-permute-start | bytes 835592 | tf_op jit(solution)/shard_map/ppermute | solution.py:26
  6.6 2.1 %shard_map.86 = (bf16[1024,128]{1,0:T(8,128)(2,1)S(1)}, bf16[1024,128]{1,0:T(8,128)(2,1)S(1)}, bf16[1024,128]{1,0:T(8,128)(2,1)S(1)}, bf16[1024,128]{1,0:T(8,128...) custom-call(s32[7]{0:T(128)S(1)} %stack.23.refs_0_.refs_5_, bf16[128,4096]{1,0:T(8,128)(2,1)} %bitcast.21, ...), custom_call_target="tpu_custom_call" | custom-call | tf_op jit(solution)/shard_map/pallas_call | solution.py:48
  8.8 1.6 %collective-permute-start = (bf16[1024,128]{1,0:T(8,128)(2,1)S(1)}, bf16[1024,128]{1,0:T(8,128)(2,1)S(1)}, u32[]{:S(2)}, u32[]{:S(2)}) collective-permute-start(bf16[1024,128]{1,0:T(8,128)(2,1)S(1)} %get-tuple-element.16), channel_id=1, source_target_pairs={{0,1},{1,0},{2,3},{3,2},{4,5},{5,4},{6,7},{7,6},{8,9},{9,8},{10,11... | collective-permute-start | bytes 786440 | tf_op jit(solution)/shard_map/ppermute | solution.py:31
  10.3 3.2 %collective-permute-done.3.refs_3_ = bf16[272,512]{1,0:T(8,128)(2,1)S(1)} collective-permute-done((bf16[272,512]{1,0:T(8,128)(2,1)S(1)}, bf16[272,512]{1,0:T(8,128)(2,1)S(1)}, u32[]{:S(2)}, u32[]{:S(2)}) %collective-permute-start.3) | collective-permute-done | bytes 278560 | tf_op jit(solution)/shard_map/ppermute | solution.py:26
  13.6 1.7 %shard_map.88 = (bf16[4,256,512]{2,1,0:T(8,128)(2,1)S(1)}, bf16[128,512]{1,0:T(8,128)(2,1)S(1)}, f32[128,512]{1,0:T(8,128)S(1)}) custom-call(bf16[128,2048]{1,0:T(8,128)(2,1)S(1)} %get-tuple-element.19.refs_0_, bf16[128,2048]{1,0:T(8,128)(2,1)S(1)} %get-tuple-element.20.refs_1_, bf16[272,512]{1,0:T(8,128)(2,1)S(1)} %shard_map.87.refs_2_, ...), custom_call_target="tpu_custom_call" | custom-call | flops 99999997952 | tf_op jit(solution)/shard_map/pallas_call | solution.py:48
  15.3 1.3 %collective-permute-start.4 = (bf16[128,512]{1,0:T(8,128)(2,1)S(1)}, bf16[128,512]{1,0:T(8,128)(2,1)S(1)}, u32[]{:S(2)}, u32[]{:S(2)}) collective-permute-start(bf16[128,512]{1,0:T(8,128)(2,1)S(1)} %get-tuple-element.22), channel_id=1, source_target_pairs={{1,0},{2,1},{3,2},{4,3},{5,4},{6,5},{7,6},{9,8},{10,9},{11,10},{12... | collective-permute-start | bytes 393224 | tf_op jit(solution)/shard_map/ppermute | solution.py:26
  16.6 1.6 %collective-permute-start.1 = (bf16[1024,128]{1,0:T(8,128)(2,1)S(1)}, bf16[1024,128]{1,0:T(8,128)(2,1)S(1)}, u32[]{:S(2)}, u32[]{:S(2)}) collective-permute-start(bf16[1024,128]{1,0:T(8,128)(2,1)S(1)} %get-tuple-element.17), channel_id=1, source_target_pairs={{0,16},{1,17},{2,18},{3,19},{4,20},{5,21},{6,22},{7,23},{8,24},{9,... | collective-permute-start | bytes 786440 | tf_op jit(solution)/shard_map/ppermute | solution.py:31
  18.1 3.1 %collective-permute-start.2 = (bf16[1024,128]{1,0:T(8,128)(2,1)S(1)}, bf16[1024,128]{1,0:T(8,128)(2,1)S(1)}, u32[]{:S(2)}, u32[]{:S(2)}) collective-permute-start(bf16[1024,128]{1,0:T(8,128)(2,1)S(1)} %get-tuple-element.18), channel_id=1, source_target_pairs={{0,17},{1,16},{2,19},{3,18},{4,21},{5,20},{6,23},{7,22},{8,25},{9,... | collective-permute-start | bytes 786440 | tf_op jit(solution)/shard_map/ppermute | solution.py:31
  21.2 2.0 %collective-permute-done.4.refs_1_ = bf16[128,512]{1,0:T(8,128)(2,1)S(1)} collective-permute-done((bf16[128,512]{1,0:T(8,128)(2,1)S(1)}, bf16[128,512]{1,0:T(8,128)(2,1)S(1)}, u32[]{:S(2)}, u32[]{:S(2)}) %collective-permute-start.4) | collective-permute-done | bytes 131104 | tf_op jit(solution)/shard_map/ppermute | solution.py:26
  23.2 4.1 %collective-permute-start.7 = (bf16[128,512]{1,0:T(8,128)(2,1)S(1)}, bf16[128,512]{1,0:T(8,128)(2,1)S(1)}, u32[]{:S(2)}, u32[]{:S(2)}) collective-permute-start(bf16[128,512]{1,0:T(8,128)(2,1)S(1)} %shard_map.89.refs_5_), channel_id=1, source_target_pairs={{0,17},{1,16},{2,19},{3,18},{4,21},{5,20},{6,23},{7,22},{8,25},{9,... | collective-permute-start | bytes 393224 | tf_op jit(solution)/shard_map/ppermute | solution.py:31
  28.0 5.7 %collective-permute-done.2.refs_4_ = bf16[1024,128]{1,0:T(8,128)(2,1)S(1)} collective-permute-done((bf16[1024,128]{1,0:T(8,128)(2,1)S(1)}, bf16[1024,128]{1,0:T(8,128)(2,1)S(1)}, u32[]{:S(2)}, u32[]{:S(2)}) %collective-permute-start.2) | collective-permute-done | bytes 262176 | tf_op jit(solution)/shard_map/ppermute | solution.py:31
  33.7 1.4 %collective-permute-done.7.refs_8_ = bf16[128,512]{1,0:T(8,128)(2,1)S(1)} collective-permute-done((bf16[128,512]{1,0:T(8,128)(2,1)S(1)}, bf16[128,512]{1,0:T(8,128)(2,1)S(1)}, u32[]{:S(2)}, u32[]{:S(2)}) %collective-permute-start.7) | collective-permute-done | bytes 131104 | tf_op jit(solution)/shard_map/ppermute | solution.py:31
  35.5 1.0 %shard_map.91 = bf16[1024,256]{1,0:T(8,128)(2,1)S(1)} custom-call(s32[7]{0:T(128)S(1)} %stack.23.refs_0_.refs_5_, bf16[1024,128]{1,0:T(8,128)(2,1)S(1)} %get-tuple-element.15.refs_1_, bf16[1024,128]{1,0:T(8,128)(2,1)S(1)} %collective-permute-done.refs_2_, bf16[1024,128]{1,0:T(8,128)(2,1)S(1)} %collective-permute-done.1.refs_3_, ...), custom_call_target="tpu_custom_call" | custom-call | tf_op jit(solution)/shard_map/pallas_call | solution.py:48
  36.6 1.0 %shard_map.90.refs_0_ = f32[1024,256]{1,0:T(8,128)S(1)} custom-call(s32[7]{0:T(128)S(1)} %stack.23.refs_0_.refs_5_, bf16[1024,128]{1,0:T(8,128)(2,1)S(1)} %get-tuple-element.15.refs_1_, bf16[1024,128]{1,0:T(8,128)(2,1)S(1)} %collective-permute-done.refs_2_, bf16[1024,128]{1,0:T(8,128)(2,1)S(1)} %collective-permute-done.1.refs_3_, ...), custom_call_target="tpu_custom_call" | custom-call | flops 3000000000 | tf_op jit(solution)/shard_map/pallas_call | solution.py:48
  38.6 2.7 %collective-permute-start.12 = (bf16[256,256]{1,0:T(8,128)(2,1)S(1)}, bf16[256,256]{1,0:T(8,128)(2,1)S(1)}, u32[]{:S(2)}, u32[]{:S(2)}) collective-permute-start(bf16[256,256]{1,0:T(8,128)(2,1)S(1)} %get-tuple-element.25), channel_id=1, source_target_pairs={{0,2},{1,3},{2,0},{3,1},{4,6},{5,7},{6,4},{7,5},{8,10},{9,11},{10,... | collective-permute-start | bytes 393224 | tf_op jit(solution)/shard_map/ppermute | solution.py:31
  41.3 2.6 %collective-permute-start.13 = (bf16[256,256]{1,0:T(8,128)(2,1)S(1)}, bf16[256,256]{1,0:T(8,128)(2,1)S(1)}, u32[]{:S(2)}, u32[]{:S(2)}) collective-permute-start(bf16[256,256]{1,0:T(8,128)(2,1)S(1)} %get-tuple-element.26), channel_id=1, source_target_pairs={{0,4},{1,5},{2,6},{3,7},{4,0},{5,1},{6,2},{7,3},{8,12},{9,13},{10,... | collective-permute-start | bytes 393224 | tf_op jit(solution)/shard_map/ppermute | solution.py:31
  43.9 1.0 %shard_map.93.refs_0_ = bf16[4,528,128]{2,1,0:T(8,128)(2,1)S(1)} custom-call(f32[256,256]{1,0:T(8,128)S(1)} %get-tuple-element.23.refs_0_.refs_1_, bf16[4,256,512]{2,1,0:T(8,128)(2,1)S(1)} %get-tuple-element.24.refs_1_, bf16[272,512]{1,0:T(8,128)(2,1)S(1)} %shard_map.87.refs_2_, bf16[272,512]{1,0:T(8,128)(2,1)S(1)} %collective-permute-done.3.refs_3_, ...), custom_call_target="tpu_custom_call" | custom-call | flops 99999997952 | tf_op jit(solution)/shard_map/pallas_call | solution.py:48
  47.0 7.2 %collective-permute-done.13.refs_3_ = bf16[256,256]{1,0:T(8,128)(2,1)S(1)} collective-permute-done((bf16[256,256]{1,0:T(8,128)(2,1)S(1)}, bf16[256,256]{1,0:T(8,128)(2,1)S(1)}, u32[]{:S(2)}, u32[]{:S(2)}) %collective-permute-start.13) | collective-permute-done | bytes 131104 | tf_op jit(solution)/shard_map/ppermute | solution.py:31
  54.3 2.6 %collective-permute-start.17 = (bf16[256,256]{1,0:T(8,128)(2,1)S(1)}, bf16[256,256]{1,0:T(8,128)(2,1)S(1)}, u32[]{:S(2)}, u32[]{:S(2)}) collective-permute-start(bf16[256,256]{1,0:T(8,128)(2,1)S(1)} %shard_map.95.refs_1_), channel_id=1, source_target_pairs={{0,17},{1,16},{2,19},{3,18},{4,21},{5,20},{6,23},{7,22},{8,25},{9,... | collective-permute-start | bytes 393224 | tf_op jit(solution)/shard_map/ppermute | solution.py:31
  58.3 1.9 %collective-permute-done.17.refs_4_ = bf16[256,256]{1,0:T(8,128)(2,1)S(1)} collective-permute-done((bf16[256,256]{1,0:T(8,128)(2,1)S(1)}, bf16[256,256]{1,0:T(8,128)(2,1)S(1)}, u32[]{:S(2)}, u32[]{:S(2)}) %collective-permute-start.17) | collective-permute-done | bytes 131104 | tf_op jit(solution)/shard_map/ppermute | solution.py:31
  60.3 1.5 %collective-permute-done.16.refs_3_ = bf16[256,256]{1,0:T(8,128)(2,1)S(1)} collective-permute-done((bf16[256,256]{1,0:T(8,128)(2,1)S(1)}, bf16[256,256]{1,0:T(8,128)(2,1)S(1)}, u32[]{:S(2)}, u32[]{:S(2)}) %collective-permute-start.16) | collective-permute-done | bytes 131104 | tf_op jit(solution)/shard_map/ppermute | solution.py:31
  62.3 1.0 %shard_map.94 = bf16[128,2048]{1,0:T(8,128)(2,1)} custom-call(bf16[528,128]{1,0:T(8,128)(2,1)S(1)} %get-tuple-element.31.refs_0_, bf16[528,128]{1,0:T(8,128)(2,1)S(1)} %collective-permute-done.9.refs_1_, bf16[528,128]{1,0:T(8,128)(2,1)S(1)} %collective-permute-done.10.refs_2_, bf16[528,128]{1,0:T(8,128)(2,1)S(1)} %collective-permute-done.11.refs_3_), custom_call_target="tpu_custom_call" | custom-call | tf_op jit(solution)/shard_map/pallas_call | solution.py:48
  63.7 1.9 %shard_map.96 = f32[1024,512]{1,0:T(8,128)} custom-call(s32[7]{0:T(128)S(1)} %stack.23.refs_0_.refs_5_, bf16[256,256]{1,0:T(8,128)(2,1)S(1)} %shard_map.95.refs_1_, bf16[256,256]{1,0:T(8,128)(2,1)S(1)} %collective-permute-done.15.refs_2_, bf16[256,256]{1,0:T(8,128)(2,1)S(1)} %collective-permute-done.16.refs_3_, ...), custom_call_target="tpu_custom_call" | custom-call | tf_op jit(solution)/shard_map/pallas_call | solution.py:48
  (35 shorter events, 6.7 us)
Async XLA Ops:
  1.6 11.9 %collective-permute-start.3 = (bf16[272,512]{1,0:T(8,128)(2,1)S(1)}, bf16[272,512]{1,0:T(8,128)(2,1)S(1)}, u32[]{:S(2)}, u32[]{:S(2)}) collective-permute-start(bf16[272,512]{1,0:T(8,128)(2,1)S(1)} %shard_map.87.refs_2_), channel_id=1, source_target_pairs={{0,1},{1,2},{2,3},{3,4},{4,5},{5,6},{6,7},{8,9},{9,10},{10,11},{11... | collective-permute-start | bytes 835592 | tf_op jit(solution)/shard_map/ppermute | solution.py:26
  8.8 19.1 %collective-permute-start = (bf16[1024,128]{1,0:T(8,128)(2,1)S(1)}, bf16[1024,128]{1,0:T(8,128)(2,1)S(1)}, u32[]{:S(2)}, u32[]{:S(2)}) collective-permute-start(bf16[1024,128]{1,0:T(8,128)(2,1)S(1)} %get-tuple-element.16), channel_id=1, source_target_pairs={{0,1},{1,0},{2,3},{3,2},{4,5},{5,4},{6,7},{7,6},{8,9},{9,8},{10,11... | collective-permute-start | bytes 786440 | tf_op jit(solution)/shard_map/ppermute | solution.py:31
  15.3 7.9 %collective-permute-start.4 = (bf16[128,512]{1,0:T(8,128)(2,1)S(1)}, bf16[128,512]{1,0:T(8,128)(2,1)S(1)}, u32[]{:S(2)}, u32[]{:S(2)}) collective-permute-start(bf16[128,512]{1,0:T(8,128)(2,1)S(1)} %get-tuple-element.22), channel_id=1, source_target_pairs={{1,0},{2,1},{3,2},{4,3},{5,4},{6,5},{7,6},{9,8},{10,9},{11,10},{12... | collective-permute-start | bytes 393224 | tf_op jit(solution)/shard_map/ppermute | solution.py:26
  16.6 11.4 %collective-permute-start.1 = (bf16[1024,128]{1,0:T(8,128)(2,1)S(1)}, bf16[1024,128]{1,0:T(8,128)(2,1)S(1)}, u32[]{:S(2)}, u32[]{:S(2)}) collective-permute-start(bf16[1024,128]{1,0:T(8,128)(2,1)S(1)} %get-tuple-element.17), channel_id=1, source_target_pairs={{0,16},{1,17},{2,18},{3,19},{4,20},{5,21},{6,22},{7,23},{8,24},{9,... | collective-permute-start | bytes 786440 | tf_op jit(solution)/shard_map/ppermute | solution.py:31
  18.1 15.6 %collective-permute-start.2 = (bf16[1024,128]{1,0:T(8,128)(2,1)S(1)}, bf16[1024,128]{1,0:T(8,128)(2,1)S(1)}, u32[]{:S(2)}, u32[]{:S(2)}) collective-permute-start(bf16[1024,128]{1,0:T(8,128)(2,1)S(1)} %get-tuple-element.18), channel_id=1, source_target_pairs={{0,17},{1,16},{2,19},{3,18},{4,21},{5,20},{6,23},{7,22},{8,25},{9,... | collective-permute-start | bytes 786440 | tf_op jit(solution)/shard_map/ppermute | solution.py:31
  23.2 11.9 %collective-permute-start.7 = (bf16[128,512]{1,0:T(8,128)(2,1)S(1)}, bf16[128,512]{1,0:T(8,128)(2,1)S(1)}, u32[]{:S(2)}, u32[]{:S(2)}) collective-permute-start(bf16[128,512]{1,0:T(8,128)(2,1)S(1)} %shard_map.89.refs_5_), channel_id=1, source_target_pairs={{0,17},{1,16},{2,19},{3,18},{4,21},{5,20},{6,23},{7,22},{8,25},{9,... | collective-permute-start | bytes 393224 | tf_op jit(solution)/shard_map/ppermute | solution.py:31
  27.3 7.8 %collective-permute-start.6 = (bf16[128,512]{1,0:T(8,128)(2,1)S(1)}, bf16[128,512]{1,0:T(8,128)(2,1)S(1)}, u32[]{:S(2)}, u32[]{:S(2)}) collective-permute-start(bf16[128,512]{1,0:T(8,128)(2,1)S(1)} %shard_map.89.refs_5_), channel_id=1, source_target_pairs={{0,16},{1,17},{2,18},{3,19},{4,20},{5,21},{6,22},{7,23},{8,24},{9,... | collective-permute-start | bytes 393224 | tf_op jit(solution)/shard_map/ppermute | solution.py:31
  27.8 7.7 %collective-permute-start.5 = (bf16[128,512]{1,0:T(8,128)(2,1)S(1)}, bf16[128,512]{1,0:T(8,128)(2,1)S(1)}, u32[]{:S(2)}, u32[]{:S(2)}) collective-permute-start(bf16[128,512]{1,0:T(8,128)(2,1)S(1)} %shard_map.89.refs_5_), channel_id=1, source_target_pairs={{0,1},{1,0},{2,3},{3,2},{4,5},{5,4},{6,7},{7,6},{8,9},{9,8},{10,11... | collective-permute-start | bytes 393224 | tf_op jit(solution)/shard_map/ppermute | solution.py:31
  36.5 7.4 %copy-start = (s32[1,4]{1,0:T(1,128)S(1)}, s32[1,4]{1,0:T(1,128)}, u32[]{:S(2)}) copy-start(s32[1,4]{1,0:T(1,128)} %param.13) | copy-start | bytes 52
  36.5 2.0 %collective-permute-start.8 = (bf16[1024,256]{1,0:T(8,128)(2,1)S(1)}, bf16[1024,256]{1,0:T(8,128)(2,1)S(1)}, u32[]{:S(2)}, u32[]{:S(2)}) collective-permute-start(bf16[1024,256]{1,0:T(8,128)(2,1)S(1)} %shard_map.91), channel_id=1, source_target_pairs={{0,8},{8,0},{16,24},{24,16},{1,9},{9,1},{17,25},{25,17},{2,10},{10... | collective-permute-start | bytes 1572872 | tf_op jit(solution)/shard_map/ppermute | solution.py:31
  38.6 8.4 %collective-permute-start.12 = (bf16[256,256]{1,0:T(8,128)(2,1)S(1)}, bf16[256,256]{1,0:T(8,128)(2,1)S(1)}, u32[]{:S(2)}, u32[]{:S(2)}) collective-permute-start(bf16[256,256]{1,0:T(8,128)(2,1)S(1)} %get-tuple-element.25), channel_id=1, source_target_pairs={{0,2},{1,3},{2,0},{3,1},{4,6},{5,7},{6,4},{7,5},{8,10},{9,11},{10,... | collective-permute-start | bytes 393224 | tf_op jit(solution)/shard_map/ppermute | solution.py:31
  41.3 12.9 %collective-permute-start.13 = (bf16[256,256]{1,0:T(8,128)(2,1)S(1)}, bf16[256,256]{1,0:T(8,128)(2,1)S(1)}, u32[]{:S(2)}, u32[]{:S(2)}) collective-permute-start(bf16[256,256]{1,0:T(8,128)(2,1)S(1)} %get-tuple-element.26), channel_id=1, source_target_pairs={{0,4},{1,5},{2,6},{3,7},{4,0},{5,1},{6,2},{7,3},{8,12},{9,13},{10,... | collective-permute-start | bytes 393224 | tf_op jit(solution)/shard_map/ppermute | solution.py:31
  43.9 10.3 %collective-permute-start.14 = (bf16[256,256]{1,0:T(8,128)(2,1)S(1)}, bf16[256,256]{1,0:T(8,128)(2,1)S(1)}, u32[]{:S(2)}, u32[]{:S(2)}) collective-permute-start(bf16[256,256]{1,0:T(8,128)(2,1)S(1)} %get-tuple-element.27), channel_id=1, source_target_pairs={{0,6},{1,7},{2,4},{3,5},{4,2},{5,3},{6,0},{7,1},{8,14},{9,15},{10,... | collective-permute-start | bytes 393224 | tf_op jit(solution)/shard_map/ppermute | solution.py:31
  45.0 12.8 %collective-permute-start.11 = (bf16[528,128]{1,0:T(8,128)(2,1)S(1)}, bf16[528,128]{1,0:T(8,128)(2,1)S(1)}, u32[]{:S(2)}, u32[]{:S(2)}) collective-permute-start(bf16[528,128]{1,0:T(8,128)(2,1)S(1)} %get-tuple-element.28), channel_id=1, source_target_pairs={{0,24},{8,16},{16,8},{24,0},{1,25},{9,17},{17,9},{25,1},{2,26},{10... | collective-permute-start | bytes 405512 | tf_op jit(solution)/shard_map/ppermute | solution.py:31
  45.8 12.1 %collective-permute-start.10 = (bf16[528,128]{1,0:T(8,128)(2,1)S(1)}, bf16[528,128]{1,0:T(8,128)(2,1)S(1)}, u32[]{:S(2)}, u32[]{:S(2)}) collective-permute-start(bf16[528,128]{1,0:T(8,128)(2,1)S(1)} %get-tuple-element.29), channel_id=1, source_target_pairs={{0,16},{8,24},{16,0},{24,8},{1,17},{9,25},{17,1},{25,9},{2,18},{10... | collective-permute-start | bytes 405512 | tf_op jit(solution)/shard_map/ppermute | solution.py:31
  54.3 6.0 %collective-permute-start.17 = (bf16[256,256]{1,0:T(8,128)(2,1)S(1)}, bf16[256,256]{1,0:T(8,128)(2,1)S(1)}, u32[]{:S(2)}, u32[]{:S(2)}) collective-permute-start(bf16[256,256]{1,0:T(8,128)(2,1)S(1)} %shard_map.95.refs_1_), channel_id=1, source_target_pairs={{0,17},{1,16},{2,19},{3,18},{4,21},{5,20},{6,23},{7,22},{8,25},{9,... | collective-permute-start | bytes 393224 | tf_op jit(solution)/shard_map/ppermute | solution.py:31
  56.8 5.0 %collective-permute-start.16 = (bf16[256,256]{1,0:T(8,128)(2,1)S(1)}, bf16[256,256]{1,0:T(8,128)(2,1)S(1)}, u32[]{:S(2)}, u32[]{:S(2)}) collective-permute-start(bf16[256,256]{1,0:T(8,128)(2,1)S(1)} %shard_map.95.refs_1_), channel_id=1, source_target_pairs={{0,16},{1,17},{2,18},{3,19},{4,20},{5,21},{6,22},{7,23},{8,24},{9,... | collective-permute-start | bytes 393224 | tf_op jit(solution)/shard_map/ppermute | solution.py:31
  57.4 5.0 %collective-permute-start.15 = (bf16[256,256]{1,0:T(8,128)(2,1)S(1)}, bf16[256,256]{1,0:T(8,128)(2,1)S(1)}, u32[]{:S(2)}, u32[]{:S(2)}) collective-permute-start(bf16[256,256]{1,0:T(8,128)(2,1)S(1)} %shard_map.95.refs_1_), channel_id=1, source_target_pairs={{0,1},{1,0},{2,3},{3,2},{4,5},{5,4},{6,7},{7,6},{8,9},{9,8},{10,11... | collective-permute-start | bytes 393224 | tf_op jit(solution)/shard_map/ppermute | solution.py:31
  57.8 4.5 %collective-permute-start.9 = (bf16[528,128]{1,0:T(8,128)(2,1)S(1)}, bf16[528,128]{1,0:T(8,128)(2,1)S(1)}, u32[]{:S(2)}, u32[]{:S(2)}) collective-permute-start(bf16[528,128]{1,0:T(8,128)(2,1)S(1)} %get-tuple-element.30), channel_id=1, source_target_pairs={{0,8},{8,0},{16,24},{24,16},{1,9},{9,1},{17,25},{25,17},{2,10},{10... | collective-permute-start | bytes 405512 | tf_op jit(solution)/shard_map/ppermute | solution.py:31
  57.8 5.5 %collective-permute-start.18 = (bf16[256,256]{1,0:T(8,128)(2,1)S(1)}, bf16[256,256]{1,0:T(8,128)(2,1)S(1)}, u32[]{:S(2)}, u32[]{:S(2)}) collective-permute-start(bf16[256,256]{1,0:T(8,128)(2,1)S(1)} %shard_map.95.refs_1_), channel_id=1, source_target_pairs={{0,8},{8,0},{16,24},{24,16},{1,9},{9,1},{17,25},{25,17},{2,10},{10... | collective-permute-start | bytes 393224 | tf_op jit(solution)/shard_map/ppermute | solution.py:31
  60.3 3.1 %collective-permute-start.21 = (bf16[256,256]{1,0:T(8,128)(2,1)S(1)}, bf16[256,256]{1,0:T(8,128)(2,1)S(1)}, u32[]{:S(2)}, u32[]{:S(2)}) collective-permute-start(bf16[256,256]{1,0:T(8,128)(2,1)S(1)} %collective-permute-done.17.refs_4_), channel_id=1, source_target_pairs={{0,8},{8,0},{16,24},{24,16},{1,9},{9,1},{17,25},{25,17},{2,10},{10... | collective-permute-start | bytes 393224 | tf_op jit(solution)/shard_map/ppermute | solution.py:31
  61.8 1.5 %collective-permute-start.20 = (bf16[256,256]{1,0:T(8,128)(2,1)S(1)}, bf16[256,256]{1,0:T(8,128)(2,1)S(1)}, u32[]{:S(2)}, u32[]{:S(2)}) collective-permute-start(bf16[256,256]{1,0:T(8,128)(2,1)S(1)} %collective-permute-done.16.refs_3_), channel_id=1, source_target_pairs={{0,8},{8,0},{16,24},{24,16},{1,9},{9,1},{17,25},{25,17},{2,10},{10... | collective-permute-start | bytes 393224 | tf_op jit(solution)/shard_map/ppermute | solution.py:31
  62.3 1.3 %collective-permute-start.19 = (bf16[256,256]{1,0:T(8,128)(2,1)S(1)}, bf16[256,256]{1,0:T(8,128)(2,1)S(1)}, u32[]{:S(2)}, u32[]{:S(2)}) collective-permute-start(bf16[256,256]{1,0:T(8,128)(2,1)S(1)} %collective-permute-done.15.refs_2_), channel_id=1, source_target_pairs={{0,8},{8,0},{16,24},{24,16},{1,9},{9,1},{17,25},{25,17},{2,10},{10... | collective-permute-start | bytes 393224 | tf_op jit(solution)/shard_map/ppermute | solution.py:31

commit v3 on v2

--- a/solution.py
+++ b/solution.py
@@ -31,6 +31,11 @@
     return lax.ppermute(value, axis, [(i, i ^ mask) for i in range(devices)])
 
 
+def chip_at():
+    dp = lax.axis_index("dp")
+    return dp % CORES, dp // CORES, lax.axis_index("ctx"), lax.axis_index("rep")
+
+
 def vmem():
     return pl.BlockSpec(memory_space=pltpu.VMEM)
 
@@ -39,7 +44,7 @@
     return pl.BlockSpec(memory_space=pltpu.SMEM)
 
 
-def call(body, outs, ins, weight=0, deps=(), hbm_in=(), hbm_out=(), scratch=()):
+def call(body, outs, ins, weight=0, deps=(), hbm_in=(), hbm_out=(), scratch=(), alias={}):
     space = pl.BlockSpec(memory_space=pltpu.HBM)
     ins_at = [smem() if a.dtype == jnp.int32 and a.ndim == 1 else vmem() for a in ins]
     ins_at = [space if i in hbm_in else at for i, at in enumerate(ins_at)]
@@ -47,10 +52,11 @@
     ins = [pltpu.with_memory_space_constraint(a, pltpu.HBM) if i in hbm_in else a for i, a in enumerate(ins)]
     return pl.pallas_call(
         lambda *refs: body(*refs[skip:]),
-        out_shape=outs,
+        out_shape=[pltpu.HBM(o.shape, o.dtype) if i in hbm_out else o for i, o in enumerate(outs)],
         in_specs=[space] * skip + ins_at,
         out_specs=[space if i in hbm_out else vmem() for i in range(len(outs))],
         scratch_shapes=list(scratch),
+        input_output_aliases={skip + i: o for i, o in alias.items()},
         cost_estimate=pl.CostEstimate(flops=weight * 10**9, bytes_accessed=0, transcendentals=0),
         compiler_params=pltpu.CompilerParams(vmem_limit_bytes=32 * 2**20),
     )(*deps, *ins)
@@ -124,12 +130,12 @@
         own_ref[:, col] = dot(po, g4, ((1,), (0,)))
 
 
-def attend_body(blocks, pt_ref, message_ref, prior_ref, plan_ref, idx_ref, out_ref):
+def attend_body(blocks, pt_ref, message_ref, prior_ref, plan_ref, out_ref):
     tokens = pt_ref.shape[1] // 2
     rows = tokens // blocks
     owners = out_ref.shape[0]
     data = KV_HEADS * GROUP * rows
-    me = idx_ref[0]
+    me = lax.axis_index("dp")
     if owners > blocks:
         out_ref[...] = jnp.zeros(out_ref.shape, BF16)
     slots = [plan_ref[j] ^ me for j in range(blocks)]
@@ -170,7 +176,7 @@
             copy.wait()
 
 
-def split_body(reduced, places, idx_ref, in_hbm, q_hbm, g_hbm, *refs):
+def split_body(reduced, places, chips, in_hbm, q_hbm, g_hbm, *refs):
     spread = len(places)
     outs, (q_ref, g_ref, in_ref, sems) = refs[:spread], refs[spread:]
     copies = [
@@ -180,8 +186,8 @@
     for copy in copies:
         copy.start()
     sub = in_ref.shape[1] // (spread * len(reduced))
-    x, y, z = idx_ref[2], idx_ref[3], idx_ref[4]
-    reps, chips = idx_ref[5], idx_ref[6]
+    core, x, z, y = chip_at()
+    reps = lax.axis_size("rep")
     copies[0].wait()
     for k, (kx, kz, ky) in enumerate(places):
         for m, (mx, mz, my) in enumerate(reduced):
@@ -196,11 +202,11 @@
     out_ref[...] = (own_ref[...] + ret_ref[...].astype(F32)).astype(BF16)
 
 
-def product_body(cross, idx_ref, *refs):
+def product_body(cross, *refs):
     *ins, out_ref = refs
     count = len(ins) // 2
     half = out_ref.shape[1]
-    core = idx_ref[1] ^ 1 if cross else idx_ref[1]
+    core = chip_at()[0] ^ cross
     cols = pl.ds(pl.multiple_of(core * half, half), half)
     a = jnp.concatenate([ref[...] for ref in ins[:count]], 1)
     b = jnp.concatenate([ref[:, cols] for ref in ins[count:]], 0)
@@ -222,19 +228,19 @@
     out_ref[...] = total.astype(BF16)
 
 
-def spread_body(chips, idx_ref, *refs):
-    mine, other, (out_hbm, wide_ref, sems) = refs[:chips], refs[chips : 2 * chips], refs[2 * chips :]
-    sub, half = mine[0].shape
-    c, q = idx_ref[1], idx_ref[2] * idx_ref[5] + idx_ref[3]
+def spread_body(blocks, *refs):
+    pieces = refs[: len(blocks)]
+    out_hbm, wide_ref, sems = refs[-3:]
+    sub, half = pieces[0].shape
+    core, x, _, y = chip_at()
+    q = x * lax.axis_size("rep") + y
     copies = []
-    for k in range(chips):
+    for i, (k, other) in enumerate(blocks):
+        wide_ref[i] = pieces[i][...].astype(F32)
         rows = pl.ds(pl.multiple_of((q ^ k) * sub, sub), sub)
-        for i, (ref, core) in enumerate(((mine[k], c), (other[k], 1 - c))):
-            at = 2 * k + i
-            wide_ref[at] = ref[...].astype(F32)
-            to = out_hbm.at[rows, pl.ds(pl.multiple_of(core * half, half), half)]
-            copies.append(pltpu.make_async_copy(wide_ref.at[at], to, sems.at[at]))
-            copies[-1].start()
+        cols = pl.ds(pl.multiple_of((core ^ other) * half, half), half)
+        copies.append(pltpu.make_async_copy(wide_ref.at[i], out_hbm.at[rows, cols], sems.at[i]))
+        copies[i].start()
     for copy in copies:
         copy.wait()
 
@@ -264,11 +270,9 @@
     chips = micro // CORES * reps
     blocks = plan.shape[1]
     rows = tokens // blocks
-    dp, ctx, rep = (lax.axis_index(axis) for axis in ("dp", "ctx", "rep"))
-    idx = jnp.stack([dp, dp % CORES, dp // CORES, rep, ctx, reps, chips]).astype(jnp.int32)
-
-    places = [(kx, 0, ky) for kx in range(micro // CORES) for ky in range(reps)]
-    reduced = [(0, mz, 0) for mz in range(owners)]
+
+    places = [(kx, kz, 0) for kx in range(micro // CORES) for kz in range(2)]
+    reduced = [(0, 2 * mz, my) for mz in range(owners // 2) for my in range(reps)]
     every = ("dp", "ctx", "rep")
 
     def away(value, x, z, y):
@@ -288,15 +292,16 @@
 
     if by_chips:
         *pieces, q_rows, g_rows = call(
-            functools.partial(split_body, reduced, places),
+            functools.partial(split_body, reduced, places, chips),
             [shape(len(reduced) * sub, tokens)] * len(places) + [shape(tokens, q_width)] * 2,
-            [idx, inputs[0], queries[0], grad_out[0]],
-            hbm_in=(1, 2, 3),
+            [inputs[0], queries[0], grad_out[0]],
+            hbm_in=(0, 1, 2),
             scratch=[pltpu.VMEM((tokens, width), BF16), pltpu.SemaphoreType.DMA((3,))],
         )
 
         def gather(value_of):
-            return [value_of(0)] + [away(value_of(k), *place) for k, place in enumerate(places) if k]
+            far_first = [away(value_of(k), *place) for k, place in reversed([*enumerate(places)]) if k]
+            return far_first + [value_of(0)]
 
         mine_in = gather(lambda k: pieces[k])
     else:
@@ -314,24 +319,24 @@
     )
     returned = from_behind(back, shards, -1)
     if by_chips:
-        (grad_values,) = call(both_body, [shape(tokens, kv_width)], [own, returned])
+        (grad_values,) = call(both_body, [shape(tokens, kv_width)], [own, returned], deps=mine_in[1:3])
         grads = gather(lambda k: grad_values)
-        factors = [idx, *mine_in, *grads]
-        (cross,) = call(functools.partial(product_body, True), [shape(len(reduced) * sub, half)], factors)
+        factors = [*mine_in, *grads]
+        (cross,) = call(functools.partial(product_body, 1), [shape(len(reduced) * sub, half)], factors)
         (kept,) = call(
-            functools.partial(product_body, False), [shape(len(reduced) * sub, half, dtype=F32)], factors, weight=3
+            functools.partial(product_body, 0), [shape(len(reduced) * sub, half, dtype=F32)], factors, weight=3
         )
         partial = call(
             add_body,
             [shape(sub, half, dtype=F32)] + [shape(sub, half)] * (len(reduced) - 1),
             [kept, swap(cross, "dp", 1)],
         )
-        arrived = [away(partial[m], *place) for m, place in enumerate(reduced) if m]
+        arrived = [away(partial[m], *reduced[m]) for m in (*range(2, len(reduced)), 1)]
 
     (outgoing,) = call(
         functools.partial(attend_body, blocks),
         [shape(micro, (q_width // LANES) * rows + LABEL_ROWS, LANES)],
-        [probs, message, prior, plan[0], idx],
+        [probs, message, prior, plan[0]],
         weight=100,
         deps=[partial[0]] if by_chips else [],
     )
@@ -343,18 +348,31 @@
         arrived_out,
         hbm_out=(0,),
         scratch=[pltpu.VMEM((micro, rows, q_width), BF16), pltpu.SemaphoreType.DMA((micro,))],
+        weight=2,
     )
     if by_chips:
         (total,) = call(sum_body, [shape(sub, half)], [partial[0], *arrived], deps=[outgoing])
-        mine_out = [total] + [away(total, k // reps, 0, k % reps) for k in range(1, chips)]
-        other_out = [swap(p, "dp", 1) for p in mine_out]
-        (weight_grad,) = call(
-            functools.partial(spread_body, chips),
-            [shape(chips * sub, kv_width, dtype=F32)],
-            [idx, *mine_out, *other_out],
-            hbm_out=(0,),
-            scratch=[pltpu.VMEM((2 * chips, sub, half), F32), pltpu.SemaphoreType.DMA((2 * chips,))],
-        )
+        last = chips - 1
+        sums = [away(total, k // reps, 0, k % reps) for k in reversed(range(1, chips))]
+        sums = [total, *reversed(sums)]
+        others = [swap(p, "dp", 1) for p in sums]
+
+        def spread(chosen, so_far=(), weight=0):
+            blocks = [(k, other) for k in chosen for other in range(CORES)]
+            pieces = [(others if other else sums)[k] for k, other in blocks]
+            (result,) = call(
+                functools.partial(spread_body, blocks),
+                [shape(chips * sub, kv_width, dtype=F32)],
+                [*pieces, *so_far],
+                weight=weight,
+                hbm_in=(len(pieces),),
+                hbm_out=(0,),
+                scratch=[pltpu.VMEM((len(blocks), sub, half), F32), pltpu.SemaphoreType.DMA((len(blocks),))],
+                alias={len(pieces): 0} if so_far else {},
+            )
+            return result
+
+        weight_grad = spread([last], [spread(range(last), weight=2)])
     else:
         weight_grad = weight_by_collectives(inputs[0], own, returned)
     return (placed[None], weight_grad)

time: 66 us -> 62.8 us (0.952)
  waiting for transfers between devices: 25.6 us -> 21.9 us
  starting transfers between devices: 28.2 us -> 30.5 us
  Pallas kernels: 10.9 us -> 9.36 us
    ppermute x2, waiting for transfers between devices: 5.22 us -> 1.17 us  [from_behind(): return lax.ppermute(value, axis, pairs)]
    ppermute x20, starting transfers between devices: 22.1 us -> 24.3 us  [swap(): return lax.ppermute(value, axis, [(i, i ^ mask) for i in range(devices)])]
    pallas_call x11 -> x12, Pallas kernels: 10.9 us -> 9.36 us  [call(): pl.pallas_call(lambda *refs: body(*refs[skip:]), out_shape=[pltpu.HBM(o.s...]
  transfers between devices with their start and end apart: 22 -> 22, of which waited for: 12 -> 11; matrix products, arithmetic and copies ran while one was open for 0% -> 0% of each run, Pallas kernels for 10% -> 11%
where the time goes in v3:
time: 62.8 us; the launch traced here: 62.6 us
  starting transfers between devices  30.5 us (49%)
  waiting for transfers between devices  21.9 us (35%)
  Pallas kernels  9.36 us (15%)
  between operations  0.79 us (1%)
    ppermute x20, starting transfers between devices, swap(): return lax.ppermute(value, axis, [(i, i ^ mask) for i in range(devices)])  24.3 us
    ppermute x20, waiting for transfers between devices, swap(): return lax.ppermute(value, axis, [(i, i ^ mask) for i in range(devices)])  20.8 us
    pallas_call x12, Pallas kernels, call(): pl.pallas_call(lambda *refs: body(*refs[skip:]), out_shape=[pltpu.HBM(o.s...  9.36 us
    ppermute x2, starting transfers between devices, from_behind(): return lax.ppermute(value, axis, pairs)  6.18 us
  transfers between devices with their start and end apart: 22, of which 11 were waited for; matrix products, arithmetic and copies ran while one was open for 0% of the time, Pallas kernels for 11%

profile of v3, /device:TPU:0, one launch (start us, length us, event | category | flops | bytes accessed | tf_op | source)
XLA Modules:
  0.0 62.6 jit_solution(10372579259056107567)
XLA Ops:
  0.6 1.0 %shard_map.87.refs_2_ = bf16[272,512]{1,0:T(8,128)(2,1)S(1)} custom-call(bf16[128,512]{1,0:T(8,128)(2,1)} %bitcast.19, bf16[128,512]{1,0:T(8,128)(2,1)} %bitcast.20, s32[1,128]{1,0:T(1,128)} %refs_2_.1), custom_call_target="tpu_custom_call" | custom-call | tf_op jit(solution)/shard_map/pallas_call | solution.py:53
  1.6 4.9 %collective-permute-start.3 = (bf16[272,512]{1,0:T(8,128)(2,1)S(1)}, bf16[272,512]{1,0:T(8,128)(2,1)S(1)}, u32[]{:S(2)}, u32[]{:S(2)}) collective-permute-start(bf16[272,512]{1,0:T(8,128)(2,1)S(1)} %shard_map.87.refs_2_), channel_id=1, source_target_pairs={{0,1},{1,2},{2,3},{3,4},{4,5},{5,6},{6,7},{8,9},{9,10},{10,11},{11... | collective-permute-start | bytes 835592 | tf_op jit(solution)/shard_map/ppermute | solution.py:26
  6.5 1.6 %shard_map.86 = (bf16[1024,128]{1,0:T(8,128)(2,1)S(1)}, bf16[1024,128]{1,0:T(8,128)(2,1)S(1)}, bf16[1024,128]{1,0:T(8,128)(2,1)S(1)}, bf16[1024,128]{1,0:T(8,128...) custom-call(bf16[128,4096]{1,0:T(8,128)(2,1)} %bitcast.16, bf16[128,2048]{1,0:T(8,128)(2,1)} %bitcast.17, ...), custom_call_target="tpu_custom_call" | custom-call | tf_op jit(solution)/shard_map/pallas_call | solution.py:53
  8.1 1.6 %collective-permute-start.1 = (bf16[1024,128]{1,0:T(8,128)(2,1)S(1)}, bf16[1024,128]{1,0:T(8,128)(2,1)S(1)}, u32[]{:S(2)}, u32[]{:S(2)}) collective-permute-start(bf16[1024,128]{1,0:T(8,128)(2,1)S(1)} %get-tuple-element.16), channel_id=1, source_target_pairs={{0,16},{1,17},{2,18},{3,19},{4,20},{5,21},{6,22},{7,23},{8,24},{9,... | collective-permute-start | bytes 786440 | tf_op jit(solution)/shard_map/ppermute | solution.py:31
  9.7 1.6 %collective-permute-start.2 = (bf16[1024,128]{1,0:T(8,128)(2,1)S(1)}, bf16[1024,128]{1,0:T(8,128)(2,1)S(1)}, u32[]{:S(2)}, u32[]{:S(2)}) collective-permute-start(bf16[1024,128]{1,0:T(8,128)(2,1)S(1)} %get-tuple-element.17), channel_id=1, source_target_pairs={{0,2},{1,3},{2,0},{3,1},{4,6},{5,7},{6,4},{7,5},{8,10},{9,11},{10,... | collective-permute-start | bytes 786440 | tf_op jit(solution)/shard_map/ppermute | solution.py:31
  11.2 1.2 %collective-permute-done.3.refs_3_ = bf16[272,512]{1,0:T(8,128)(2,1)S(1)} collective-permute-done((bf16[272,512]{1,0:T(8,128)(2,1)S(1)}, bf16[272,512]{1,0:T(8,128)(2,1)S(1)}, u32[]{:S(2)}, u32[]{:S(2)}) %collective-permute-start.3) | collective-permute-done | bytes 278560 | tf_op jit(solution)/shard_map/ppermute | solution.py:26
  12.4 1.7 %shard_map.88 = (bf16[4,256,512]{2,1,0:T(8,128)(2,1)S(1)}, bf16[128,512]{1,0:T(8,128)(2,1)S(1)}, f32[128,512]{1,0:T(8,128)S(1)}) custom-call(bf16[128,2048]{1,0:T(8,128)(2,1)S(1)} %get-tuple-element.19.refs_0_, bf16[128,2048]{1,0:T(8,128)(2,1)S(1)} %get-tuple-element.20.refs_1_, bf16[272,512]{1,0:T(8,128)(2,1)S(1)} %shard_map.87.refs_2_, ...), custom_call_target="tpu_custom_call" | custom-call | flops 99999997952 | tf_op jit(solution)/shard_map/pallas_call | solution.py:53
  14.1 1.3 %collective-permute-start.4 = (bf16[128,512]{1,0:T(8,128)(2,1)S(1)}, bf16[128,512]{1,0:T(8,128)(2,1)S(1)}, u32[]{:S(2)}, u32[]{:S(2)}) collective-permute-start(bf16[128,512]{1,0:T(8,128)(2,1)S(1)} %get-tuple-element.22), channel_id=1, source_target_pairs={{1,0},{2,1},{3,2},{4,3},{5,4},{6,5},{7,6},{9,8},{10,9},{11,10},{12... | collective-permute-start | bytes 393224 | tf_op jit(solution)/shard_map/ppermute | solution.py:26
  15.4 6.2 %collective-permute-start = (bf16[1024,128]{1,0:T(8,128)(2,1)S(1)}, bf16[1024,128]{1,0:T(8,128)(2,1)S(1)}, u32[]{:S(2)}, u32[]{:S(2)}) collective-permute-start(bf16[1024,128]{1,0:T(8,128)(2,1)S(1)} %get-tuple-element.15), channel_id=1, source_target_pairs={{0,18},{1,19},{2,16},{3,17},{4,22},{5,23},{6,20},{7,21},{8,26},{9,... | collective-permute-start | bytes 786440 | tf_op jit(solution)/shard_map/ppermute | solution.py:31
  21.7 4.0 %collective-permute-start.7 = (bf16[128,512]{1,0:T(8,128)(2,1)S(1)}, bf16[128,512]{1,0:T(8,128)(2,1)S(1)}, u32[]{:S(2)}, u32[]{:S(2)}) collective-permute-start(bf16[128,512]{1,0:T(8,128)(2,1)S(1)} %shard_map.89.refs_7_), channel_id=1, source_target_pairs={{0,2},{1,3},{2,0},{3,1},{4,6},{5,7},{6,4},{7,5},{8,10},{9,11},{10,... | collective-permute-start | bytes 393224 | tf_op jit(solution)/shard_map/ppermute | solution.py:31
  25.6 1.5 %collective-permute-start.6 = (bf16[128,512]{1,0:T(8,128)(2,1)S(1)}, bf16[128,512]{1,0:T(8,128)(2,1)S(1)}, u32[]{:S(2)}, u32[]{:S(2)}) collective-permute-start(bf16[128,512]{1,0:T(8,128)(2,1)S(1)} %shard_map.89.refs_7_), channel_id=1, source_target_pairs={{0,16},{1,17},{2,18},{3,19},{4,20},{5,21},{6,22},{7,23},{8,24},{9,... | collective-permute-start | bytes 393224 | tf_op jit(solution)/shard_map/ppermute | solution.py:31
  27.2 4.4 %collective-permute-done.refs_0_ = bf16[1024,128]{1,0:T(8,128)(2,1)S(1)} collective-permute-done((bf16[1024,128]{1,0:T(8,128)(2,1)S(1)}, bf16[1024,128]{1,0:T(8,128)(2,1)S(1)}, u32[]{:S(2)}, u32[]{:S(2)}) %collective-permute-start) | collective-permute-done | bytes 262176 | tf_op jit(solution)/shard_map/ppermute | solution.py:31
  33.0 1.4 %collective-permute-done.5.refs_4_ = bf16[128,512]{1,0:T(8,128)(2,1)S(1)} collective-permute-done((bf16[128,512]{1,0:T(8,128)(2,1)S(1)}, bf16[128,512]{1,0:T(8,128)(2,1)S(1)}, u32[]{:S(2)}, u32[]{:S(2)}) %collective-permute-start.5) | collective-permute-done | bytes 131104 | tf_op jit(solution)/shard_map/ppermute | solution.py:31
  35.4 1.4 %collective-permute-done.8.refs_1_ = bf16[1024,256]{1,0:T(8,128)(2,1)S(1)} collective-permute-done((bf16[1024,256]{1,0:T(8,128)(2,1)S(1)}, bf16[1024,256]{1,0:T(8,128)(2,1)S(1)}, u32[]{:S(2)}, u32[]{:S(2)}) %collective-permute-start.8) | collective-permute-done | bytes 524320 | tf_op jit(solution)/shard_map/ppermute | solution.py:31
  37.0 2.7 %collective-permute-start.12 = (bf16[256,256]{1,0:T(8,128)(2,1)S(1)}, bf16[256,256]{1,0:T(8,128)(2,1)S(1)}, u32[]{:S(2)}, u32[]{:S(2)}) collective-permute-start(bf16[256,256]{1,0:T(8,128)(2,1)S(1)} %get-tuple-element.25), channel_id=1, source_target_pairs={{0,4},{1,5},{2,6},{3,7},{4,0},{5,1},{6,2},{7,3},{8,12},{9,13},{10,... | collective-permute-start | bytes 393224 | tf_op jit(solution)/shard_map/ppermute | solution.py:31
  39.6 1.8 %collective-permute-start.14 = (bf16[256,256]{1,0:T(8,128)(2,1)S(1)}, bf16[256,256]{1,0:T(8,128)(2,1)S(1)}, u32[]{:S(2)}, u32[]{:S(2)}) collective-permute-start(bf16[256,256]{1,0:T(8,128)(2,1)S(1)} %get-tuple-element.27), channel_id=1, source_target_pairs={{0,1},{1,0},{2,3},{3,2},{4,5},{5,4},{6,7},{7,6},{8,9},{9,8},{10,11... | collective-permute-start | bytes 393224 | tf_op jit(solution)/shard_map/ppermute | solution.py:31
  41.4 1.0 %shard_map.93.refs_0_ = bf16[4,528,128]{2,1,0:T(8,128)(2,1)S(1)} custom-call(f32[256,256]{1,0:T(8,128)S(1)} %get-tuple-element.23.refs_0_.refs_1_, bf16[4,256,512]{2,1,0:T(8,128)(2,1)S(1)} %get-tuple-element.24.refs_1_, bf16[272,512]{1,0:T(8,128)(2,1)S(1)} %shard_map.87.refs_2_, bf16[272,512]{1,0:T(8,128)(2,1)S(1)} %collective-permute-done.3.refs_3_, ...), custom_call_target="tpu_custom_call" | custom-call | flops 99999997952 | tf_op jit(solution)/shard_map/pallas_call | solution.py:53
  43.5 4.2 %collective-permute-done.12.refs_2_ = bf16[256,256]{1,0:T(8,128)(2,1)S(1)} collective-permute-done((bf16[256,256]{1,0:T(8,128)(2,1)S(1)}, bf16[256,256]{1,0:T(8,128)(2,1)S(1)}, u32[]{:S(2)}, u32[]{:S(2)}) %collective-permute-start.12) | collective-permute-done | bytes 131104 | tf_op jit(solution)/shard_map/ppermute | solution.py:31
  47.7 3.2 %collective-permute-done.13.refs_3_ = bf16[256,256]{1,0:T(8,128)(2,1)S(1)} collective-permute-done((bf16[256,256]{1,0:T(8,128)(2,1)S(1)}, bf16[256,256]{1,0:T(8,128)(2,1)S(1)}, u32[]{:S(2)}, u32[]{:S(2)}) %collective-permute-start.13) | collective-permute-done | bytes 131104 | tf_op jit(solution)/shard_map/ppermute | solution.py:31
  51.9 1.5 %collective-permute-start.18 = (bf16[256,256]{1,0:T(8,128)(2,1)S(1)}, bf16[256,256]{1,0:T(8,128)(2,1)S(1)}, u32[]{:S(2)}, u32[]{:S(2)}) collective-permute-start(bf16[256,256]{1,0:T(8,128)(2,1)S(1)} %shard_map.95.refs_0_), channel_id=1, source_target_pairs={{0,1},{1,0},{2,3},{3,2},{4,5},{5,4},{6,7},{7,6},{8,9},{9,8},{10,11... | collective-permute-start | bytes 393224 | tf_op jit(solution)/shard_map/ppermute | solution.py:31
  53.4 1.1 %collective-permute-start.15 = (bf16[256,256]{1,0:T(8,128)(2,1)S(1)}, bf16[256,256]{1,0:T(8,128)(2,1)S(1)}, u32[]{:S(2)}, u32[]{:S(2)}) collective-permute-start(bf16[256,256]{1,0:T(8,128)(2,1)S(1)} %shard_map.95.refs_0_), channel_id=1, source_target_pairs={{0,17},{1,16},{2,19},{3,18},{4,21},{5,20},{6,23},{7,22},{8,25},{9,... | collective-permute-start | bytes 393224 | tf_op jit(solution)/shard_map/ppermute | solution.py:31
  54.6 1.4 %collective-permute-done.20.refs_4_ = bf16[256,256]{1,0:T(8,128)(2,1)S(1)} collective-permute-done((bf16[256,256]{1,0:T(8,128)(2,1)S(1)}, bf16[256,256]{1,0:T(8,128)(2,1)S(1)}, u32[]{:S(2)}, u32[]{:S(2)}) %collective-permute-start.20) | collective-permute-done | bytes 131104 | tf_op jit(solution)/shard_map/ppermute | solution.py:31
  56.0 3.0 %collective-permute-done.18.refs_2_ = bf16[256,256]{1,0:T(8,128)(2,1)S(1)} collective-permute-done((bf16[256,256]{1,0:T(8,128)(2,1)S(1)}, bf16[256,256]{1,0:T(8,128)(2,1)S(1)}, u32[]{:S(2)}, u32[]{:S(2)}) %collective-permute-start.18) | collective-permute-done | bytes 131104 | tf_op jit(solution)/shard_map/ppermute | solution.py:31
  60.5 1.2 %shard_map.96.refs_2_ = f32[1024,512]{1,0:T(8,128)} custom-call(bf16[256,256]{1,0:T(8,128)(2,1)S(1)} %shard_map.95.refs_0_, bf16[256,256]{1,0:T(8,128)(2,1)S(1)} %collective-permute-done.17.refs_1_, bf16[256,256]{1,0:T(8,128)(2,1)S(1)} %collective-permute-done.18.refs_2_, bf16[256,256]{1,0:T(8,128)(2,1)S(1)} %collective-permute-done.19.refs_3_, ...), custom_call_target="tpu_custom_call" | custom-call | flops 2000000000 | tf_op jit(solution)/shard_map/pallas_call | solution.py:53
  (35 shorter events, 7.0 us)
Async XLA Ops:
  1.6 10.8 %collective-permute-start.3 = (bf16[272,512]{1,0:T(8,128)(2,1)S(1)}, bf16[272,512]{1,0:T(8,128)(2,1)S(1)}, u32[]{:S(2)}, u32[]{:S(2)}) collective-permute-start(bf16[272,512]{1,0:T(8,128)(2,1)S(1)} %shard_map.87.refs_2_), channel_id=1, source_target_pairs={{0,1},{1,2},{2,3},{3,4},{4,5},{5,6},{6,7},{8,9},{9,10},{10,11},{11... | collective-permute-start | bytes 835592 | tf_op jit(solution)/shard_map/ppermute | solution.py:26
  8.1 13.5 %collective-permute-start.1 = (bf16[1024,128]{1,0:T(8,128)(2,1)S(1)}, bf16[1024,128]{1,0:T(8,128)(2,1)S(1)}, u32[]{:S(2)}, u32[]{:S(2)}) collective-permute-start(bf16[1024,128]{1,0:T(8,128)(2,1)S(1)} %get-tuple-element.16), channel_id=1, source_target_pairs={{0,16},{1,17},{2,18},{3,19},{4,20},{5,21},{6,22},{7,23},{8,24},{9,... | collective-permute-start | bytes 786440 | tf_op jit(solution)/shard_map/ppermute | solution.py:31
  9.7 11.9 %collective-permute-start.2 = (bf16[1024,128]{1,0:T(8,128)(2,1)S(1)}, bf16[1024,128]{1,0:T(8,128)(2,1)S(1)}, u32[]{:S(2)}, u32[]{:S(2)}) collective-permute-start(bf16[1024,128]{1,0:T(8,128)(2,1)S(1)} %get-tuple-element.17), channel_id=1, source_target_pairs={{0,2},{1,3},{2,0},{3,1},{4,6},{5,7},{6,4},{7,5},{8,10},{9,11},{10,... | collective-permute-start | bytes 786440 | tf_op jit(solution)/shard_map/ppermute | solution.py:31
  14.1 7.5 %collective-permute-start.4 = (bf16[128,512]{1,0:T(8,128)(2,1)S(1)}, bf16[128,512]{1,0:T(8,128)(2,1)S(1)}, u32[]{:S(2)}, u32[]{:S(2)}) collective-permute-start(bf16[128,512]{1,0:T(8,128)(2,1)S(1)} %get-tuple-element.22), channel_id=1, source_target_pairs={{1,0},{2,1},{3,2},{4,3},{5,4},{6,5},{7,6},{9,8},{10,9},{11,10},{12... | collective-permute-start | bytes 393224 | tf_op jit(solution)/shard_map/ppermute | solution.py:26
  15.4 16.2 %collective-permute-start = (bf16[1024,128]{1,0:T(8,128)(2,1)S(1)}, bf16[1024,128]{1,0:T(8,128)(2,1)S(1)}, u32[]{:S(2)}, u32[]{:S(2)}) collective-permute-start(bf16[1024,128]{1,0:T(8,128)(2,1)S(1)} %get-tuple-element.15), channel_id=1, source_target_pairs={{0,18},{1,19},{2,16},{3,17},{4,22},{5,23},{6,20},{7,21},{8,26},{9,... | collective-permute-start | bytes 786440 | tf_op jit(solution)/shard_map/ppermute | solution.py:31
  21.7 10.5 %collective-permute-start.7 = (bf16[128,512]{1,0:T(8,128)(2,1)S(1)}, bf16[128,512]{1,0:T(8,128)(2,1)S(1)}, u32[]{:S(2)}, u32[]{:S(2)}) collective-permute-start(bf16[128,512]{1,0:T(8,128)(2,1)S(1)} %shard_map.89.refs_7_), channel_id=1, source_target_pairs={{0,2},{1,3},{2,0},{3,1},{4,6},{5,7},{6,4},{7,5},{8,10},{9,11},{10,... | collective-permute-start | bytes 393224 | tf_op jit(solution)/shard_map/ppermute | solution.py:31
  25.6 7.4 %collective-permute-start.6 = (bf16[128,512]{1,0:T(8,128)(2,1)S(1)}, bf16[128,512]{1,0:T(8,128)(2,1)S(1)}, u32[]{:S(2)}, u32[]{:S(2)}) collective-permute-start(bf16[128,512]{1,0:T(8,128)(2,1)S(1)} %shard_map.89.refs_7_), channel_id=1, source_target_pairs={{0,16},{1,17},{2,18},{3,19},{4,20},{5,21},{6,22},{7,23},{8,24},{9,... | collective-permute-start | bytes 393224 | tf_op jit(solution)/shard_map/ppermute | solution.py:31
  27.1 7.3 %collective-permute-start.5 = (bf16[128,512]{1,0:T(8,128)(2,1)S(1)}, bf16[128,512]{1,0:T(8,128)(2,1)S(1)}, u32[]{:S(2)}, u32[]{:S(2)}) collective-permute-start(bf16[128,512]{1,0:T(8,128)(2,1)S(1)} %shard_map.89.refs_7_), channel_id=1, source_target_pairs={{0,18},{1,19},{2,16},{3,17},{4,22},{5,23},{6,20},{7,21},{8,26},{9,... | collective-permute-start | bytes 393224 | tf_op jit(solution)/shard_map/ppermute | solution.py:31
  34.9 6.5 %copy-start = (s32[1,4]{1,0:T(1,128)S(1)}, s32[1,4]{1,0:T(1,128)}, u32[]{:S(2)}) copy-start(s32[1,4]{1,0:T(1,128)} %param.13) | copy-start | bytes 52
  34.9 2.0 %collective-permute-start.8 = (bf16[1024,256]{1,0:T(8,128)(2,1)S(1)}, bf16[1024,256]{1,0:T(8,128)(2,1)S(1)}, u32[]{:S(2)}, u32[]{:S(2)}) collective-permute-start(bf16[1024,256]{1,0:T(8,128)(2,1)S(1)} %shard_map.91), channel_id=1, source_target_pairs={{0,8},{8,0},{16,24},{24,16},{1,9},{9,1},{17,25},{25,17},{2,10},{10... | collective-permute-start | bytes 1572872 | tf_op jit(solution)/shard_map/ppermute | solution.py:31
  37.0 10.8 %collective-permute-start.12 = (bf16[256,256]{1,0:T(8,128)(2,1)S(1)}, bf16[256,256]{1,0:T(8,128)(2,1)S(1)}, u32[]{:S(2)}, u32[]{:S(2)}) collective-permute-start(bf16[256,256]{1,0:T(8,128)(2,1)S(1)} %get-tuple-element.25), channel_id=1, source_target_pairs={{0,4},{1,5},{2,6},{3,7},{4,0},{5,1},{6,2},{7,3},{8,12},{9,13},{10,... | collective-permute-start | bytes 393224 | tf_op jit(solution)/shard_map/ppermute | solution.py:31
  39.6 11.3 %collective-permute-start.13 = (bf16[256,256]{1,0:T(8,128)(2,1)S(1)}, bf16[256,256]{1,0:T(8,128)(2,1)S(1)}, u32[]{:S(2)}, u32[]{:S(2)}) collective-permute-start(bf16[256,256]{1,0:T(8,128)(2,1)S(1)} %get-tuple-element.26), channel_id=1, source_target_pairs={{0,5},{1,4},{2,7},{3,6},{4,1},{5,0},{6,3},{7,2},{8,13},{9,12},{10,... | collective-permute-start | bytes 393224 | tf_op jit(solution)/shard_map/ppermute | solution.py:31
  39.6 11.3 %collective-permute-start.14 = (bf16[256,256]{1,0:T(8,128)(2,1)S(1)}, bf16[256,256]{1,0:T(8,128)(2,1)S(1)}, u32[]{:S(2)}, u32[]{:S(2)}) collective-permute-start(bf16[256,256]{1,0:T(8,128)(2,1)S(1)} %get-tuple-element.27), channel_id=1, source_target_pairs={{0,1},{1,0},{2,3},{3,2},{4,5},{5,4},{6,7},{7,6},{8,9},{9,8},{10,11... | collective-permute-start | bytes 393224 | tf_op jit(solution)/shard_map/ppermute | solution.py:31
  42.5 10.9 %collective-permute-start.11 = (bf16[528,128]{1,0:T(8,128)(2,1)S(1)}, bf16[528,128]{1,0:T(8,128)(2,1)S(1)}, u32[]{:S(2)}, u32[]{:S(2)}) collective-permute-start(bf16[528,128]{1,0:T(8,128)(2,1)S(1)} %get-tuple-element.28), channel_id=1, source_target_pairs={{0,24},{8,16},{16,8},{24,0},{1,25},{9,17},{17,9},{25,1},{2,26},{10... | collective-permute-start | bytes 405512 | tf_op jit(solution)/shard_map/ppermute | solution.py:31
  42.6 10.9 %collective-permute-start.10 = (bf16[528,128]{1,0:T(8,128)(2,1)S(1)}, bf16[528,128]{1,0:T(8,128)(2,1)S(1)}, u32[]{:S(2)}, u32[]{:S(2)}) collective-permute-start(bf16[528,128]{1,0:T(8,128)(2,1)S(1)} %get-tuple-element.29), channel_id=1, source_target_pairs={{0,16},{8,24},{16,0},{24,8},{1,17},{9,25},{17,1},{25,9},{2,18},{10... | collective-permute-start | bytes 405512 | tf_op jit(solution)/shard_map/ppermute | solution.py:31
  47.7 11.2 %collective-permute-start.9 = (bf16[528,128]{1,0:T(8,128)(2,1)S(1)}, bf16[528,128]{1,0:T(8,128)(2,1)S(1)}, u32[]{:S(2)}, u32[]{:S(2)}) collective-permute-start(bf16[528,128]{1,0:T(8,128)(2,1)S(1)} %get-tuple-element.30), channel_id=1, source_target_pairs={{0,8},{8,0},{16,24},{24,16},{1,9},{9,1},{17,25},{25,17},{2,10},{10... | collective-permute-start | bytes 405512 | tf_op jit(solution)/shard_map/ppermute | solution.py:31
  51.0 5.0 %collective-permute-start.20 = (bf16[256,256]{1,0:T(8,128)(2,1)S(1)}, bf16[256,256]{1,0:T(8,128)(2,1)S(1)}, u32[]{:S(2)}, u32[]{:S(2)}) collective-permute-start(bf16[256,256]{1,0:T(8,128)(2,1)S(1)} %shard_map.95.refs_0_), channel_id=1, source_target_pairs={{0,16},{1,17},{2,18},{3,19},{4,20},{5,21},{6,22},{7,23},{8,24},{9,... | collective-permute-start | bytes 393224 | tf_op jit(solution)/shard_map/ppermute | solution.py:31
  51.9 7.1 %collective-permute-start.18 = (bf16[256,256]{1,0:T(8,128)(2,1)S(1)}, bf16[256,256]{1,0:T(8,128)(2,1)S(1)}, u32[]{:S(2)}, u32[]{:S(2)}) collective-permute-start(bf16[256,256]{1,0:T(8,128)(2,1)S(1)} %shard_map.95.refs_0_), channel_id=1, source_target_pairs={{0,1},{1,0},{2,3},{3,2},{4,5},{5,4},{6,7},{7,6},{8,9},{9,8},{10,11... | collective-permute-start | bytes 393224 | tf_op jit(solution)/shard_map/ppermute | solution.py:31
  53.4 7.1 %collective-permute-start.17 = (bf16[256,256]{1,0:T(8,128)(2,1)S(1)}, bf16[256,256]{1,0:T(8,128)(2,1)S(1)}, u32[]{:S(2)}, u32[]{:S(2)}) collective-permute-start(bf16[256,256]{1,0:T(8,128)(2,1)S(1)} %shard_map.95.refs_0_), channel_id=1, source_target_pairs={{0,8},{8,0},{16,24},{24,16},{1,9},{9,1},{17,25},{25,17},{2,10},{10... | collective-permute-start | bytes 393224 | tf_op jit(solution)/shard_map/ppermute | solution.py:31
  53.4 6.8 %collective-permute-start.15 = (bf16[256,256]{1,0:T(8,128)(2,1)S(1)}, bf16[256,256]{1,0:T(8,128)(2,1)S(1)}, u32[]{:S(2)}, u32[]{:S(2)}) collective-permute-start(bf16[256,256]{1,0:T(8,128)(2,1)S(1)} %shard_map.95.refs_0_), channel_id=1, source_target_pairs={{0,17},{1,16},{2,19},{3,18},{4,21},{5,20},{6,23},{7,22},{8,25},{9,... | collective-permute-start | bytes 393224 | tf_op jit(solution)/shard_map/ppermute | solution.py:31
  56.0 4.5 %collective-permute-start.21 = (bf16[256,256]{1,0:T(8,128)(2,1)S(1)}, bf16[256,256]{1,0:T(8,128)(2,1)S(1)}, u32[]{:S(2)}, u32[]{:S(2)}) collective-permute-start(bf16[256,256]{1,0:T(8,128)(2,1)S(1)} %collective-permute-done.20.refs_4_), channel_id=1, source_target_pairs={{0,8},{8,0},{16,24},{24,16},{1,9},{9,1},{17,25},{25,17},{2,10},{10... | collective-permute-start | bytes 393224 | tf_op jit(solution)/shard_map/ppermute | solution.py:31
  59.0 1.6 %collective-permute-start.19 = (bf16[256,256]{1,0:T(8,128)(2,1)S(1)}, bf16[256,256]{1,0:T(8,128)(2,1)S(1)}, u32[]{:S(2)}, u32[]{:S(2)}) collective-permute-start(bf16[256,256]{1,0:T(8,128)(2,1)S(1)} %collective-permute-done.18.refs_2_), channel_id=1, source_target_pairs={{0,8},{8,0},{16,24},{24,16},{1,9},{9,1},{17,25},{25,17},{2,10},{10... | collective-permute-start | bytes 393224 | tf_op jit(solution)/shard_map/ppermute | solution.py:31
  60.3 1.5 %collective-permute-start.16 = (bf16[256,256]{1,0:T(8,128)(2,1)S(1)}, bf16[256,256]{1,0:T(8,128)(2,1)S(1)}, u32[]{:S(2)}, u32[]{:S(2)}) collective-permute-start(bf16[256,256]{1,0:T(8,128)(2,1)S(1)} %collective-permute-done.15.refs_0_), channel_id=1, source_target_pairs={{0,8},{8,0},{16,24},{24,16},{1,9},{9,1},{17,25},{25,17},{2,10},{10... | collective-permute-start | bytes 393224 | tf_op jit(solution)/shard_map/ppermute | solution.py:31

commit v4 on v3

--- a/solution.py
+++ b/solution.py
@@ -70,29 +70,27 @@
     return lax.dot_general(a, b, (dims, ((), ())), preferred_element_type=F32)
 
 
-def message_body(key_hbm, value_hbm, doc_hbm, out_ref, doc_ref, sems):
+def message_body(key_hbm, doc_hbm, out_ref, doc_ref, sems):
     tokens, width = key_hbm.shape
     copies = [
-        pltpu.make_async_copy(ref, out_ref.at[pl.ds(i * tokens, tokens)], sems.at[i])
-        for i, ref in enumerate((key_hbm, value_hbm))
+        pltpu.make_async_copy(doc_hbm, doc_ref, sems.at[0]),
+        pltpu.make_async_copy(key_hbm, out_ref.at[pl.ds(0, tokens)], sems.at[1]),
     ]
-    copies.append(pltpu.make_async_copy(doc_hbm, doc_ref, sems.at[2]))
     for copy in copies:
         copy.start()
-    copies.pop().wait()
+    copies[0].wait()
     plus = doc_ref[...] + 1
     high = plus // DOC_BASE
     digits = jnp.concatenate([plus - high * DOC_BASE, high], 1).astype(F32)
     digits = jnp.broadcast_to(digits, (LABEL_ROWS, 2 * tokens)).astype(BF16)
-    out_ref[2 * tokens :, : 2 * tokens] = digits
+    out_ref[tokens:, : 2 * tokens] = digits
     if width > 2 * tokens:
-        out_ref[2 * tokens :, 2 * tokens :] = jnp.zeros((LABEL_ROWS, width - 2 * tokens), BF16)
-    for copy in copies:
-        copy.wait()
+        out_ref[tokens:, 2 * tokens :] = jnp.zeros((LABEL_ROWS, width - 2 * tokens), BF16)
+    copies[1].wait()
 
 
 def docs_of(message_ref, tokens):
-    codes = message_ref[2 * tokens :, : 2 * tokens].astype(F32)[0:1]
+    codes = message_ref[tokens:, : 2 * tokens].astype(F32)[0:1]
     return codes[:, :tokens] + DOC_BASE * codes[:, tokens:] - 1.0
 
 
@@ -130,7 +128,11 @@
         own_ref[:, col] = dot(po, g4, ((1,), (0,)))
 
 
-def attend_body(blocks, pt_ref, message_ref, prior_ref, plan_ref, out_ref):
+def copy_body(in_ref, out_ref):
+    out_ref[...] = in_ref[...]
+
+
+def attend_body(blocks, pt_ref, value_ref, prior_ref, plan_ref, out_ref):
     tokens = pt_ref.shape[1] // 2
     rows = tokens // blocks
     owners = out_ref.shape[0]
@@ -143,8 +145,8 @@
         out_ref[slots[j], data:, :] = jnp.full((LABEL_ROWS, LANES), j + 1, F32).astype(BF16)
     for g in range(KV_HEADS):
         col = slice(g * HEAD_DIM, (g + 1) * HEAD_DIM)
-        att = dot(pt_ref[g, :tokens, :], prior_ref[tokens : 2 * tokens, col], ((0,), (0,)))
-        att = att + dot(pt_ref[g, tokens:, :], message_ref[tokens : 2 * tokens, col], ((0,), (0,)))
+        att = dot(pt_ref[g, :tokens, :], prior_ref[:, col], ((0,), (0,)))
+        att = att + dot(pt_ref[g, tokens:, :], value_ref[:, col], ((0,), (0,)))
         att = att.astype(BF16)
         for r in range(GROUP):
             first = (g * GROUP + r) * rows
@@ -154,7 +156,8 @@
 
 
 def place_body(blocks, *refs):
-    *arrived, out_hbm, wide_ref, sems = refs
+    *arrived, out_hbm, done_ref, wide_ref, sems = refs
+    done_ref[...] = jnp.zeros(done_ref.shape, F32)
     rows = out_hbm.shape[0] // blocks
     heads = out_hbm.shape[1] // LANES
     labels = [jnp.max(a[heads * rows :, :].astype(F32)).astype(jnp.int32) for a in arrived]
@@ -176,12 +179,12 @@
             copy.wait()
 
 
-def split_body(reduced, places, chips, in_hbm, q_hbm, g_hbm, *refs):
+def split_body(reduced, places, chips, in_hbm, q_hbm, g_hbm, v_hbm, *refs):
     spread = len(places)
-    outs, (q_ref, g_ref, in_ref, sems) = refs[:spread], refs[spread:]
+    outs, (q_ref, g_ref, v_ref, in_ref, sems) = refs[:spread], refs[spread:]
     copies = [
         pltpu.make_async_copy(src, dst, sems.at[i])
-        for i, (src, dst) in enumerate(((in_hbm, in_ref), (q_hbm, q_ref), (g_hbm, g_ref)))
+        for i, (src, dst) in enumerate(((in_hbm, in_ref), (q_hbm, q_ref), (g_hbm, g_ref), (v_hbm, v_ref)))
     ]
     for copy in copies:
         copy.start()
@@ -194,8 +197,8 @@
             first = (z ^ kz ^ mz) * chips + (x ^ kx ^ mx) * reps + (y ^ ky ^ my)
             first = pl.multiple_of(first * sub, sub)
             outs[k][m * sub : (m + 1) * sub, :] = in_ref[:, pl.ds(first, sub)].T
-    copies[1].wait()
-    copies[2].wait()
+    for copy in copies[1:]:
+        copy.wait()
 
 
 def both_body(own_ref, ret_ref, out_ref):
@@ -228,18 +231,22 @@
     out_ref[...] = total.astype(BF16)
 
 
-def spread_body(blocks, *refs):
-    pieces = refs[: len(blocks)]
-    out_hbm, wide_ref, sems = refs[-3:]
-    sub, half = pieces[0].shape
+def spread_body(places, resumed, *refs):
+    count = len(places)
+    mine, other = refs[:count], refs[count : 2 * count]
+    *dones, wide_ref, sems = refs[2 * count + resumed :]
+    out_hbm, *dones = dones
+    for done_ref in dones:
+        done_ref[...] = jnp.zeros(done_ref.shape, F32)
+    sub, half = mine[0].shape
     core, x, _, y = chip_at()
     q = x * lax.axis_size("rep") + y
     copies = []
-    for i, (k, other) in enumerate(blocks):
-        wide_ref[i] = pieces[i][...].astype(F32)
+    for i, k in enumerate(places):
+        for ref, at in ((mine[i], core), (other[i], core ^ 1)):
+            wide_ref[i, :, pl.ds(pl.multiple_of(at * half, half), half)] = ref[...].astype(F32)
         rows = pl.ds(pl.multiple_of((q ^ k) * sub, sub), sub)
-        cols = pl.ds(pl.multiple_of((core ^ other) * half, half), half)
-        copies.append(pltpu.make_async_copy(wide_ref.at[i], out_hbm.at[rows, cols], sems.at[i]))
+        copies.append(pltpu.make_async_copy(wide_ref.at[i], out_hbm.at[rows], sems.at[i]))
         copies[i].start()
     for copy in copies:
         copy.wait()
@@ -283,20 +290,20 @@
 
     (message,) = call(
         message_body,
-        [shape(2 * tokens + LABEL_ROWS, kv_width)],
-        [keys[0], values[0], doc_ids],
-        hbm_in=(0, 1, 2),
-        scratch=[pltpu.VMEM(doc_ids.shape, jnp.int32), pltpu.SemaphoreType.DMA((3,))],
+        [shape(tokens + LABEL_ROWS, kv_width)],
+        [keys[0], doc_ids],
+        hbm_in=(0, 1),
+        scratch=[pltpu.VMEM(doc_ids.shape, jnp.int32), pltpu.SemaphoreType.DMA((2,))],
     )
     prior = from_behind(message, shards, 1)
 
     if by_chips:
-        *pieces, q_rows, g_rows = call(
+        *pieces, q_rows, g_rows, value_rows = call(
             functools.partial(split_body, reduced, places, chips),
-            [shape(len(reduced) * sub, tokens)] * len(places) + [shape(tokens, q_width)] * 2,
-            [inputs[0], queries[0], grad_out[0]],
-            hbm_in=(0, 1, 2),
-            scratch=[pltpu.VMEM((tokens, width), BF16), pltpu.SemaphoreType.DMA((3,))],
+            [shape(len(reduced) * sub, tokens)] * len(places) + [shape(tokens, q_width)] * 2 + [shape(tokens, kv_width)],
+            [inputs[0], queries[0], grad_out[0], values[0]],
+            hbm_in=(0, 1, 2, 3),
+            scratch=[pltpu.VMEM((tokens, width), BF16), pltpu.SemaphoreType.DMA((4,))],
         )
 
         def gather(value_of):
@@ -305,7 +312,7 @@
 
         mine_in = gather(lambda k: pieces[k])
     else:
-        q_rows, g_rows = queries[0], grad_out[0]
+        q_rows, g_rows, value_rows = queries[0], grad_out[0], values[0]
 
     probs, back, own = call(
         probs_body,
@@ -318,13 +325,14 @@
         weight=100,
     )
     returned = from_behind(back, shards, -1)
+    prior_values = from_behind(value_rows, shards, 1)
     if by_chips:
         (grad_values,) = call(both_body, [shape(tokens, kv_width)], [own, returned], deps=mine_in[1:3])
         grads = gather(lambda k: grad_values)
         factors = [*mine_in, *grads]
-        (cross,) = call(functools.partial(product_body, 1), [shape(len(reduced) * sub, half)], factors)
+        (cross,) = call(functools.partial(product_body, 1), [shape(len(reduced) * sub, half)], factors, deps=[prior_values])
         (kept,) = call(
-            functools.partial(product_body, 0), [shape(len(reduced) * sub, half, dtype=F32)], factors, weight=3
+            functools.partial(product_body, 0), [shape(len(reduced) * sub, half, dtype=F32)], factors
         )
         partial = call(
             add_body,
@@ -336,15 +344,16 @@
     (outgoing,) = call(
         functools.partial(attend_body, blocks),
         [shape(micro, (q_width // LANES) * rows + LABEL_ROWS, LANES)],
-        [probs, message, prior, plan[0]],
+        [probs, value_rows, prior_values, plan[0]],
         weight=100,
         deps=[partial[0]] if by_chips else [],
     )
     arrived_out = [outgoing[0]] + [swap(outgoing[m], "dp", m) for m in range(1, micro)]
 
-    (placed,) = call(
+    token = shape(8, LANES, dtype=F32)
+    placed, in_place = call(
         functools.partial(place_body, blocks),
-        [shape(tokens, q_width)],
+        [shape(tokens, q_width), token],
         arrived_out,
         hbm_out=(0,),
         scratch=[pltpu.VMEM((micro, rows, q_width), BF16), pltpu.SemaphoreType.DMA((micro,))],
@@ -352,27 +361,32 @@
     )
     if by_chips:
         (total,) = call(sum_body, [shape(sub, half)], [partial[0], *arrived], deps=[outgoing])
-        last = chips - 1
         sums = [away(total, k // reps, 0, k % reps) for k in reversed(range(1, chips))]
         sums = [total, *reversed(sums)]
-        others = [swap(p, "dp", 1) for p in sums]
+        others = {}
 
         def spread(chosen, so_far=(), weight=0):
-            blocks = [(k, other) for k in chosen for other in range(CORES)]
-            pieces = [(others if other else sums)[k] for k, other in blocks]
-            (result,) = call(
-                functools.partial(spread_body, blocks),
-                [shape(chips * sub, kv_width, dtype=F32)],
+            pieces = [sums[k] for k in chosen] + [others[k] for k in chosen]
+            return call(
+                functools.partial(spread_body, chosen, len(so_far)),
+                [shape(chips * sub, kv_width, dtype=F32)] + [token] * (not so_far),
                 [*pieces, *so_far],
                 weight=weight,
                 hbm_in=(len(pieces),),
                 hbm_out=(0,),
-                scratch=[pltpu.VMEM((len(blocks), sub, half), F32), pltpu.SemaphoreType.DMA((len(blocks),))],
+                scratch=[pltpu.VMEM((len(chosen), sub, kv_width), F32), pltpu.SemaphoreType.DMA((len(chosen),))],
                 alias={len(pieces): 0} if so_far else {},
             )
-            return result
-
-        weight_grad = spread([last], [spread(range(last), weight=2)])
+
+        early = [k for k in range(chips) if k % reps == 0]
+        late = [k for k in reversed(range(chips)) if k % reps]
+        for k in early:
+            others[k] = swap(sums[k], "dp", 1)
+        weight_grad, written = spread(early, weight=2)
+        for k in late:
+            (sums[k],) = call(copy_body, [shape(sub, half)], [sums[k]], deps=[written, in_place])
+            others[k] = swap(sums[k], "dp", 1)
+        (weight_grad,) = spread(late, [weight_grad])
     else:
         weight_grad = weight_by_collectives(inputs[0], own, returned)
     return (placed[None], weight_grad)

time: 62.8 us -> 60.9 us (0.970)
  waiting for transfers between devices: 21.9 us -> 20.4 us
    ppermute x20, starting transfers between devices: 24.3 us -> 20.5 us  [swap(): return lax.ppermute(value, axis, [(i, i ^ mask) for i in range(devices)])]
    ppermute x2 -> x3, starting transfers between devices: 6.18 us -> 9.59 us  [from_behind(): return lax.ppermute(value, axis, pairs)]
    ppermute x2 -> x3, waiting for transfers between devices: 1.17 us -> 0.01 us  [from_behind(): return lax.ppermute(value, axis, pairs)]
    pallas_call x12 -> x14, Pallas kernels: 9.36 us -> 9.36 us  [call(): pl.pallas_call(lambda *refs: body(*refs[skip:]), out_shape=[pltpu.HBM(o.s...]
  transfers between devices with their start and end apart: 22 -> 23, of which waited for: 11 -> 13; matrix products, arithmetic and copies ran while one was open for 0% -> 0% of each run, Pallas kernels for 11% -> 11%
where the time goes in v4:
time: 60.9 us; the launch traced here: 60.7 us
  starting transfers between devices  30.1 us (49%)
  waiting for transfers between devices  20.4 us (33%)
  Pallas kernels  9.36 us (15%)
  between operations  0.82 us (1%)
    ppermute x20, starting transfers between devices, swap(): return lax.ppermute(value, axis, [(i, i ^ mask) for i in range(devices)])  20.5 us
    ppermute x20, waiting for transfers between devices, swap(): return lax.ppermute(value, axis, [(i, i ^ mask) for i in range(devices)])  20.4 us
    ppermute x3, starting transfers between devices, from_behind(): return lax.ppermute(value, axis, pairs)  9.59 us
    pallas_call x14, Pallas kernels, call(): pl.pallas_call(lambda *refs: body(*refs[skip:]), out_shape=[pltpu.HBM(o.s...  9.36 us
  transfers between devices with their start and end apart: 23, of which 13 were waited for; matrix products, arithmetic and copies ran while one was open for 0% of the time, Pallas kernels for 11%

profile of v4, /device:TPU:0, one launch (start us, length us, event | category | flops | bytes accessed | tf_op | source)
XLA Modules:
  0.0 60.7 jit_solution(308395068201958554)
XLA Ops:
  1.6 4.9 %collective-permute-start.3 = (bf16[144,512]{1,0:T(8,128)(2,1)S(1)}, bf16[144,512]{1,0:T(8,128)(2,1)S(1)}, u32[]{:S(2)}, u32[]{:S(2)}) collective-permute-start(bf16[144,512]{1,0:T(8,128)(2,1)S(1)} %shard_map.87.refs_2_), channel_id=1, source_target_pairs={{0,1},{1,2},{2,3},{3,4},{4,5},{5,6},{6,7},{8,9},{9,10},{10,11},{11... | collective-permute-start | bytes 442376 | tf_op jit(solution)/shard_map/ppermute | solution.py:26
  6.5 1.6 %shard_map.86 = (bf16[1024,128]{1,0:T(8,128)(2,1)S(1)}, bf16[1024,128]{1,0:T(8,128)(2,1)S(1)}, bf16[1024,128]{1,0:T(8,128)(2,1)S(1)}, bf16[1024,128]{1,0:T(8,128...) custom-call(bf16[128,4096]{1,0:T(8,128)(2,1)} %bitcast.16, ...), custom_call_target="tpu_custom_call" | custom-call | tf_op jit(solution)/shard_map/pallas_call | solution.py:53
  8.1 1.6 %collective-permute-start.1 = (bf16[1024,128]{1,0:T(8,128)(2,1)S(1)}, bf16[1024,128]{1,0:T(8,128)(2,1)S(1)}, u32[]{:S(2)}, u32[]{:S(2)}) collective-permute-start(bf16[1024,128]{1,0:T(8,128)(2,1)S(1)} %get-tuple-element.21), channel_id=1, source_target_pairs={{0,16},{1,17},{2,18},{3,19},{4,20},{5,21},{6,22},{7,23},{8,24},{9,... | collective-permute-start | bytes 786440 | tf_op jit(solution)/shard_map/ppermute | solution.py:31
  9.6 1.6 %collective-permute-start.2 = (bf16[1024,128]{1,0:T(8,128)(2,1)S(1)}, bf16[1024,128]{1,0:T(8,128)(2,1)S(1)}, u32[]{:S(2)}, u32[]{:S(2)}) collective-permute-start(bf16[1024,128]{1,0:T(8,128)(2,1)S(1)} %get-tuple-element.22), channel_id=1, source_target_pairs={{0,2},{1,3},{2,0},{3,1},{4,6},{5,7},{6,4},{7,5},{8,10},{9,11},{10,... | collective-permute-start | bytes 786440 | tf_op jit(solution)/shard_map/ppermute | solution.py:31
  11.2 1.7 %shard_map.88 = (bf16[4,256,512]{2,1,0:T(8,128)(2,1)S(1)}, bf16[128,512]{1,0:T(8,128)(2,1)S(1)}, f32[128,512]{1,0:T(8,128)S(1)}) custom-call(bf16[128,2048]{1,0:T(8,128)(2,1)S(1)} %get-tuple-element.24.refs_0_, bf16[128,2048]{1,0:T(8,128)(2,1)S(1)} %get-tuple-element.25.refs_1_, bf16[144,512]{1,0:T(8,128)(2,1)S(1)} %shard_map.87.refs_2_, ...), custom_call_target="tpu_custom_call" | custom-call | flops 99999997952 | tf_op jit(solution)/shard_map/pallas_call | solution.py:53
  12.9 1.3 %collective-permute-start.4 = (bf16[128,512]{1,0:T(8,128)(2,1)S(1)}, bf16[128,512]{1,0:T(8,128)(2,1)S(1)}, u32[]{:S(2)}, u32[]{:S(2)}) collective-permute-start(bf16[128,512]{1,0:T(8,128)(2,1)S(1)} %get-tuple-element.27), channel_id=1, source_target_pairs={{1,0},{2,1},{3,2},{4,3},{5,4},{6,5},{7,6},{9,8},{10,9},{11,10},{12... | collective-permute-start | bytes 393224 | tf_op jit(solution)/shard_map/ppermute | solution.py:26
  14.2 3.9 %collective-permute-start = (bf16[1024,128]{1,0:T(8,128)(2,1)S(1)}, bf16[1024,128]{1,0:T(8,128)(2,1)S(1)}, u32[]{:S(2)}, u32[]{:S(2)}) collective-permute-start(bf16[1024,128]{1,0:T(8,128)(2,1)S(1)} %get-tuple-element.20), channel_id=1, source_target_pairs={{0,18},{1,19},{2,16},{3,17},{4,22},{5,23},{6,20},{7,21},{8,26},{9,... | collective-permute-start | bytes 786440 | tf_op jit(solution)/shard_map/ppermute | solution.py:31
  18.1 3.4 %collective-permute-start.8 = (bf16[128,512]{1,0:T(8,128)(2,1)S(1)}, bf16[128,512]{1,0:T(8,128)(2,1)S(1)}, u32[]{:S(2)}, u32[]{:S(2)}) collective-permute-start(bf16[128,512]{1,0:T(8,128)(2,1)S(1)} %get-tuple-element.28.refs_2_), channel_id=1, source_target_pairs={{0,1},{1,2},{2,3},{3,4},{4,5},{5,6},{6,7},{8,9},{9,10},{10,11},{11... | collective-permute-start | bytes 393224 | tf_op jit(solution)/shard_map/ppermute | solution.py:26
  21.8 1.3 %collective-permute-start.6 = (bf16[128,512]{1,0:T(8,128)(2,1)S(1)}, bf16[128,512]{1,0:T(8,128)(2,1)S(1)}, u32[]{:S(2)}, u32[]{:S(2)}) collective-permute-start(bf16[128,512]{1,0:T(8,128)(2,1)S(1)} %shard_map.89.refs_7_.refs_8_), channel_id=1, source_target_pairs={{0,16},{1,17},{2,18},{3,19},{4,20},{5,21},{6,22},{7,23},{8,24},{9,... | collective-permute-start | bytes 393224 | tf_op jit(solution)/shard_map/ppermute | solution.py:31
  23.1 2.0 %collective-permute-start.5 = (bf16[128,512]{1,0:T(8,128)(2,1)S(1)}, bf16[128,512]{1,0:T(8,128)(2,1)S(1)}, u32[]{:S(2)}, u32[]{:S(2)}) collective-permute-start(bf16[128,512]{1,0:T(8,128)(2,1)S(1)} %shard_map.89.refs_7_.refs_8_), channel_id=1, source_target_pairs={{0,18},{1,19},{2,16},{3,17},{4,22},{5,23},{6,20},{7,21},{8,26},{9,... | collective-permute-start | bytes 393224 | tf_op jit(solution)/shard_map/ppermute | solution.py:31
  25.1 2.9 %collective-permute-done.refs_0_.refs_1_ = bf16[1024,128]{1,0:T(8,128)(2,1)S(1)} collective-permute-done((bf16[1024,128]{1,0:T(8,128)(2,1)S(1)}, bf16[1024,128]{1,0:T(8,128)(2,1)S(1)}, u32[]{:S(2)}, u32[]{:S(2)}) %collective-permute-start) | collective-permute-done | bytes 262176 | tf_op jit(solution)/shard_map/ppermute | solution.py:31
  28.1 1.9 %collective-permute-done.7.refs_6_.refs_7_ = bf16[128,512]{1,0:T(8,128)(2,1)S(1)} collective-permute-done((bf16[128,512]{1,0:T(8,128)(2,1)S(1)}, bf16[128,512]{1,0:T(8,128)(2,1)S(1)}, u32[]{:S(2)}, u32[]{:S(2)}) %collective-permute-start.7) | collective-permute-done | bytes 131104 | tf_op jit(solution)/shard_map/ppermute | solution.py:31
  30.2 1.4 %collective-permute-done.5.refs_4_.refs_5_ = bf16[128,512]{1,0:T(8,128)(2,1)S(1)} collective-permute-done((bf16[128,512]{1,0:T(8,128)(2,1)S(1)}, bf16[128,512]{1,0:T(8,128)(2,1)S(1)}, u32[]{:S(2)}, u32[]{:S(2)}) %collective-permute-start.5) | collective-permute-done | bytes 131104 | tf_op jit(solution)/shard_map/ppermute | solution.py:31
  32.6 1.4 %collective-permute-done.9.refs_1_ = bf16[1024,256]{1,0:T(8,128)(2,1)S(1)} collective-permute-done((bf16[1024,256]{1,0:T(8,128)(2,1)S(1)}, bf16[1024,256]{1,0:T(8,128)(2,1)S(1)}, u32[]{:S(2)}, u32[]{:S(2)}) %collective-permute-start.9) | collective-permute-done | bytes 524320 | tf_op jit(solution)/shard_map/ppermute | solution.py:31
  34.1 2.7 %collective-permute-start.13 = (bf16[256,256]{1,0:T(8,128)(2,1)S(1)}, bf16[256,256]{1,0:T(8,128)(2,1)S(1)}, u32[]{:S(2)}, u32[]{:S(2)}) collective-permute-start(bf16[256,256]{1,0:T(8,128)(2,1)S(1)} %get-tuple-element.32), channel_id=1, source_target_pairs={{0,4},{1,5},{2,6},{3,7},{4,0},{5,1},{6,2},{7,3},{8,12},{9,13},{10,... | collective-permute-start | bytes 393224 | tf_op jit(solution)/shard_map/ppermute | solution.py:31
  37.4 1.2 %collective-permute-start.15 = (bf16[256,256]{1,0:T(8,128)(2,1)S(1)}, bf16[256,256]{1,0:T(8,128)(2,1)S(1)}, u32[]{:S(2)}, u32[]{:S(2)}) collective-permute-start(bf16[256,256]{1,0:T(8,128)(2,1)S(1)} %get-tuple-element.34), channel_id=1, source_target_pairs={{0,1},{1,0},{2,3},{3,2},{4,5},{5,4},{6,7},{7,6},{8,9},{9,8},{10,11... | collective-permute-start | bytes 393224 | tf_op jit(solution)/shard_map/ppermute | solution.py:31
  38.6 1.0 %shard_map.93.refs_0_ = bf16[4,528,128]{2,1,0:T(8,128)(2,1)S(1)} custom-call(f32[256,256]{1,0:T(8,128)S(1)} %get-tuple-element.29.refs_0_.refs_1_, bf16[4,256,512]{2,1,0:T(8,128)(2,1)S(1)} %get-tuple-element.30.refs_1_, bf16[128,512]{1,0:T(8,128)(2,1)S(1)} %get-tuple-element.28.refs_2_, bf16[128,512]{1,0:T(8,128)(2,1)S(1)} %collective-permute-done.8.refs_0_.refs_3_, ...), custom_call_target="tpu_custom_call" | custom-call | flops 99999997952 | tf_op jit(solution)/shard_map/pallas_call | solution.py:53
  39.9 1.2 %collective-permute-start.11 = (bf16[528,128]{1,0:T(8,128)(2,1)S(1)}, bf16[528,128]{1,0:T(8,128)(2,1)S(1)}, u32[]{:S(2)}, u32[]{:S(2)}) collective-permute-start(bf16[528,128]{1,0:T(8,128)(2,1)S(1)} %get-tuple-element.39), channel_id=1, source_target_pairs={{0,16},{8,24},{16,0},{24,8},{1,17},{9,25},{17,1},{25,9},{2,18},{10... | collective-permute-start | bytes 405512 | tf_op jit(solution)/shard_map/ppermute | solution.py:31
  41.1 4.8 %collective-permute-done.13.refs_2_ = bf16[256,256]{1,0:T(8,128)(2,1)S(1)} collective-permute-done((bf16[256,256]{1,0:T(8,128)(2,1)S(1)}, bf16[256,256]{1,0:T(8,128)(2,1)S(1)}, u32[]{:S(2)}, u32[]{:S(2)}) %collective-permute-start.13) | collective-permute-done | bytes 131104 | tf_op jit(solution)/shard_map/ppermute | solution.py:31
  45.8 3.5 %collective-permute-done.14.refs_3_ = bf16[256,256]{1,0:T(8,128)(2,1)S(1)} collective-permute-done((bf16[256,256]{1,0:T(8,128)(2,1)S(1)}, bf16[256,256]{1,0:T(8,128)(2,1)S(1)}, u32[]{:S(2)}, u32[]{:S(2)}) %collective-permute-start.14) | collective-permute-done | bytes 131104 | tf_op jit(solution)/shard_map/ppermute | solution.py:31
  51.2 1.8 %collective-permute-start.19 = (bf16[256,256]{1,0:T(8,128)(2,1)S(1)}, bf16[256,256]{1,0:T(8,128)(2,1)S(1)}, u32[]{:S(2)}, u32[]{:S(2)}) collective-permute-start(bf16[256,256]{1,0:T(8,128)(2,1)S(1)} %shard_map.95.refs_0_), channel_id=1, source_target_pairs={{0,17},{1,16},{2,19},{3,18},{4,21},{5,20},{6,23},{7,22},{8,25},{9,... | collective-permute-start | bytes 393224 | tf_op jit(solution)/shard_map/ppermute | solution.py:31
  53.0 2.1 %collective-permute-done.16.refs_1_ = bf16[256,256]{1,0:T(8,128)(2,1)S(1)} collective-permute-done((bf16[256,256]{1,0:T(8,128)(2,1)S(1)}, bf16[256,256]{1,0:T(8,128)(2,1)S(1)}, u32[]{:S(2)}, u32[]{:S(2)}) %collective-permute-start.16) | collective-permute-done | bytes 131104 | tf_op jit(solution)/shard_map/ppermute | solution.py:31
  56.4 1.0 %shard_map.96 = (f32[1024,512]{1,0:T(8,128)}, f32[8,128]{1,0:T(8,128)S(1)}) custom-call(bf16[256,256]{1,0:T(8,128)(2,1)S(1)} %shard_map.95.refs_0_, bf16[256,256]{1,0:T(8,128)(2,1)S(1)} %collective-permute-done.16.refs_1_, bf16[256,256]{1,0:T(8,128)(2,1)S(1)} %collective-permute-done.17.refs_2_, bf16[256,256]{1,0:T(8,128)(2,1)S(1)} %collective-permute-done.18.refs_3_), custom_call_target="tpu_custom_call" | custom-call | flops 2000000000 | tf_op jit(solution)/shard_map/pallas_call | solution.py:53
  59.7 1.0 %shard_map.99 = f32[1024,512]{1,0:T(8,128)} custom-call(bf16[256,256]{1,0:T(8,128)(2,1)S(1)} %shard_map.97.refs_0_, bf16[256,256]{1,0:T(8,128)(2,1)S(1)} %shard_map.98.refs_1_, bf16[256,256]{1,0:T(8,128)(2,1)S(1)} %collective-permute-done.21.refs_2_, bf16[256,256]{1,0:T(8,128)(2,1)S(1)} %collective-permute-done.22.refs_3_, ...), custom_call_target="tpu_custom_call", output_to_operand_aliasing={{}: (4, {})} | custom-call | tf_op jit(solution)/shard_map/pallas_call | solution.py:53
  (39 shorter events, 8.7 us)
Async XLA Ops:
  1.6 9.6 %collective-permute-start.3 = (bf16[144,512]{1,0:T(8,128)(2,1)S(1)}, bf16[144,512]{1,0:T(8,128)(2,1)S(1)}, u32[]{:S(2)}, u32[]{:S(2)}) collective-permute-start(bf16[144,512]{1,0:T(8,128)(2,1)S(1)} %shard_map.87.refs_2_), channel_id=1, source_target_pairs={{0,1},{1,2},{2,3},{3,4},{4,5},{5,6},{6,7},{8,9},{9,10},{10,11},{11... | collective-permute-start | bytes 442376 | tf_op jit(solution)/shard_map/ppermute | solution.py:26
  8.1 13.5 %collective-permute-start.1 = (bf16[1024,128]{1,0:T(8,128)(2,1)S(1)}, bf16[1024,128]{1,0:T(8,128)(2,1)S(1)}, u32[]{:S(2)}, u32[]{:S(2)}) collective-permute-start(bf16[1024,128]{1,0:T(8,128)(2,1)S(1)} %get-tuple-element.21), channel_id=1, source_target_pairs={{0,16},{1,17},{2,18},{3,19},{4,20},{5,21},{6,22},{7,23},{8,24},{9,... | collective-permute-start | bytes 786440 | tf_op jit(solution)/shard_map/ppermute | solution.py:31
  9.6 11.9 %collective-permute-start.2 = (bf16[1024,128]{1,0:T(8,128)(2,1)S(1)}, bf16[1024,128]{1,0:T(8,128)(2,1)S(1)}, u32[]{:S(2)}, u32[]{:S(2)}) collective-permute-start(bf16[1024,128]{1,0:T(8,128)(2,1)S(1)} %get-tuple-element.22), channel_id=1, source_target_pairs={{0,2},{1,3},{2,0},{3,1},{4,6},{5,7},{6,4},{7,5},{8,10},{9,11},{10,... | collective-permute-start | bytes 786440 | tf_op jit(solution)/shard_map/ppermute | solution.py:31
  12.9 8.6 %collective-permute-start.4 = (bf16[128,512]{1,0:T(8,128)(2,1)S(1)}, bf16[128,512]{1,0:T(8,128)(2,1)S(1)}, u32[]{:S(2)}, u32[]{:S(2)}) collective-permute-start(bf16[128,512]{1,0:T(8,128)(2,1)S(1)} %get-tuple-element.27), channel_id=1, source_target_pairs={{1,0},{2,1},{3,2},{4,3},{5,4},{6,5},{7,6},{9,8},{10,9},{11,10},{12... | collective-permute-start | bytes 393224 | tf_op jit(solution)/shard_map/ppermute | solution.py:26
  14.2 13.9 %collective-permute-start = (bf16[1024,128]{1,0:T(8,128)(2,1)S(1)}, bf16[1024,128]{1,0:T(8,128)(2,1)S(1)}, u32[]{:S(2)}, u32[]{:S(2)}) collective-permute-start(bf16[1024,128]{1,0:T(8,128)(2,1)S(1)} %get-tuple-element.20), channel_id=1, source_target_pairs={{0,18},{1,19},{2,16},{3,17},{4,22},{5,23},{6,20},{7,21},{8,26},{9,... | collective-permute-start | bytes 786440 | tf_op jit(solution)/shard_map/ppermute | solution.py:31
  18.1 7.1 %collective-permute-start.8 = (bf16[128,512]{1,0:T(8,128)(2,1)S(1)}, bf16[128,512]{1,0:T(8,128)(2,1)S(1)}, u32[]{:S(2)}, u32[]{:S(2)}) collective-permute-start(bf16[128,512]{1,0:T(8,128)(2,1)S(1)} %get-tuple-element.28.refs_2_), channel_id=1, source_target_pairs={{0,1},{1,2},{2,3},{3,4},{4,5},{5,6},{6,7},{8,9},{9,10},{10,11},{11... | collective-permute-start | bytes 393224 | tf_op jit(solution)/shard_map/ppermute | solution.py:26
  21.6 8.4 %collective-permute-start.7 = (bf16[128,512]{1,0:T(8,128)(2,1)S(1)}, bf16[128,512]{1,0:T(8,128)(2,1)S(1)}, u32[]{:S(2)}, u32[]{:S(2)}) collective-permute-start(bf16[128,512]{1,0:T(8,128)(2,1)S(1)} %shard_map.89.refs_7_.refs_8_), channel_id=1, source_target_pairs={{0,2},{1,3},{2,0},{3,1},{4,6},{5,7},{6,4},{7,5},{8,10},{9,11},{10,... | collective-permute-start | bytes 393224 | tf_op jit(solution)/shard_map/ppermute | solution.py:31
  21.8 8.4 %collective-permute-start.6 = (bf16[128,512]{1,0:T(8,128)(2,1)S(1)}, bf16[128,512]{1,0:T(8,128)(2,1)S(1)}, u32[]{:S(2)}, u32[]{:S(2)}) collective-permute-start(bf16[128,512]{1,0:T(8,128)(2,1)S(1)} %shard_map.89.refs_7_.refs_8_), channel_id=1, source_target_pairs={{0,16},{1,17},{2,18},{3,19},{4,20},{5,21},{6,22},{7,23},{8,24},{9,... | collective-permute-start | bytes 393224 | tf_op jit(solution)/shard_map/ppermute | solution.py:31
  23.1 8.5 %collective-permute-start.5 = (bf16[128,512]{1,0:T(8,128)(2,1)S(1)}, bf16[128,512]{1,0:T(8,128)(2,1)S(1)}, u32[]{:S(2)}, u32[]{:S(2)}) collective-permute-start(bf16[128,512]{1,0:T(8,128)(2,1)S(1)} %shard_map.89.refs_7_.refs_8_), channel_id=1, source_target_pairs={{0,18},{1,19},{2,16},{3,17},{4,22},{5,23},{6,20},{7,21},{8,26},{9,... | collective-permute-start | bytes 393224 | tf_op jit(solution)/shard_map/ppermute | solution.py:31
  32.0 6.5 %copy-start = (s32[1,4]{1,0:T(1,128)S(1)}, s32[1,4]{1,0:T(1,128)}, u32[]{:S(2)}) copy-start(s32[1,4]{1,0:T(1,128)} %param.13) | copy-start | bytes 52
  32.0 2.0 %collective-permute-start.9 = (bf16[1024,256]{1,0:T(8,128)(2,1)S(1)}, bf16[1024,256]{1,0:T(8,128)(2,1)S(1)}, u32[]{:S(2)}, u32[]{:S(2)}) collective-permute-start(bf16[1024,256]{1,0:T(8,128)(2,1)S(1)} %shard_map.91), channel_id=1, source_target_pairs={{0,8},{8,0},{16,24},{24,16},{1,9},{9,1},{17,25},{25,17},{2,10},{10... | collective-permute-start | bytes 1572872 | tf_op jit(solution)/shard_map/ppermute | solution.py:31
  34.1 11.7 %collective-permute-start.13 = (bf16[256,256]{1,0:T(8,128)(2,1)S(1)}, bf16[256,256]{1,0:T(8,128)(2,1)S(1)}, u32[]{:S(2)}, u32[]{:S(2)}) collective-permute-start(bf16[256,256]{1,0:T(8,128)(2,1)S(1)} %get-tuple-element.32), channel_id=1, source_target_pairs={{0,4},{1,5},{2,6},{3,7},{4,0},{5,1},{6,2},{7,3},{8,12},{9,13},{10,... | collective-permute-start | bytes 393224 | tf_op jit(solution)/shard_map/ppermute | solution.py:31
  36.8 12.6 %collective-permute-start.14 = (bf16[256,256]{1,0:T(8,128)(2,1)S(1)}, bf16[256,256]{1,0:T(8,128)(2,1)S(1)}, u32[]{:S(2)}, u32[]{:S(2)}) collective-permute-start(bf16[256,256]{1,0:T(8,128)(2,1)S(1)} %get-tuple-element.33), channel_id=1, source_target_pairs={{0,5},{1,4},{2,7},{3,6},{4,1},{5,0},{6,3},{7,2},{8,13},{9,12},{10,... | collective-permute-start | bytes 393224 | tf_op jit(solution)/shard_map/ppermute | solution.py:31
  37.4 11.9 %collective-permute-start.15 = (bf16[256,256]{1,0:T(8,128)(2,1)S(1)}, bf16[256,256]{1,0:T(8,128)(2,1)S(1)}, u32[]{:S(2)}, u32[]{:S(2)}) collective-permute-start(bf16[256,256]{1,0:T(8,128)(2,1)S(1)} %get-tuple-element.34), channel_id=1, source_target_pairs={{0,1},{1,0},{2,3},{3,2},{4,5},{5,4},{6,7},{7,6},{8,9},{9,8},{10,11... | collective-permute-start | bytes 393224 | tf_op jit(solution)/shard_map/ppermute | solution.py:31
  39.6 11.5 %collective-permute-start.12 = (bf16[528,128]{1,0:T(8,128)(2,1)S(1)}, bf16[528,128]{1,0:T(8,128)(2,1)S(1)}, u32[]{:S(2)}, u32[]{:S(2)}) collective-permute-start(bf16[528,128]{1,0:T(8,128)(2,1)S(1)} %get-tuple-element.38), channel_id=1, source_target_pairs={{0,24},{8,16},{16,8},{24,0},{1,25},{9,17},{17,9},{25,1},{2,26},{10... | collective-permute-start | bytes 405512 | tf_op jit(solution)/shard_map/ppermute | solution.py:31
  39.9 13.1 %collective-permute-start.11 = (bf16[528,128]{1,0:T(8,128)(2,1)S(1)}, bf16[528,128]{1,0:T(8,128)(2,1)S(1)}, u32[]{:S(2)}, u32[]{:S(2)}) collective-permute-start(bf16[528,128]{1,0:T(8,128)(2,1)S(1)} %get-tuple-element.39), channel_id=1, source_target_pairs={{0,16},{8,24},{16,0},{24,8},{1,17},{9,25},{17,1},{25,9},{2,18},{10... | collective-permute-start | bytes 405512 | tf_op jit(solution)/shard_map/ppermute | solution.py:31
  45.8 9.3 %collective-permute-start.10 = (bf16[528,128]{1,0:T(8,128)(2,1)S(1)}, bf16[528,128]{1,0:T(8,128)(2,1)S(1)}, u32[]{:S(2)}, u32[]{:S(2)}) collective-permute-start(bf16[528,128]{1,0:T(8,128)(2,1)S(1)} %get-tuple-element.40), channel_id=1, source_target_pairs={{0,8},{8,0},{16,24},{24,16},{1,9},{9,1},{17,25},{25,17},{2,10},{10... | collective-permute-start | bytes 405512 | tf_op jit(solution)/shard_map/ppermute | solution.py:31
  49.4 5.7 %collective-permute-start.16 = (bf16[256,256]{1,0:T(8,128)(2,1)S(1)}, bf16[256,256]{1,0:T(8,128)(2,1)S(1)}, u32[]{:S(2)}, u32[]{:S(2)}) collective-permute-start(bf16[256,256]{1,0:T(8,128)(2,1)S(1)} %shard_map.95.refs_0_), channel_id=1, source_target_pairs={{0,16},{1,17},{2,18},{3,19},{4,20},{5,21},{6,22},{7,23},{8,24},{9,... | collective-permute-start | bytes 393224 | tf_op jit(solution)/shard_map/ppermute | solution.py:31
  50.3 7.9 %collective-permute-start.20 = (bf16[256,256]{1,0:T(8,128)(2,1)S(1)}, bf16[256,256]{1,0:T(8,128)(2,1)S(1)}, u32[]{:S(2)}, u32[]{:S(2)}) collective-permute-start(bf16[256,256]{1,0:T(8,128)(2,1)S(1)} %shard_map.95.refs_0_), channel_id=1, source_target_pairs={{0,1},{1,0},{2,3},{3,2},{4,5},{5,4},{6,7},{7,6},{8,9},{9,8},{10,11... | collective-permute-start | bytes 393224 | tf_op jit(solution)/shard_map/ppermute | solution.py:31
  51.2 6.8 %collective-permute-start.19 = (bf16[256,256]{1,0:T(8,128)(2,1)S(1)}, bf16[256,256]{1,0:T(8,128)(2,1)S(1)}, u32[]{:S(2)}, u32[]{:S(2)}) collective-permute-start(bf16[256,256]{1,0:T(8,128)(2,1)S(1)} %shard_map.95.refs_0_), channel_id=1, source_target_pairs={{0,17},{1,16},{2,19},{3,18},{4,21},{5,20},{6,23},{7,22},{8,25},{9,... | collective-permute-start | bytes 393224 | tf_op jit(solution)/shard_map/ppermute | solution.py:31
  53.0 3.1 %collective-permute-start.17 = (bf16[256,256]{1,0:T(8,128)(2,1)S(1)}, bf16[256,256]{1,0:T(8,128)(2,1)S(1)}, u32[]{:S(2)}, u32[]{:S(2)}) collective-permute-start(bf16[256,256]{1,0:T(8,128)(2,1)S(1)} %shard_map.95.refs_0_), channel_id=1, source_target_pairs={{0,8},{8,0},{16,24},{24,16},{1,9},{9,1},{17,25},{25,17},{2,10},{10... | collective-permute-start | bytes 393224 | tf_op jit(solution)/shard_map/ppermute | solution.py:31
  55.1 1.3 %collective-permute-start.18 = (bf16[256,256]{1,0:T(8,128)(2,1)S(1)}, bf16[256,256]{1,0:T(8,128)(2,1)S(1)}, u32[]{:S(2)}, u32[]{:S(2)}) collective-permute-start(bf16[256,256]{1,0:T(8,128)(2,1)S(1)} %collective-permute-done.16.refs_1_), channel_id=1, source_target_pairs={{0,8},{8,0},{16,24},{24,16},{1,9},{9,1},{17,25},{25,17},{2,10},{10... | collective-permute-start | bytes 393224 | tf_op jit(solution)/shard_map/ppermute | solution.py:31
  57.9 1.4 %collective-permute-start.21 = (bf16[256,256]{1,0:T(8,128)(2,1)S(1)}, bf16[256,256]{1,0:T(8,128)(2,1)S(1)}, u32[]{:S(2)}, u32[]{:S(2)}) collective-permute-start(bf16[256,256]{1,0:T(8,128)(2,1)S(1)} %shard_map.97.refs_0_), channel_id=1, source_target_pairs={{0,8},{8,0},{16,24},{24,16},{1,9},{9,1},{17,25},{25,17},{2,10},{10... | collective-permute-start | bytes 393224 | tf_op jit(solution)/shard_map/ppermute | solution.py:31
  58.3 1.4 %collective-permute-start.22 = (bf16[256,256]{1,0:T(8,128)(2,1)S(1)}, bf16[256,256]{1,0:T(8,128)(2,1)S(1)}, u32[]{:S(2)}, u32[]{:S(2)}) collective-permute-start(bf16[256,256]{1,0:T(8,128)(2,1)S(1)} %shard_map.98.refs_1_), channel_id=1, source_target_pairs={{0,8},{8,0},{16,24},{24,16},{1,9},{9,1},{17,25},{25,17},{2,10},{10... | collective-permute-start | bytes 393224 | tf_op jit(solution)/shard_map/ppermute | solution.py:31

commit v5 on v4

--- a/solution.py
+++ b/solution.py
@@ -21,6 +21,11 @@
 
 
 def from_behind(value, axis, by):
+    devices = lax.axis_size(axis)
+    return lax.ppermute(value, axis, [(i, (i + by) % devices) for i in range(devices)])
+
+
+def open_ended(value, axis, by):
     devices = lax.axis_size(axis)
     pairs = [(i, i + by) for i in range(devices) if 0 <= i + by < devices]
     return lax.ppermute(value, axis, pairs)
@@ -104,7 +109,9 @@
     t = lax.broadcasted_iota(jnp.int32, (tokens, tokens), 1)
     eye = u == t
     own_docs = docs_of(k_ref, tokens)
-    prior_ok = column_of(docs_of(prior_ref, tokens), eye) == own_docs
+    first = (lax.axis_index("ctx") == 0) & (lax.axis_index("rep") == 0)
+    prior_docs = jnp.where(first, -1.0, docs_of(prior_ref, tokens))
+    prior_ok = column_of(prior_docs, eye) == own_docs
     own_ok = (column_of(own_docs, eye) == own_docs) & (u <= t)
     prior_ok = jnp.concatenate([prior_ok] * GROUP, 1)
     own_ok = jnp.concatenate([own_ok] * GROUP, 1)
@@ -205,13 +212,13 @@
     out_ref[...] = (own_ref[...] + ret_ref[...].astype(F32)).astype(BF16)
 
 
-def product_body(cross, *refs):
+def product_body(cross, rows, *refs):
     *ins, out_ref = refs
     count = len(ins) // 2
     half = out_ref.shape[1]
     core = chip_at()[0] ^ cross
     cols = pl.ds(pl.multiple_of(core * half, half), half)
-    a = jnp.concatenate([ref[...] for ref in ins[:count]], 1)
+    a = jnp.concatenate([ref[rows, :] for ref in ins[:count]], 1)
     b = jnp.concatenate([ref[:, cols] for ref in ins[count:]], 0)
     out_ref[...] = dot(a, b, ((1,), (0,))).astype(out_ref.dtype)
 
@@ -325,20 +332,28 @@
         weight=100,
     )
     returned = from_behind(back, shards, -1)
-    prior_values = from_behind(value_rows, shards, 1)
+    prior_values = open_ended(value_rows, shards, 1)
     if by_chips:
         (grad_values,) = call(both_body, [shape(tokens, kv_width)], [own, returned], deps=mine_in[1:3])
         grads = gather(lambda k: grad_values)
         factors = [*mine_in, *grads]
-        (cross,) = call(functools.partial(product_body, 1), [shape(len(reduced) * sub, half)], factors, deps=[prior_values])
-        (kept,) = call(
-            functools.partial(product_body, 0), [shape(len(reduced) * sub, half, dtype=F32)], factors
-        )
-        partial = call(
-            add_body,
-            [shape(sub, half, dtype=F32)] + [shape(sub, half)] * (len(reduced) - 1),
-            [kept, swap(cross, "dp", 1)],
-        )
+
+        def products(first, last, deps):
+            rows = slice(first * sub, last * sub)
+            many = (last - first) * sub
+            (cross,) = call(functools.partial(product_body, 1, rows), [shape(many, half)], factors, deps=deps)
+            (kept,) = call(
+                functools.partial(product_body, 0, rows), [shape(many, half, dtype=F32)], factors, deps=deps, weight=3
+            )
+            return call(
+                add_body,
+                [shape(sub, half, dtype=BF16 if m else F32) for m in range(first, last)],
+                [kept, swap(cross, "dp", 1)],
+            )
+
+        far = products(2, len(reduced), [prior_values])
+        near = products(0, 2, [far[0]])
+        partial = [*near, *far]
         arrived = [away(partial[m], *reduced[m]) for m in (*range(2, len(reduced)), 1)]
 
     (outgoing,) = call(

time: 60.9 us -> 58.2 us (0.956)
  starting transfers between devices: 30.1 us -> 24.5 us
  waiting for transfers between devices: 20.4 us -> 23 us
    ppermute x20 -> x21, starting transfers between devices: 20.5 us -> 17 us  [swap(): return lax.ppermute(value, axis, [(i, i ^ mask) for i in range(devices)])]
    ppermute x3, waiting for transfers between devices: 0.01 us -> 3.41 us  [the longest x2 3.41 us: from_behind(): lax.ppermute(value, axis, [(i, (i + by) % devices) for i in range(devices)])]
    ppermute x3, starting transfers between devices: 9.59 us -> 7.48 us  [the longest x2 4.72 us: from_behind(): lax.ppermute(value, axis, [(i, (i + by) % devices) for i in range(devices)])]
    ppermute x20 -> x21, waiting for transfers between devices: 20.4 us -> 19.6 us  [swap(): return lax.ppermute(value, axis, [(i, i ^ mask) for i in range(devices)])]
    pallas_call x14 -> x17, Pallas kernels: 9.36 us -> 9.7 us  [call(): pl.pallas_call(lambda *refs: body(*refs[skip:]), out_shape=[pltpu.HBM(o.s...]
  transfers between devices with their start and end apart: 23 -> 24, of which waited for: 13 -> 15; matrix products, arithmetic and copies ran while one was open for 0% -> 0% of each run, Pallas kernels for 11% -> 13%
where the time goes in v5:
time: 58.2 us; the launch traced here: 58 us
  starting transfers between devices  24.5 us (42%)
  waiting for transfers between devices  23 us (40%)
  Pallas kernels  9.7 us (17%)
  between operations  0.82 us (1%)
    ppermute x21, waiting for transfers between devices, swap(): return lax.ppermute(value, axis, [(i, i ^ mask) for i in range(devices)])  19.6 us
    ppermute x21, starting transfers between devices, swap(): return lax.ppermute(value, axis, [(i, i ^ mask) for i in range(devices)])  17 us
    pallas_call x17, Pallas kernels, call(): pl.pallas_call(lambda *refs: body(*refs[skip:]), out_shape=[pltpu.HBM(o.s...  9.7 us
    ppermute x2, starting transfers between devices, from_behind(): lax.ppermute(value, axis, [(i, (i + by) % devices) for i in range(devices)])  4.72 us
    ppermute x2, waiting for transfers between devices, from_behind(): lax.ppermute(value, axis, [(i, (i + by) % devices) for i in range(devices)])  3.41 us
    ppermute x1, starting transfers between devices, open_ended(): return lax.ppermute(value, axis, pairs)  2.76 us
  transfers between devices with their start and end apart: 24, of which 15 were waited for; matrix products, arithmetic and copies ran while one was open for 0% of the time, Pallas kernels for 13%

profile of v5, /device:TPU:0, one launch (start us, length us, event | category | flops | bytes accessed | tf_op | source)
XLA Modules:
  0.0 58.0 jit_solution(6094667232164915499)
XLA Ops:
  1.6 3.0 %collective-permute-start.4 = (bf16[144,512]{1,0:T(8,128)(2,1)S(1)}, bf16[144,512]{1,0:T(8,128)(2,1)S(1)}, u32[]{:S(2)}, u32[]{:S(2)}) collective-permute-start(bf16[144,512]{1,0:T(8,128)(2,1)S(1)} %shard_map.87.refs_2_), channel_id=1, source_target_pairs={{0,1},{1,2},{2,3},{3,4},{4,5},{5,6},{6,7},{7,0},{8,9},{9,10},{10,1... | collective-permute-start | bytes 442376 | tf_op jit(solution)/shard_map/ppermute | solution.py:25
  4.6 1.6 %shard_map.86 = (bf16[1024,128]{1,0:T(8,128)(2,1)S(1)}, bf16[1024,128]{1,0:T(8,128)(2,1)S(1)}, bf16[1024,128]{1,0:T(8,128)(2,1)S(1)}, bf16[1024,128]{1,0:T(8,128...) custom-call(bf16[128,4096]{1,0:T(8,128)(2,1)} %bitcast.16, ...), custom_call_target="tpu_custom_call" | custom-call | tf_op jit(solution)/shard_map/pallas_call | solution.py:58
  6.2 1.6 %collective-permute-start.2 = (bf16[1024,128]{1,0:T(8,128)(2,1)S(1)}, bf16[1024,128]{1,0:T(8,128)(2,1)S(1)}, u32[]{:S(2)}, u32[]{:S(2)}) collective-permute-start(bf16[1024,128]{1,0:T(8,128)(2,1)S(1)} %get-tuple-element.22), channel_id=1, source_target_pairs={{0,16},{1,17},{2,18},{3,19},{4,20},{5,21},{6,22},{7,23},{8,24},{9,... | collective-permute-start | bytes 786440 | tf_op jit(solution)/shard_map/ppermute | solution.py:36
  7.8 1.6 %collective-permute-start.3 = (bf16[1024,128]{1,0:T(8,128)(2,1)S(1)}, bf16[1024,128]{1,0:T(8,128)(2,1)S(1)}, u32[]{:S(2)}, u32[]{:S(2)}) collective-permute-start(bf16[1024,128]{1,0:T(8,128)(2,1)S(1)} %get-tuple-element.23), channel_id=1, source_target_pairs={{0,2},{1,3},{2,0},{3,1},{4,6},{5,7},{6,4},{7,5},{8,10},{9,11},{10,... | collective-permute-start | bytes 786440 | tf_op jit(solution)/shard_map/ppermute | solution.py:36
  9.3 2.3 %collective-permute-done.4.refs_3_ = bf16[144,512]{1,0:T(8,128)(2,1)S(1)} collective-permute-done((bf16[144,512]{1,0:T(8,128)(2,1)S(1)}, bf16[144,512]{1,0:T(8,128)(2,1)S(1)}, u32[]{:S(2)}, u32[]{:S(2)}) %collective-permute-start.4) | collective-permute-done | bytes 147488 | tf_op jit(solution)/shard_map/ppermute | solution.py:25
  11.6 1.7 %shard_map.88 = (bf16[4,256,512]{2,1,0:T(8,128)(2,1)S(1)}, bf16[128,512]{1,0:T(8,128)(2,1)S(1)}, f32[128,512]{1,0:T(8,128)S(1)}) custom-call(bf16[128,2048]{1,0:T(8,128)(2,1)S(1)} %get-tuple-element.25.refs_0_, bf16[128,2048]{1,0:T(8,128)(2,1)S(1)} %get-tuple-element.26.refs_1_, bf16[144,512]{1,0:T(8,128)(2,1)S(1)} %shard_map.87.refs_2_, ...), custom_call_target="tpu_custom_call" | custom-call | flops 99999997952 | tf_op jit(solution)/shard_map/pallas_call | solution.py:58
  13.3 1.7 %collective-permute-start.5 = (bf16[128,512]{1,0:T(8,128)(2,1)S(1)}, bf16[128,512]{1,0:T(8,128)(2,1)S(1)}, u32[]{:S(2)}, u32[]{:S(2)}) collective-permute-start(bf16[128,512]{1,0:T(8,128)(2,1)S(1)} %get-tuple-element.28), channel_id=1, source_target_pairs={{0,7},{1,0},{2,1},{3,2},{4,3},{5,4},{6,5},{7,6},{8,15},{9,8},{10,9... | collective-permute-start | bytes 393224 | tf_op jit(solution)/shard_map/ppermute | solution.py:25
  15.0 2.8 %collective-permute-start = (bf16[128,512]{1,0:T(8,128)(2,1)S(1)}, bf16[128,512]{1,0:T(8,128)(2,1)S(1)}, u32[]{:S(2)}, u32[]{:S(2)}) collective-permute-start(bf16[128,512]{1,0:T(8,128)(2,1)S(1)} %get-tuple-element.20.refs_2_), channel_id=1, source_target_pairs={{0,1},{1,2},{2,3},{3,4},{4,5},{5,6},{6,7},{8,9},{9,10},{10,11},{11... | collective-permute-start | bytes 393224 | tf_op jit(solution)/shard_map/ppermute | solution.py:31
  17.8 1.2 %collective-permute-done.5.refs_3_ = bf16[128,512]{1,0:T(8,128)(2,1)S(1)} collective-permute-done((bf16[128,512]{1,0:T(8,128)(2,1)S(1)}, bf16[128,512]{1,0:T(8,128)(2,1)S(1)}, u32[]{:S(2)}, u32[]{:S(2)}) %collective-permute-start.5) | collective-permute-done | bytes 131104 | tf_op jit(solution)/shard_map/ppermute | solution.py:25
  19.0 1.4 %collective-permute-start.8 = (bf16[128,512]{1,0:T(8,128)(2,1)S(1)}, bf16[128,512]{1,0:T(8,128)(2,1)S(1)}, u32[]{:S(2)}, u32[]{:S(2)}) collective-permute-start(bf16[128,512]{1,0:T(8,128)(2,1)S(1)} %shard_map.89.refs_8_), channel_id=1, source_target_pairs={{0,2},{1,3},{2,0},{3,1},{4,6},{5,7},{6,4},{7,5},{8,10},{9,11},{10,... | collective-permute-start | bytes 393224 | tf_op jit(solution)/shard_map/ppermute | solution.py:36
  20.9 1.6 %collective-permute-start.6 = (bf16[128,512]{1,0:T(8,128)(2,1)S(1)}, bf16[128,512]{1,0:T(8,128)(2,1)S(1)}, u32[]{:S(2)}, u32[]{:S(2)}) collective-permute-start(bf16[128,512]{1,0:T(8,128)(2,1)S(1)} %shard_map.89.refs_8_), channel_id=1, source_target_pairs={{0,18},{1,19},{2,16},{3,17},{4,22},{5,23},{6,20},{7,21},{8,26},{9,... | collective-permute-start | bytes 393224 | tf_op jit(solution)/shard_map/ppermute | solution.py:36
  22.5 2.6 %collective-permute-done.1.refs_1_ = bf16[1024,128]{1,0:T(8,128)(2,1)S(1)} collective-permute-done((bf16[1024,128]{1,0:T(8,128)(2,1)S(1)}, bf16[1024,128]{1,0:T(8,128)(2,1)S(1)}, u32[]{:S(2)}, u32[]{:S(2)}) %collective-permute-start.1) | collective-permute-done | bytes 262176 | tf_op jit(solution)/shard_map/ppermute | solution.py:36
  25.1 2.8 %collective-permute-done.8.refs_7_ = bf16[128,512]{1,0:T(8,128)(2,1)S(1)} collective-permute-done((bf16[128,512]{1,0:T(8,128)(2,1)S(1)}, bf16[128,512]{1,0:T(8,128)(2,1)S(1)}, u32[]{:S(2)}, u32[]{:S(2)}) %collective-permute-start.8) | collective-permute-done | bytes 131104 | tf_op jit(solution)/shard_map/ppermute | solution.py:36
  27.9 1.3 %collective-permute-done.6.refs_5_ = bf16[128,512]{1,0:T(8,128)(2,1)S(1)} collective-permute-done((bf16[128,512]{1,0:T(8,128)(2,1)S(1)}, bf16[128,512]{1,0:T(8,128)(2,1)S(1)}, u32[]{:S(2)}, u32[]{:S(2)}) %collective-permute-start.6) | collective-permute-done | bytes 131104 | tf_op jit(solution)/shard_map/ppermute | solution.py:36
  30.0 1.2 %collective-permute-done.9.refs_1_ = bf16[512,256]{1,0:T(8,128)(2,1)S(1)} collective-permute-done((bf16[512,256]{1,0:T(8,128)(2,1)S(1)}, bf16[512,256]{1,0:T(8,128)(2,1)S(1)}, u32[]{:S(2)}, u32[]{:S(2)}) %collective-permute-start.9) | collective-permute-done | bytes 262176 | tf_op jit(solution)/shard_map/ppermute | solution.py:36
  31.2 2.9 %collective-permute-start.15 = (bf16[256,256]{1,0:T(8,128)(2,1)S(1)}, bf16[256,256]{1,0:T(8,128)(2,1)S(1)}, u32[]{:S(2)}, u32[]{:S(2)}) collective-permute-start(bf16[256,256]{1,0:T(8,128)(2,1)S(1)} %get-tuple-element.33), channel_id=1, source_target_pairs={{0,5},{1,4},{2,7},{3,6},{4,1},{5,0},{6,3},{7,2},{8,13},{9,12},{10,... | collective-permute-start | bytes 393224 | tf_op jit(solution)/shard_map/ppermute | solution.py:36
  35.0 1.2 %collective-permute-done.10.refs_1_ = bf16[512,256]{1,0:T(8,128)(2,1)S(1)} collective-permute-done((bf16[512,256]{1,0:T(8,128)(2,1)S(1)}, bf16[512,256]{1,0:T(8,128)(2,1)S(1)}, u32[]{:S(2)}, u32[]{:S(2)}) %collective-permute-start.10) | collective-permute-done | bytes 262176 | tf_op jit(solution)/shard_map/ppermute | solution.py:36
  36.3 1.4 %collective-permute-start.16 = (bf16[256,256]{1,0:T(8,128)(2,1)S(1)}, bf16[256,256]{1,0:T(8,128)(2,1)S(1)}, u32[]{:S(2)}, u32[]{:S(2)}) collective-permute-start(bf16[256,256]{1,0:T(8,128)(2,1)S(1)} %get-tuple-element.34), channel_id=1, source_target_pairs={{0,1},{1,0},{2,3},{3,2},{4,5},{5,4},{6,7},{7,6},{8,9},{9,8},{10,11... | collective-permute-start | bytes 393224 | tf_op jit(solution)/shard_map/ppermute | solution.py:36
  38.8 1.1 %collective-permute-start.13 = (bf16[528,128]{1,0:T(8,128)(2,1)S(1)}, bf16[528,128]{1,0:T(8,128)(2,1)S(1)}, u32[]{:S(2)}, u32[]{:S(2)}) collective-permute-start(bf16[528,128]{1,0:T(8,128)(2,1)S(1)} %get-tuple-element.38), channel_id=1, source_target_pairs={{0,24},{8,16},{16,8},{24,0},{1,25},{9,17},{17,9},{25,1},{2,26},{10... | collective-permute-start | bytes 405512 | tf_op jit(solution)/shard_map/ppermute | solution.py:36
  40.5 4.6 %collective-permute-done.15.refs_3_ = bf16[256,256]{1,0:T(8,128)(2,1)S(1)} collective-permute-done((bf16[256,256]{1,0:T(8,128)(2,1)S(1)}, bf16[256,256]{1,0:T(8,128)(2,1)S(1)}, u32[]{:S(2)}, u32[]{:S(2)}) %collective-permute-start.15) | collective-permute-done | bytes 131104 | tf_op jit(solution)/shard_map/ppermute | solution.py:36
  45.0 1.2 %collective-permute-done.14.refs_2_ = bf16[256,256]{1,0:T(8,128)(2,1)S(1)} collective-permute-done((bf16[256,256]{1,0:T(8,128)(2,1)S(1)}, bf16[256,256]{1,0:T(8,128)(2,1)S(1)}, u32[]{:S(2)}, u32[]{:S(2)}) %collective-permute-start.14) | collective-permute-done | bytes 131104 | tf_op jit(solution)/shard_map/ppermute | solution.py:36
  46.3 1.5 %collective-permute-start.17 = (bf16[256,256]{1,0:T(8,128)(2,1)S(1)}, bf16[256,256]{1,0:T(8,128)(2,1)S(1)}, u32[]{:S(2)}, u32[]{:S(2)}) collective-permute-start(bf16[256,256]{1,0:T(8,128)(2,1)S(1)} %shard_map.98.refs_0_), channel_id=1, source_target_pairs={{0,16},{1,17},{2,18},{3,19},{4,20},{5,21},{6,22},{7,23},{8,24},{9,... | collective-permute-start | bytes 393224 | tf_op jit(solution)/shard_map/ppermute | solution.py:36
  47.8 1.5 %collective-permute-start.21 = (bf16[256,256]{1,0:T(8,128)(2,1)S(1)}, bf16[256,256]{1,0:T(8,128)(2,1)S(1)}, u32[]{:S(2)}, u32[]{:S(2)}) collective-permute-start(bf16[256,256]{1,0:T(8,128)(2,1)S(1)} %shard_map.98.refs_0_), channel_id=1, source_target_pairs={{0,1},{1,0},{2,3},{3,2},{4,5},{5,4},{6,7},{7,6},{8,9},{9,8},{10,11... | collective-permute-start | bytes 393224 | tf_op jit(solution)/shard_map/ppermute | solution.py:36
  49.9 1.9 %collective-permute-done.17.refs_1_ = bf16[256,256]{1,0:T(8,128)(2,1)S(1)} collective-permute-done((bf16[256,256]{1,0:T(8,128)(2,1)S(1)}, bf16[256,256]{1,0:T(8,128)(2,1)S(1)}, u32[]{:S(2)}, u32[]{:S(2)}) %collective-permute-start.17) | collective-permute-done | bytes 131104 | tf_op jit(solution)/shard_map/ppermute | solution.py:36
  (44 shorter events, 11.6 us)
Async XLA Ops:
  1.6 10.0 %collective-permute-start.4 = (bf16[144,512]{1,0:T(8,128)(2,1)S(1)}, bf16[144,512]{1,0:T(8,128)(2,1)S(1)}, u32[]{:S(2)}, u32[]{:S(2)}) collective-permute-start(bf16[144,512]{1,0:T(8,128)(2,1)S(1)} %shard_map.87.refs_2_), channel_id=1, source_target_pairs={{0,1},{1,2},{2,3},{3,4},{4,5},{5,6},{6,7},{7,0},{8,9},{9,10},{10,1... | collective-permute-start | bytes 442376 | tf_op jit(solution)/shard_map/ppermute | solution.py:25
  6.2 11.6 %collective-permute-start.2 = (bf16[1024,128]{1,0:T(8,128)(2,1)S(1)}, bf16[1024,128]{1,0:T(8,128)(2,1)S(1)}, u32[]{:S(2)}, u32[]{:S(2)}) collective-permute-start(bf16[1024,128]{1,0:T(8,128)(2,1)S(1)} %get-tuple-element.22), channel_id=1, source_target_pairs={{0,16},{1,17},{2,18},{3,19},{4,20},{5,21},{6,22},{7,23},{8,24},{9,... | collective-permute-start | bytes 786440 | tf_op jit(solution)/shard_map/ppermute | solution.py:36
  7.8 10.0 %collective-permute-start.3 = (bf16[1024,128]{1,0:T(8,128)(2,1)S(1)}, bf16[1024,128]{1,0:T(8,128)(2,1)S(1)}, u32[]{:S(2)}, u32[]{:S(2)}) collective-permute-start(bf16[1024,128]{1,0:T(8,128)(2,1)S(1)} %get-tuple-element.23), channel_id=1, source_target_pairs={{0,2},{1,3},{2,0},{3,1},{4,6},{5,7},{6,4},{7,5},{8,10},{9,11},{10,... | collective-permute-start | bytes 786440 | tf_op jit(solution)/shard_map/ppermute | solution.py:36
  13.3 5.7 %collective-permute-start.5 = (bf16[128,512]{1,0:T(8,128)(2,1)S(1)}, bf16[128,512]{1,0:T(8,128)(2,1)S(1)}, u32[]{:S(2)}, u32[]{:S(2)}) collective-permute-start(bf16[128,512]{1,0:T(8,128)(2,1)S(1)} %get-tuple-element.28), channel_id=1, source_target_pairs={{0,7},{1,0},{2,1},{3,2},{4,3},{5,4},{6,5},{7,6},{8,15},{9,8},{10,9... | collective-permute-start | bytes 393224 | tf_op jit(solution)/shard_map/ppermute | solution.py:25
  15.0 10.2 %collective-permute-start.1 = (bf16[1024,128]{1,0:T(8,128)(2,1)S(1)}, bf16[1024,128]{1,0:T(8,128)(2,1)S(1)}, u32[]{:S(2)}, u32[]{:S(2)}) collective-permute-start(bf16[1024,128]{1,0:T(8,128)(2,1)S(1)} %get-tuple-element.21), channel_id=1, source_target_pairs={{0,18},{1,19},{2,16},{3,17},{4,22},{5,23},{6,20},{7,21},{8,26},{9,... | collective-permute-start | bytes 786440 | tf_op jit(solution)/shard_map/ppermute | solution.py:36
  15.0 7.5 %collective-permute-start = (bf16[128,512]{1,0:T(8,128)(2,1)S(1)}, bf16[128,512]{1,0:T(8,128)(2,1)S(1)}, u32[]{:S(2)}, u32[]{:S(2)}) collective-permute-start(bf16[128,512]{1,0:T(8,128)(2,1)S(1)} %get-tuple-element.20.refs_2_), channel_id=1, source_target_pairs={{0,1},{1,2},{2,3},{3,4},{4,5},{5,6},{6,7},{8,9},{9,10},{10,11},{11... | collective-permute-start | bytes 393224 | tf_op jit(solution)/shard_map/ppermute | solution.py:31
  19.0 9.0 %collective-permute-start.8 = (bf16[128,512]{1,0:T(8,128)(2,1)S(1)}, bf16[128,512]{1,0:T(8,128)(2,1)S(1)}, u32[]{:S(2)}, u32[]{:S(2)}) collective-permute-start(bf16[128,512]{1,0:T(8,128)(2,1)S(1)} %shard_map.89.refs_8_), channel_id=1, source_target_pairs={{0,2},{1,3},{2,0},{3,1},{4,6},{5,7},{6,4},{7,5},{8,10},{9,11},{10,... | collective-permute-start | bytes 393224 | tf_op jit(solution)/shard_map/ppermute | solution.py:36
  20.4 7.6 %collective-permute-start.7 = (bf16[128,512]{1,0:T(8,128)(2,1)S(1)}, bf16[128,512]{1,0:T(8,128)(2,1)S(1)}, u32[]{:S(2)}, u32[]{:S(2)}) collective-permute-start(bf16[128,512]{1,0:T(8,128)(2,1)S(1)} %shard_map.89.refs_8_), channel_id=1, source_target_pairs={{0,16},{1,17},{2,18},{3,19},{4,20},{5,21},{6,22},{7,23},{8,24},{9,... | collective-permute-start | bytes 393224 | tf_op jit(solution)/shard_map/ppermute | solution.py:36
  20.9 8.4 %collective-permute-start.6 = (bf16[128,512]{1,0:T(8,128)(2,1)S(1)}, bf16[128,512]{1,0:T(8,128)(2,1)S(1)}, u32[]{:S(2)}, u32[]{:S(2)}) collective-permute-start(bf16[128,512]{1,0:T(8,128)(2,1)S(1)} %shard_map.89.refs_8_), channel_id=1, source_target_pairs={{0,18},{1,19},{2,16},{3,17},{4,22},{5,23},{6,20},{7,21},{8,26},{9,... | collective-permute-start | bytes 393224 | tf_op jit(solution)/shard_map/ppermute | solution.py:36
  29.6 1.6 %collective-permute-start.9 = (bf16[512,256]{1,0:T(8,128)(2,1)S(1)}, bf16[512,256]{1,0:T(8,128)(2,1)S(1)}, u32[]{:S(2)}, u32[]{:S(2)}) collective-permute-start(bf16[512,256]{1,0:T(8,128)(2,1)S(1)} %shard_map.91), channel_id=1, source_target_pairs={{0,8},{8,0},{16,24},{24,16},{1,9},{9,1},{17,25},{25,17},{2,10},{10... | collective-permute-start | bytes 786440 | tf_op jit(solution)/shard_map/ppermute | solution.py:36
  31.2 13.8 %collective-permute-start.15 = (bf16[256,256]{1,0:T(8,128)(2,1)S(1)}, bf16[256,256]{1,0:T(8,128)(2,1)S(1)}, u32[]{:S(2)}, u32[]{:S(2)}) collective-permute-start(bf16[256,256]{1,0:T(8,128)(2,1)S(1)} %get-tuple-element.33), channel_id=1, source_target_pairs={{0,5},{1,4},{2,7},{3,6},{4,1},{5,0},{6,3},{7,2},{8,13},{9,12},{10,... | collective-permute-start | bytes 393224 | tf_op jit(solution)/shard_map/ppermute | solution.py:36
  34.2 12.1 %collective-permute-start.14 = (bf16[256,256]{1,0:T(8,128)(2,1)S(1)}, bf16[256,256]{1,0:T(8,128)(2,1)S(1)}, u32[]{:S(2)}, u32[]{:S(2)}) collective-permute-start(bf16[256,256]{1,0:T(8,128)(2,1)S(1)} %get-tuple-element.29.refs_0_), channel_id=1, source_target_pairs={{0,4},{1,5},{2,6},{3,7},{4,0},{5,1},{6,2},{7,3},{8,12},{9,13},{10,... | collective-permute-start | bytes 393224 | tf_op jit(solution)/shard_map/ppermute | solution.py:36
  34.6 1.6 %collective-permute-start.10 = (bf16[512,256]{1,0:T(8,128)(2,1)S(1)}, bf16[512,256]{1,0:T(8,128)(2,1)S(1)}, u32[]{:S(2)}, u32[]{:S(2)}) collective-permute-start(bf16[512,256]{1,0:T(8,128)(2,1)S(1)} %shard_map.94), channel_id=1, source_target_pairs={{0,8},{8,0},{16,24},{24,16},{1,9},{9,1},{17,25},{25,17},{2,10},{10... | collective-permute-start | bytes 786440 | tf_op jit(solution)/shard_map/ppermute | solution.py:36
  36.3 10.0 %collective-permute-start.16 = (bf16[256,256]{1,0:T(8,128)(2,1)S(1)}, bf16[256,256]{1,0:T(8,128)(2,1)S(1)}, u32[]{:S(2)}, u32[]{:S(2)}) collective-permute-start(bf16[256,256]{1,0:T(8,128)(2,1)S(1)} %get-tuple-element.34), channel_id=1, source_target_pairs={{0,1},{1,0},{2,3},{3,2},{4,5},{5,4},{6,7},{7,6},{8,9},{9,8},{10,11... | collective-permute-start | bytes 393224 | tf_op jit(solution)/shard_map/ppermute | solution.py:36
  38.8 10.5 %collective-permute-start.13 = (bf16[528,128]{1,0:T(8,128)(2,1)S(1)}, bf16[528,128]{1,0:T(8,128)(2,1)S(1)}, u32[]{:S(2)}, u32[]{:S(2)}) collective-permute-start(bf16[528,128]{1,0:T(8,128)(2,1)S(1)} %get-tuple-element.38), channel_id=1, source_target_pairs={{0,24},{8,16},{16,8},{24,0},{1,25},{9,17},{17,9},{25,1},{2,26},{10... | collective-permute-start | bytes 405512 | tf_op jit(solution)/shard_map/ppermute | solution.py:36
  39.8 10.0 %collective-permute-start.12 = (bf16[528,128]{1,0:T(8,128)(2,1)S(1)}, bf16[528,128]{1,0:T(8,128)(2,1)S(1)}, u32[]{:S(2)}, u32[]{:S(2)}) collective-permute-start(bf16[528,128]{1,0:T(8,128)(2,1)S(1)} %get-tuple-element.39), channel_id=1, source_target_pairs={{0,16},{8,24},{16,0},{24,8},{1,17},{9,25},{17,1},{25,9},{2,18},{10... | collective-permute-start | bytes 405512 | tf_op jit(solution)/shard_map/ppermute | solution.py:36
  45.0 6.7 %collective-permute-start.11 = (bf16[528,128]{1,0:T(8,128)(2,1)S(1)}, bf16[528,128]{1,0:T(8,128)(2,1)S(1)}, u32[]{:S(2)}, u32[]{:S(2)}) collective-permute-start(bf16[528,128]{1,0:T(8,128)(2,1)S(1)} %get-tuple-element.40), channel_id=1, source_target_pairs={{0,8},{8,0},{16,24},{24,16},{1,9},{9,1},{17,25},{25,17},{2,10},{10... | collective-permute-start | bytes 405512 | tf_op jit(solution)/shard_map/ppermute | solution.py:36
  46.3 5.5 %collective-permute-start.17 = (bf16[256,256]{1,0:T(8,128)(2,1)S(1)}, bf16[256,256]{1,0:T(8,128)(2,1)S(1)}, u32[]{:S(2)}, u32[]{:S(2)}) collective-permute-start(bf16[256,256]{1,0:T(8,128)(2,1)S(1)} %shard_map.98.refs_0_), channel_id=1, source_target_pairs={{0,16},{1,17},{2,18},{3,19},{4,20},{5,21},{6,22},{7,23},{8,24},{9,... | collective-permute-start | bytes 393224 | tf_op jit(solution)/shard_map/ppermute | solution.py:36
  47.8 7.8 %collective-permute-start.21 = (bf16[256,256]{1,0:T(8,128)(2,1)S(1)}, bf16[256,256]{1,0:T(8,128)(2,1)S(1)}, u32[]{:S(2)}, u32[]{:S(2)}) collective-permute-start(bf16[256,256]{1,0:T(8,128)(2,1)S(1)} %shard_map.98.refs_0_), channel_id=1, source_target_pairs={{0,1},{1,0},{2,3},{3,2},{4,5},{5,4},{6,7},{7,6},{8,9},{9,8},{10,11... | collective-permute-start | bytes 393224 | tf_op jit(solution)/shard_map/ppermute | solution.py:36
  49.3 5.9 %collective-permute-start.20 = (bf16[256,256]{1,0:T(8,128)(2,1)S(1)}, bf16[256,256]{1,0:T(8,128)(2,1)S(1)}, u32[]{:S(2)}, u32[]{:S(2)}) collective-permute-start(bf16[256,256]{1,0:T(8,128)(2,1)S(1)} %shard_map.98.refs_0_), channel_id=1, source_target_pairs={{0,17},{1,16},{2,19},{3,18},{4,21},{5,20},{6,23},{7,22},{8,25},{9,... | collective-permute-start | bytes 393224 | tf_op jit(solution)/shard_map/ppermute | solution.py:36
  49.9 2.9 %collective-permute-start.18 = (bf16[256,256]{1,0:T(8,128)(2,1)S(1)}, bf16[256,256]{1,0:T(8,128)(2,1)S(1)}, u32[]{:S(2)}, u32[]{:S(2)}) collective-permute-start(bf16[256,256]{1,0:T(8,128)(2,1)S(1)} %shard_map.98.refs_0_), channel_id=1, source_target_pairs={{0,8},{8,0},{16,24},{24,16},{1,9},{9,1},{17,25},{25,17},{2,10},{10... | collective-permute-start | bytes 393224 | tf_op jit(solution)/shard_map/ppermute | solution.py:36
  51.8 1.3 %collective-permute-start.19 = (bf16[256,256]{1,0:T(8,128)(2,1)S(1)}, bf16[256,256]{1,0:T(8,128)(2,1)S(1)}, u32[]{:S(2)}, u32[]{:S(2)}) collective-permute-start(bf16[256,256]{1,0:T(8,128)(2,1)S(1)} %collective-permute-done.17.refs_1_), channel_id=1, source_target_pairs={{0,8},{8,0},{16,24},{24,16},{1,9},{9,1},{17,25},{25,17},{2,10},{10... | collective-permute-start | bytes 393224 | tf_op jit(solution)/shard_map/ppermute | solution.py:36
  55.2 1.4 %collective-permute-start.22 = (bf16[256,256]{1,0:T(8,128)(2,1)S(1)}, bf16[256,256]{1,0:T(8,128)(2,1)S(1)}, u32[]{:S(2)}, u32[]{:S(2)}) collective-permute-start(bf16[256,256]{1,0:T(8,128)(2,1)S(1)} %shard_map.100.refs_0_), channel_id=1, source_target_pairs={{0,8},{8,0},{16,24},{24,16},{1,9},{9,1},{17,25},{25,17},{2,10},{10... | collective-permute-start | bytes 393224 | tf_op jit(solution)/shard_map/ppermute | solution.py:36
  55.6 1.4 %collective-permute-start.23 = (bf16[256,256]{1,0:T(8,128)(2,1)S(1)}, bf16[256,256]{1,0:T(8,128)(2,1)S(1)}, u32[]{:S(2)}, u32[]{:S(2)}) collective-permute-start(bf16[256,256]{1,0:T(8,128)(2,1)S(1)} %shard_map.101.refs_1_), channel_id=1, source_target_pairs={{0,8},{8,0},{16,24},{24,16},{1,9},{9,1},{17,25},{25,17},{2,10},{10... | collective-permute-start | bytes 393224 | tf_op jit(solution)/shard_map/ppermute | solution.py:36
  (1 other events, 3.1 us)

commit v6 on v5

--- a/solution.py
+++ b/solution.py
@@ -103,7 +103,7 @@
     return jnp.sum(jnp.where(eye, row, 0.0), axis=1, keepdims=True)
 
 
-def probs_body(q_ref, g_ref, k_ref, prior_ref, pt_ref, back_ref, own_ref):
+def probs_body(q_ref, g_ref, k_ref, prior_ref, pt_ref, back_ref):
     tokens = q_ref.shape[0]
     u = lax.broadcasted_iota(jnp.int32, (tokens, tokens), 0)
     t = lax.broadcasted_iota(jnp.int32, (tokens, tokens), 1)
@@ -115,7 +115,7 @@
     own_ok = (column_of(own_docs, eye) == own_docs) & (u <= t)
     prior_ok = jnp.concatenate([prior_ok] * GROUP, 1)
     own_ok = jnp.concatenate([own_ok] * GROUP, 1)
-    scale = 1.0 / math.sqrt(HEAD_DIM)
+    scale = math.log2(math.e) / math.sqrt(HEAD_DIM)
     for g in range(KV_HEADS):
         heads = [slice((g * GROUP + r) * HEAD_DIM, (g * GROUP + r + 1) * HEAD_DIM) for r in range(GROUP)]
         col = slice(g * HEAD_DIM, (g + 1) * HEAD_DIM)
@@ -124,15 +124,22 @@
         sp = jnp.where(prior_ok, dot(prior_ref[:tokens, col], q4, ((1,), (1,))), MASKED)
         so = jnp.where(own_ok, dot(k_ref[:tokens, col], q4, ((1,), (1,))), MASKED)
         top = jnp.maximum(jnp.max(sp, 0, keepdims=True), jnp.max(so, 0, keepdims=True))
-        ep = jnp.exp((sp - top) * scale)
-        eo = jnp.exp((so - top) * scale)
+        ep = jnp.exp2((sp - top) * scale)
+        eo = jnp.exp2((so - top) * scale)
         inv = 1.0 / (jnp.sum(ep, 0, keepdims=True) + jnp.sum(eo, 0, keepdims=True))
         pp = (ep * inv).astype(BF16)
         po = (eo * inv).astype(BF16)
         pt_ref[g, :tokens, :] = pp
         pt_ref[g, tokens:, :] = po
         back_ref[:, col] = dot(pp, g4, ((1,), (0,))).astype(BF16)
-        own_ref[:, col] = dot(po, g4, ((1,), (0,)))
+
+
+def own_body(pt_ref, g_ref, own_ref):
+    tokens = g_ref.shape[0]
+    for g in range(KV_HEADS):
+        heads = [slice((g * GROUP + r) * HEAD_DIM, (g * GROUP + r + 1) * HEAD_DIM) for r in range(GROUP)]
+        g4 = jnp.concatenate([g_ref[:, h] for h in heads], 0)
+        own_ref[:, g * HEAD_DIM : (g + 1) * HEAD_DIM] = dot(pt_ref[g, tokens:, :], g4, ((1,), (0,)))
 
 
 def copy_body(in_ref, out_ref):
@@ -315,26 +322,24 @@
 
         def gather(value_of):
             far_first = [away(value_of(k), *place) for k, place in reversed([*enumerate(places)]) if k]
-            return far_first + [value_of(0)]
+            x, z = far_first[1:]
+            return [far_first[0], z, x, value_of(0)]
 
         mine_in = gather(lambda k: pieces[k])
     else:
         q_rows, g_rows, value_rows = queries[0], grad_out[0], values[0]
 
-    probs, back, own = call(
+    probs, back = call(
         probs_body,
-        [
-            shape(KV_HEADS, 2 * tokens, GROUP * tokens),
-            shape(tokens, kv_width),
-            shape(tokens, kv_width, dtype=F32),
-        ],
+        [shape(KV_HEADS, 2 * tokens, GROUP * tokens), shape(tokens, kv_width)],
         [q_rows, g_rows, message, prior],
         weight=100,
     )
+    (own,) = call(own_body, [shape(tokens, kv_width, dtype=F32)], [probs, g_rows], weight=1)
     returned = from_behind(back, shards, -1)
     prior_values = open_ended(value_rows, shards, 1)
     if by_chips:
-        (grad_values,) = call(both_body, [shape(tokens, kv_width)], [own, returned], deps=mine_in[1:3])
+        (grad_values,) = call(both_body, [shape(tokens, kv_width)], [own, returned], deps=mine_in[1:3], weight=0)
         grads = gather(lambda k: grad_values)
         factors = [*mine_in, *grads]
 

time: 58.2 us -> 57.8 us (level)
  waiting for transfers between devices: 23 us -> 22.2 us
    pallas_call x17 -> x18, Pallas kernels: 9.7 us -> 9.84 us  [call(): pl.pallas_call(lambda *refs: body(*refs[skip:]), out_shape=[pltpu.HBM(o.s...]
  transfers between devices with their start and end apart: 24 -> 24, of which waited for: 15 -> 13; matrix products, arithmetic and copies ran while one was open for 0% -> 0% of each run, Pallas kernels for 13% -> 13%
where the time goes in v6:
time: 57.8 us; the launch traced here: 57.6 us
  starting transfers between devices  24.7 us (43%)
  waiting for transfers between devices  22.2 us (38%)
  Pallas kernels  9.84 us (17%)
  between operations  0.83 us (1%)
    ppermute x21, waiting for transfers between devices, swap(): return lax.ppermute(value, axis, [(i, i ^ mask) for i in range(devices)])  19.2 us
    ppermute x21, starting transfers between devices, swap(): return lax.ppermute(value, axis, [(i, i ^ mask) for i in range(devices)])  17.1 us
    pallas_call x18, Pallas kernels, call(): pl.pallas_call(lambda *refs: body(*refs[skip:]), out_shape=[pltpu.HBM(o.s...  9.84 us
    ppermute x2, starting transfers between devices, from_behind(): lax.ppermute(value, axis, [(i, (i + by) % devices) for i in range(devices)])  4.71 us
    ppermute x2, waiting for transfers between devices, from_behind(): lax.ppermute(value, axis, [(i, (i + by) % devices) for i in range(devices)])  2.99 us
    ppermute x1, starting transfers between devices, open_ended(): return lax.ppermute(value, axis, pairs)  2.9 us
  transfers between devices with their start and end apart: 24, of which 13 were waited for; matrix products, arithmetic and copies ran while one was open for 0% of the time, Pallas kernels for 13%

profile of v6, /device:TPU:0, one launch (start us, length us, event | category | flops | bytes accessed | tf_op | source)
XLA Modules:
  0.0 57.6 jit_solution(2207622538445309456)
XLA Ops:
  1.6 3.0 %collective-permute-start.4 = (bf16[144,512]{1,0:T(8,128)(2,1)S(1)}, bf16[144,512]{1,0:T(8,128)(2,1)S(1)}, u32[]{:S(2)}, u32[]{:S(2)}) collective-permute-start(bf16[144,512]{1,0:T(8,128)(2,1)S(1)} %shard_map.87.refs_2_), channel_id=1, source_target_pairs={{0,1},{1,2},{2,3},{3,4},{4,5},{5,6},{6,7},{7,0},{8,9},{9,10},{10,1... | collective-permute-start | bytes 442376 | tf_op jit(solution)/shard_map/ppermute | solution.py:25
  4.6 1.6 %shard_map.86 = (bf16[1024,128]{1,0:T(8,128)(2,1)S(1)}, bf16[1024,128]{1,0:T(8,128)(2,1)S(1)}, bf16[1024,128]{1,0:T(8,128)(2,1)S(1)}, bf16[1024,128]{1,0:T(8,128...) custom-call(bf16[128,4096]{1,0:T(8,128)(2,1)} %bitcast.16, ...), custom_call_target="tpu_custom_call" | custom-call | tf_op jit(solution)/shard_map/pallas_call | solution.py:58
  6.2 1.6 %collective-permute-start.2 = (bf16[1024,128]{1,0:T(8,128)(2,1)S(1)}, bf16[1024,128]{1,0:T(8,128)(2,1)S(1)}, u32[]{:S(2)}, u32[]{:S(2)}) collective-permute-start(bf16[1024,128]{1,0:T(8,128)(2,1)S(1)} %get-tuple-element.21), channel_id=1, source_target_pairs={{0,2},{1,3},{2,0},{3,1},{4,6},{5,7},{6,4},{7,5},{8,10},{9,11},{10,... | collective-permute-start | bytes 786440 | tf_op jit(solution)/shard_map/ppermute | solution.py:36
  7.8 1.5 %collective-permute-start.3 = (bf16[1024,128]{1,0:T(8,128)(2,1)S(1)}, bf16[1024,128]{1,0:T(8,128)(2,1)S(1)}, u32[]{:S(2)}, u32[]{:S(2)}) collective-permute-start(bf16[1024,128]{1,0:T(8,128)(2,1)S(1)} %get-tuple-element.22), channel_id=1, source_target_pairs={{0,16},{1,17},{2,18},{3,19},{4,20},{5,21},{6,22},{7,23},{8,24},{9,... | collective-permute-start | bytes 786440 | tf_op jit(solution)/shard_map/ppermute | solution.py:36
  9.3 2.3 %collective-permute-done.4.refs_3_ = bf16[144,512]{1,0:T(8,128)(2,1)S(1)} collective-permute-done((bf16[144,512]{1,0:T(8,128)(2,1)S(1)}, bf16[144,512]{1,0:T(8,128)(2,1)S(1)}, u32[]{:S(2)}, u32[]{:S(2)}) %collective-permute-start.4) | collective-permute-done | bytes 147488 | tf_op jit(solution)/shard_map/ppermute | solution.py:25
  11.6 1.6 %shard_map.88 = (bf16[4,256,512]{2,1,0:T(8,128)(2,1)S(1)}, bf16[128,512]{1,0:T(8,128)(2,1)S(1)}) custom-call(bf16[128,2048]{1,0:T(8,128)(2,1)S(1)} %get-tuple-element.24.refs_0_, bf16[128,2048]{1,0:T(8,128)(2,1)S(1)} %get-tuple-element.25.refs_1_, bf16[144,512]{1,0:T(8,128)(2,1)S(1)} %shard_map.87.refs_2_, bf16[144,512]{1,0:T(8,128)(2,1)S(1)} %collective-permute-done.4.refs_3_), custom_call_target="tpu_custom_call" | custom-call | flops 99999997952 | tf_op jit(solution)/shard_map/pallas_call | solution.py:58
  13.1 1.7 %collective-permute-start.5 = (bf16[128,512]{1,0:T(8,128)(2,1)S(1)}, bf16[128,512]{1,0:T(8,128)(2,1)S(1)}, u32[]{:S(2)}, u32[]{:S(2)}) collective-permute-start(bf16[128,512]{1,0:T(8,128)(2,1)S(1)} %get-tuple-element.27), channel_id=1, source_target_pairs={{0,7},{1,0},{2,1},{3,2},{4,3},{5,4},{6,5},{7,6},{8,15},{9,8},{10,9... | collective-permute-start | bytes 393224 | tf_op jit(solution)/shard_map/ppermute | solution.py:25
  14.8 2.9 %collective-permute-start = (bf16[128,512]{1,0:T(8,128)(2,1)S(1)}, bf16[128,512]{1,0:T(8,128)(2,1)S(1)}, u32[]{:S(2)}, u32[]{:S(2)}) collective-permute-start(bf16[128,512]{1,0:T(8,128)(2,1)S(1)} %get-tuple-element.19.refs_2_), channel_id=1, source_target_pairs={{0,1},{1,2},{2,3},{3,4},{4,5},{5,6},{6,7},{8,9},{9,10},{10,11},{11... | collective-permute-start | bytes 393224 | tf_op jit(solution)/shard_map/ppermute | solution.py:31
  18.8 1.5 %collective-permute-start.8 = (bf16[128,512]{1,0:T(8,128)(2,1)S(1)}, bf16[128,512]{1,0:T(8,128)(2,1)S(1)}, u32[]{:S(2)}, u32[]{:S(2)}) collective-permute-start(bf16[128,512]{1,0:T(8,128)(2,1)S(1)} %shard_map.90.refs_8_), channel_id=1, source_target_pairs={{0,16},{1,17},{2,18},{3,19},{4,20},{5,21},{6,22},{7,23},{8,24},{9,... | collective-permute-start | bytes 393224 | tf_op jit(solution)/shard_map/ppermute | solution.py:36
  21.0 1.3 %collective-permute-start.6 = (bf16[128,512]{1,0:T(8,128)(2,1)S(1)}, bf16[128,512]{1,0:T(8,128)(2,1)S(1)}, u32[]{:S(2)}, u32[]{:S(2)}) collective-permute-start(bf16[128,512]{1,0:T(8,128)(2,1)S(1)} %shard_map.90.refs_8_), channel_id=1, source_target_pairs={{0,18},{1,19},{2,16},{3,17},{4,22},{5,23},{6,20},{7,21},{8,26},{9,... | collective-permute-start | bytes 393224 | tf_op jit(solution)/shard_map/ppermute | solution.py:36
  22.4 2.7 %collective-permute-done.1.refs_1_ = bf16[1024,128]{1,0:T(8,128)(2,1)S(1)} collective-permute-done((bf16[1024,128]{1,0:T(8,128)(2,1)S(1)}, bf16[1024,128]{1,0:T(8,128)(2,1)S(1)}, u32[]{:S(2)}, u32[]{:S(2)}) %collective-permute-start.1) | collective-permute-done | bytes 262176 | tf_op jit(solution)/shard_map/ppermute | solution.py:36
  25.1 2.5 %collective-permute-done.8.refs_7_ = bf16[128,512]{1,0:T(8,128)(2,1)S(1)} collective-permute-done((bf16[128,512]{1,0:T(8,128)(2,1)S(1)}, bf16[128,512]{1,0:T(8,128)(2,1)S(1)}, u32[]{:S(2)}, u32[]{:S(2)}) %collective-permute-start.8) | collective-permute-done | bytes 131104 | tf_op jit(solution)/shard_map/ppermute | solution.py:36
  27.6 1.4 %collective-permute-done.6.refs_5_ = bf16[128,512]{1,0:T(8,128)(2,1)S(1)} collective-permute-done((bf16[128,512]{1,0:T(8,128)(2,1)S(1)}, bf16[128,512]{1,0:T(8,128)(2,1)S(1)}, u32[]{:S(2)}, u32[]{:S(2)}) %collective-permute-start.6) | collective-permute-done | bytes 131104 | tf_op jit(solution)/shard_map/ppermute | solution.py:36
  29.7 1.2 %collective-permute-done.9.refs_1_ = bf16[512,256]{1,0:T(8,128)(2,1)S(1)} collective-permute-done((bf16[512,256]{1,0:T(8,128)(2,1)S(1)}, bf16[512,256]{1,0:T(8,128)(2,1)S(1)}, u32[]{:S(2)}, u32[]{:S(2)}) %collective-permute-start.9) | collective-permute-done | bytes 262176 | tf_op jit(solution)/shard_map/ppermute | solution.py:36
  31.0 3.0 %collective-permute-start.15 = (bf16[256,256]{1,0:T(8,128)(2,1)S(1)}, bf16[256,256]{1,0:T(8,128)(2,1)S(1)}, u32[]{:S(2)}, u32[]{:S(2)}) collective-permute-start(bf16[256,256]{1,0:T(8,128)(2,1)S(1)} %get-tuple-element.31), channel_id=1, source_target_pairs={{0,5},{1,4},{2,7},{3,6},{4,1},{5,0},{6,3},{7,2},{8,13},{9,12},{10,... | collective-permute-start | bytes 393224 | tf_op jit(solution)/shard_map/ppermute | solution.py:36
  35.0 1.2 %collective-permute-done.10.refs_1_ = bf16[512,256]{1,0:T(8,128)(2,1)S(1)} collective-permute-done((bf16[512,256]{1,0:T(8,128)(2,1)S(1)}, bf16[512,256]{1,0:T(8,128)(2,1)S(1)}, u32[]{:S(2)}, u32[]{:S(2)}) %collective-permute-start.10) | collective-permute-done | bytes 262176 | tf_op jit(solution)/shard_map/ppermute | solution.py:36
  36.2 1.3 %collective-permute-start.16 = (bf16[256,256]{1,0:T(8,128)(2,1)S(1)}, bf16[256,256]{1,0:T(8,128)(2,1)S(1)}, u32[]{:S(2)}, u32[]{:S(2)}) collective-permute-start(bf16[256,256]{1,0:T(8,128)(2,1)S(1)} %get-tuple-element.32), channel_id=1, source_target_pairs={{0,1},{1,0},{2,3},{3,2},{4,5},{5,4},{6,7},{7,6},{8,9},{9,8},{10,11... | collective-permute-start | bytes 393224 | tf_op jit(solution)/shard_map/ppermute | solution.py:36
  38.8 1.3 %collective-permute-start.12 = (bf16[528,128]{1,0:T(8,128)(2,1)S(1)}, bf16[528,128]{1,0:T(8,128)(2,1)S(1)}, u32[]{:S(2)}, u32[]{:S(2)}) collective-permute-start(bf16[528,128]{1,0:T(8,128)(2,1)S(1)} %get-tuple-element.37), channel_id=1, source_target_pairs={{0,16},{8,24},{16,0},{24,8},{1,17},{9,25},{17,1},{25,9},{2,18},{10... | collective-permute-start | bytes 405512 | tf_op jit(solution)/shard_map/ppermute | solution.py:36
  40.1 4.7 %collective-permute-done.15.refs_3_ = bf16[256,256]{1,0:T(8,128)(2,1)S(1)} collective-permute-done((bf16[256,256]{1,0:T(8,128)(2,1)S(1)}, bf16[256,256]{1,0:T(8,128)(2,1)S(1)}, u32[]{:S(2)}, u32[]{:S(2)}) %collective-permute-start.15) | collective-permute-done | bytes 131104 | tf_op jit(solution)/shard_map/ppermute | solution.py:36
  44.8 1.4 %collective-permute-done.14.refs_2_ = bf16[256,256]{1,0:T(8,128)(2,1)S(1)} collective-permute-done((bf16[256,256]{1,0:T(8,128)(2,1)S(1)}, bf16[256,256]{1,0:T(8,128)(2,1)S(1)}, u32[]{:S(2)}, u32[]{:S(2)}) %collective-permute-start.14) | collective-permute-done | bytes 131104 | tf_op jit(solution)/shard_map/ppermute | solution.py:36
  46.9 1.4 %collective-permute-start.21 = (bf16[256,256]{1,0:T(8,128)(2,1)S(1)}, bf16[256,256]{1,0:T(8,128)(2,1)S(1)}, u32[]{:S(2)}, u32[]{:S(2)}) collective-permute-start(bf16[256,256]{1,0:T(8,128)(2,1)S(1)} %shard_map.99.refs_0_), channel_id=1, source_target_pairs={{0,1},{1,0},{2,3},{3,2},{4,5},{5,4},{6,7},{7,6},{8,9},{9,8},{10,11... | collective-permute-start | bytes 393224 | tf_op jit(solution)/shard_map/ppermute | solution.py:36
  48.2 1.6 %collective-permute-start.20 = (bf16[256,256]{1,0:T(8,128)(2,1)S(1)}, bf16[256,256]{1,0:T(8,128)(2,1)S(1)}, u32[]{:S(2)}, u32[]{:S(2)}) collective-permute-start(bf16[256,256]{1,0:T(8,128)(2,1)S(1)} %shard_map.99.refs_0_), channel_id=1, source_target_pairs={{0,17},{1,16},{2,19},{3,18},{4,21},{5,20},{6,23},{7,22},{8,25},{9,... | collective-permute-start | bytes 393224 | tf_op jit(solution)/shard_map/ppermute | solution.py:36
  49.8 2.6 %collective-permute-done.17.refs_1_ = bf16[256,256]{1,0:T(8,128)(2,1)S(1)} collective-permute-done((bf16[256,256]{1,0:T(8,128)(2,1)S(1)}, bf16[256,256]{1,0:T(8,128)(2,1)S(1)}, u32[]{:S(2)}, u32[]{:S(2)}) %collective-permute-start.17) | collective-permute-done | bytes 131104 | tf_op jit(solution)/shard_map/ppermute | solution.py:36
  53.8 1.0 %shard_map.100 = (f32[1024,512]{1,0:T(8,128)}, f32[8,128]{1,0:T(8,128)S(1)}) custom-call(bf16[256,256]{1,0:T(8,128)(2,1)S(1)} %shard_map.99.refs_0_, bf16[256,256]{1,0:T(8,128)(2,1)S(1)} %collective-permute-done.17.refs_1_, bf16[256,256]{1,0:T(8,128)(2,1)S(1)} %collective-permute-done.18.refs_2_, bf16[256,256]{1,0:T(8,128)(2,1)S(1)} %collective-permute-done.19.refs_3_), custom_call_target="tpu_custom_call" | custom-call | flops 2000000000 | tf_op jit(solution)/shard_map/pallas_call | solution.py:58
  (45 shorter events, 10.4 us)
Async XLA Ops:
  1.6 10.0 %collective-permute-start.4 = (bf16[144,512]{1,0:T(8,128)(2,1)S(1)}, bf16[144,512]{1,0:T(8,128)(2,1)S(1)}, u32[]{:S(2)}, u32[]{:S(2)}) collective-permute-start(bf16[144,512]{1,0:T(8,128)(2,1)S(1)} %shard_map.87.refs_2_), channel_id=1, source_target_pairs={{0,1},{1,2},{2,3},{3,4},{4,5},{5,6},{6,7},{7,0},{8,9},{9,10},{10,1... | collective-permute-start | bytes 442376 | tf_op jit(solution)/shard_map/ppermute | solution.py:25
  6.2 11.8 %collective-permute-start.2 = (bf16[1024,128]{1,0:T(8,128)(2,1)S(1)}, bf16[1024,128]{1,0:T(8,128)(2,1)S(1)}, u32[]{:S(2)}, u32[]{:S(2)}) collective-permute-start(bf16[1024,128]{1,0:T(8,128)(2,1)S(1)} %get-tuple-element.21), channel_id=1, source_target_pairs={{0,2},{1,3},{2,0},{3,1},{4,6},{5,7},{6,4},{7,5},{8,10},{9,11},{10,... | collective-permute-start | bytes 786440 | tf_op jit(solution)/shard_map/ppermute | solution.py:36
  7.8 10.2 %collective-permute-start.3 = (bf16[1024,128]{1,0:T(8,128)(2,1)S(1)}, bf16[1024,128]{1,0:T(8,128)(2,1)S(1)}, u32[]{:S(2)}, u32[]{:S(2)}) collective-permute-start(bf16[1024,128]{1,0:T(8,128)(2,1)S(1)} %get-tuple-element.22), channel_id=1, source_target_pairs={{0,16},{1,17},{2,18},{3,19},{4,20},{5,21},{6,22},{7,23},{8,24},{9,... | collective-permute-start | bytes 786440 | tf_op jit(solution)/shard_map/ppermute | solution.py:36
  13.1 5.6 %collective-permute-start.5 = (bf16[128,512]{1,0:T(8,128)(2,1)S(1)}, bf16[128,512]{1,0:T(8,128)(2,1)S(1)}, u32[]{:S(2)}, u32[]{:S(2)}) collective-permute-start(bf16[128,512]{1,0:T(8,128)(2,1)S(1)} %get-tuple-element.27), channel_id=1, source_target_pairs={{0,7},{1,0},{2,1},{3,2},{4,3},{5,4},{6,5},{7,6},{8,15},{9,8},{10,9... | collective-permute-start | bytes 393224 | tf_op jit(solution)/shard_map/ppermute | solution.py:25
  14.8 10.2 %collective-permute-start.1 = (bf16[1024,128]{1,0:T(8,128)(2,1)S(1)}, bf16[1024,128]{1,0:T(8,128)(2,1)S(1)}, u32[]{:S(2)}, u32[]{:S(2)}) collective-permute-start(bf16[1024,128]{1,0:T(8,128)(2,1)S(1)} %get-tuple-element.20), channel_id=1, source_target_pairs={{0,18},{1,19},{2,16},{3,17},{4,22},{5,23},{6,20},{7,21},{8,26},{9,... | collective-permute-start | bytes 786440 | tf_op jit(solution)/shard_map/ppermute | solution.py:36
  14.8 7.5 %collective-permute-start = (bf16[128,512]{1,0:T(8,128)(2,1)S(1)}, bf16[128,512]{1,0:T(8,128)(2,1)S(1)}, u32[]{:S(2)}, u32[]{:S(2)}) collective-permute-start(bf16[128,512]{1,0:T(8,128)(2,1)S(1)} %get-tuple-element.19.refs_2_), channel_id=1, source_target_pairs={{0,1},{1,2},{2,3},{3,4},{4,5},{5,6},{6,7},{8,9},{9,10},{10,11},{11... | collective-permute-start | bytes 393224 | tf_op jit(solution)/shard_map/ppermute | solution.py:31
  18.8 8.8 %collective-permute-start.8 = (bf16[128,512]{1,0:T(8,128)(2,1)S(1)}, bf16[128,512]{1,0:T(8,128)(2,1)S(1)}, u32[]{:S(2)}, u32[]{:S(2)}) collective-permute-start(bf16[128,512]{1,0:T(8,128)(2,1)S(1)} %shard_map.90.refs_8_), channel_id=1, source_target_pairs={{0,16},{1,17},{2,18},{3,19},{4,20},{5,21},{6,22},{7,23},{8,24},{9,... | collective-permute-start | bytes 393224 | tf_op jit(solution)/shard_map/ppermute | solution.py:36
  20.4 7.2 %collective-permute-start.7 = (bf16[128,512]{1,0:T(8,128)(2,1)S(1)}, bf16[128,512]{1,0:T(8,128)(2,1)S(1)}, u32[]{:S(2)}, u32[]{:S(2)}) collective-permute-start(bf16[128,512]{1,0:T(8,128)(2,1)S(1)} %shard_map.90.refs_8_), channel_id=1, source_target_pairs={{0,2},{1,3},{2,0},{3,1},{4,6},{5,7},{6,4},{7,5},{8,10},{9,11},{10,... | collective-permute-start | bytes 393224 | tf_op jit(solution)/shard_map/ppermute | solution.py:36
  21.0 8.0 %collective-permute-start.6 = (bf16[128,512]{1,0:T(8,128)(2,1)S(1)}, bf16[128,512]{1,0:T(8,128)(2,1)S(1)}, u32[]{:S(2)}, u32[]{:S(2)}) collective-permute-start(bf16[128,512]{1,0:T(8,128)(2,1)S(1)} %shard_map.90.refs_8_), channel_id=1, source_target_pairs={{0,18},{1,19},{2,16},{3,17},{4,22},{5,23},{6,20},{7,21},{8,26},{9,... | collective-permute-start | bytes 393224 | tf_op jit(solution)/shard_map/ppermute | solution.py:36
  29.3 1.6 %collective-permute-start.9 = (bf16[512,256]{1,0:T(8,128)(2,1)S(1)}, bf16[512,256]{1,0:T(8,128)(2,1)S(1)}, u32[]{:S(2)}, u32[]{:S(2)}) collective-permute-start(bf16[512,256]{1,0:T(8,128)(2,1)S(1)} %shard_map.92), channel_id=1, source_target_pairs={{0,8},{8,0},{16,24},{24,16},{1,9},{9,1},{17,25},{25,17},{2,10},{10... | collective-permute-start | bytes 786440 | tf_op jit(solution)/shard_map/ppermute | solution.py:36
  31.0 13.8 %collective-permute-start.15 = (bf16[256,256]{1,0:T(8,128)(2,1)S(1)}, bf16[256,256]{1,0:T(8,128)(2,1)S(1)}, u32[]{:S(2)}, u32[]{:S(2)}) collective-permute-start(bf16[256,256]{1,0:T(8,128)(2,1)S(1)} %get-tuple-element.31), channel_id=1, source_target_pairs={{0,5},{1,4},{2,7},{3,6},{4,1},{5,0},{6,3},{7,2},{8,13},{9,12},{10,... | collective-permute-start | bytes 393224 | tf_op jit(solution)/shard_map/ppermute | solution.py:36
  34.0 12.2 %collective-permute-start.14 = (bf16[256,256]{1,0:T(8,128)(2,1)S(1)}, bf16[256,256]{1,0:T(8,128)(2,1)S(1)}, u32[]{:S(2)}, u32[]{:S(2)}) collective-permute-start(bf16[256,256]{1,0:T(8,128)(2,1)S(1)} %get-tuple-element.28.refs_0_), channel_id=1, source_target_pairs={{0,4},{1,5},{2,6},{3,7},{4,0},{5,1},{6,2},{7,3},{8,12},{9,13},{10,... | collective-permute-start | bytes 393224 | tf_op jit(solution)/shard_map/ppermute | solution.py:36
  34.6 1.6 %collective-permute-start.10 = (bf16[512,256]{1,0:T(8,128)(2,1)S(1)}, bf16[512,256]{1,0:T(8,128)(2,1)S(1)}, u32[]{:S(2)}, u32[]{:S(2)}) collective-permute-start(bf16[512,256]{1,0:T(8,128)(2,1)S(1)} %shard_map.95), channel_id=1, source_target_pairs={{0,8},{8,0},{16,24},{24,16},{1,9},{9,1},{17,25},{25,17},{2,10},{10... | collective-permute-start | bytes 786440 | tf_op jit(solution)/shard_map/ppermute | solution.py:36
  36.2 10.0 %collective-permute-start.16 = (bf16[256,256]{1,0:T(8,128)(2,1)S(1)}, bf16[256,256]{1,0:T(8,128)(2,1)S(1)}, u32[]{:S(2)}, u32[]{:S(2)}) collective-permute-start(bf16[256,256]{1,0:T(8,128)(2,1)S(1)} %get-tuple-element.32), channel_id=1, source_target_pairs={{0,1},{1,0},{2,3},{3,2},{4,5},{5,4},{6,7},{7,6},{8,9},{9,8},{10,11... | collective-permute-start | bytes 393224 | tf_op jit(solution)/shard_map/ppermute | solution.py:36
  38.6 9.7 %collective-permute-start.13 = (bf16[528,128]{1,0:T(8,128)(2,1)S(1)}, bf16[528,128]{1,0:T(8,128)(2,1)S(1)}, u32[]{:S(2)}, u32[]{:S(2)}) collective-permute-start(bf16[528,128]{1,0:T(8,128)(2,1)S(1)} %get-tuple-element.36), channel_id=1, source_target_pairs={{0,24},{8,16},{16,8},{24,0},{1,25},{9,17},{17,9},{25,1},{2,26},{10... | collective-permute-start | bytes 405512 | tf_op jit(solution)/shard_map/ppermute | solution.py:36
  38.8 11.0 %collective-permute-start.12 = (bf16[528,128]{1,0:T(8,128)(2,1)S(1)}, bf16[528,128]{1,0:T(8,128)(2,1)S(1)}, u32[]{:S(2)}, u32[]{:S(2)}) collective-permute-start(bf16[528,128]{1,0:T(8,128)(2,1)S(1)} %get-tuple-element.37), channel_id=1, source_target_pairs={{0,16},{8,24},{16,0},{24,8},{1,17},{9,25},{17,1},{25,9},{2,18},{10... | collective-permute-start | bytes 405512 | tf_op jit(solution)/shard_map/ppermute | solution.py:36
  44.8 7.7 %collective-permute-start.11 = (bf16[528,128]{1,0:T(8,128)(2,1)S(1)}, bf16[528,128]{1,0:T(8,128)(2,1)S(1)}, u32[]{:S(2)}, u32[]{:S(2)}) collective-permute-start(bf16[528,128]{1,0:T(8,128)(2,1)S(1)} %get-tuple-element.38), channel_id=1, source_target_pairs={{0,8},{8,0},{16,24},{24,16},{1,9},{9,1},{17,25},{25,17},{2,10},{10... | collective-permute-start | bytes 405512 | tf_op jit(solution)/shard_map/ppermute | solution.py:36
  46.3 6.2 %collective-permute-start.17 = (bf16[256,256]{1,0:T(8,128)(2,1)S(1)}, bf16[256,256]{1,0:T(8,128)(2,1)S(1)}, u32[]{:S(2)}, u32[]{:S(2)}) collective-permute-start(bf16[256,256]{1,0:T(8,128)(2,1)S(1)} %shard_map.99.refs_0_), channel_id=1, source_target_pairs={{0,16},{1,17},{2,18},{3,19},{4,20},{5,21},{6,22},{7,23},{8,24},{9,... | collective-permute-start | bytes 393224 | tf_op jit(solution)/shard_map/ppermute | solution.py:36
  46.9 8.3 %collective-permute-start.21 = (bf16[256,256]{1,0:T(8,128)(2,1)S(1)}, bf16[256,256]{1,0:T(8,128)(2,1)S(1)}, u32[]{:S(2)}, u32[]{:S(2)}) collective-permute-start(bf16[256,256]{1,0:T(8,128)(2,1)S(1)} %shard_map.99.refs_0_), channel_id=1, source_target_pairs={{0,1},{1,0},{2,3},{3,2},{4,5},{5,4},{6,7},{7,6},{8,9},{9,8},{10,11... | collective-permute-start | bytes 393224 | tf_op jit(solution)/shard_map/ppermute | solution.py:36
  48.2 6.6 %collective-permute-start.20 = (bf16[256,256]{1,0:T(8,128)(2,1)S(1)}, bf16[256,256]{1,0:T(8,128)(2,1)S(1)}, u32[]{:S(2)}, u32[]{:S(2)}) collective-permute-start(bf16[256,256]{1,0:T(8,128)(2,1)S(1)} %shard_map.99.refs_0_), channel_id=1, source_target_pairs={{0,17},{1,16},{2,19},{3,18},{4,21},{5,20},{6,23},{7,22},{8,25},{9,... | collective-permute-start | bytes 393224 | tf_op jit(solution)/shard_map/ppermute | solution.py:36
  49.8 3.6 %collective-permute-start.18 = (bf16[256,256]{1,0:T(8,128)(2,1)S(1)}, bf16[256,256]{1,0:T(8,128)(2,1)S(1)}, u32[]{:S(2)}, u32[]{:S(2)}) collective-permute-start(bf16[256,256]{1,0:T(8,128)(2,1)S(1)} %shard_map.99.refs_0_), channel_id=1, source_target_pairs={{0,8},{8,0},{16,24},{24,16},{1,9},{9,1},{17,25},{25,17},{2,10},{10... | collective-permute-start | bytes 393224 | tf_op jit(solution)/shard_map/ppermute | solution.py:36
  52.5 1.3 %collective-permute-start.19 = (bf16[256,256]{1,0:T(8,128)(2,1)S(1)}, bf16[256,256]{1,0:T(8,128)(2,1)S(1)}, u32[]{:S(2)}, u32[]{:S(2)}) collective-permute-start(bf16[256,256]{1,0:T(8,128)(2,1)S(1)} %collective-permute-done.17.refs_1_), channel_id=1, source_target_pairs={{0,8},{8,0},{16,24},{24,16},{1,9},{9,1},{17,25},{25,17},{2,10},{10... | collective-permute-start | bytes 393224 | tf_op jit(solution)/shard_map/ppermute | solution.py:36
  54.9 1.4 %collective-permute-start.22 = (bf16[256,256]{1,0:T(8,128)(2,1)S(1)}, bf16[256,256]{1,0:T(8,128)(2,1)S(1)}, u32[]{:S(2)}, u32[]{:S(2)}) collective-permute-start(bf16[256,256]{1,0:T(8,128)(2,1)S(1)} %shard_map.101.refs_0_), channel_id=1, source_target_pairs={{0,8},{8,0},{16,24},{24,16},{1,9},{9,1},{17,25},{25,17},{2,10},{10... | collective-permute-start | bytes 393224 | tf_op jit(solution)/shard_map/ppermute | solution.py:36
  55.2 1.4 %collective-permute-start.23 = (bf16[256,256]{1,0:T(8,128)(2,1)S(1)}, bf16[256,256]{1,0:T(8,128)(2,1)S(1)}, u32[]{:S(2)}, u32[]{:S(2)}) collective-permute-start(bf16[256,256]{1,0:T(8,128)(2,1)S(1)} %shard_map.102.refs_1_), channel_id=1, source_target_pairs={{0,8},{8,0},{16,24},{24,16},{1,9},{9,1},{17,25},{25,17},{2,10},{10... | collective-permute-start | bytes 393224 | tf_op jit(solution)/shard_map/ppermute | solution.py:36
  (1 other events, 2.9 us)

commit v7 on v6

--- a/solution.py
+++ b/solution.py
@@ -366,21 +366,24 @@
         [shape(micro, (q_width // LANES) * rows + LABEL_ROWS, LANES)],
         [probs, value_rows, prior_values, plan[0]],
         weight=100,
-        deps=[partial[0]] if by_chips else [],
+        deps=[far[0]] if by_chips else [],
     )
     arrived_out = [outgoing[0]] + [swap(outgoing[m], "dp", m) for m in range(1, micro)]
 
     token = shape(8, LANES, dtype=F32)
+    if by_chips:
+        (total,) = call(sum_body, [shape(sub, half)], [partial[0], *arrived], deps=[outgoing])
+
     placed, in_place = call(
         functools.partial(place_body, blocks),
         [shape(tokens, q_width), token],
         arrived_out,
         hbm_out=(0,),
         scratch=[pltpu.VMEM((micro, rows, q_width), BF16), pltpu.SemaphoreType.DMA((micro,))],
-        weight=2,
+        weight=100,
+        deps=[total] if by_chips else [],
     )
     if by_chips:
-        (total,) = call(sum_body, [shape(sub, half)], [partial[0], *arrived], deps=[outgoing])
         sums = [away(total, k // reps, 0, k % reps) for k in reversed(range(1, chips))]
         sums = [total, *reversed(sums)]
         others = {}

time: 57.8 us -> 57.8 us (level)
  no operation moved by 1% of the time
where the time goes in v7:
time: 57.8 us; the launch traced here: 57.6 us
  starting transfers between devices  24.9 us (43%)
  waiting for transfers between devices  22 us (38%)
  Pallas kernels  9.84 us (17%)
  between operations  0.83 us (1%)
    ppermute x21, waiting for transfers between devices, swap(): return lax.ppermute(value, axis, [(i, i ^ mask) for i in range(devices)])  19 us
    ppermute x21, starting transfers between devices, swap(): return lax.ppermute(value, axis, [(i, i ^ mask) for i in range(devices)])  17.3 us
    pallas_call x18, Pallas kernels, call(): pl.pallas_call(lambda *refs: body(*refs[skip:]), out_shape=[pltpu.HBM(o.s...  9.84 us
    ppermute x2, starting transfers between devices, from_behind(): lax.ppermute(value, axis, [(i, (i + by) % devices) for i in range(devices)])  4.71 us
    ppermute x2, waiting for transfers between devices, from_behind(): lax.ppermute(value, axis, [(i, (i + by) % devices) for i in range(devices)])  2.99 us
    ppermute x1, starting transfers between devices, open_ended(): return lax.ppermute(value, axis, pairs)  2.9 us
  transfers between devices with their start and end apart: 24, of which 13 were waited for; matrix products, arithmetic and copies ran while one was open for 0% of the time, Pallas kernels for 13%

profile of v7, /device:TPU:0, one launch (start us, length us, event | category | flops | bytes accessed | tf_op | source)
XLA Modules:
  0.0 57.6 jit_solution(6097973097693674119)
XLA Ops:
  1.6 3.0 %collective-permute-start.4 = (bf16[144,512]{1,0:T(8,128)(2,1)S(1)}, bf16[144,512]{1,0:T(8,128)(2,1)S(1)}, u32[]{:S(2)}, u32[]{:S(2)}) collective-permute-start(bf16[144,512]{1,0:T(8,128)(2,1)S(1)} %shard_map.87.refs_2_), channel_id=1, source_target_pairs={{0,1},{1,2},{2,3},{3,4},{4,5},{5,6},{6,7},{7,0},{8,9},{9,10},{10,1... | collective-permute-start | bytes 442376 | tf_op jit(solution)/shard_map/ppermute | solution.py:25
  4.6 1.6 %shard_map.86 = (bf16[1024,128]{1,0:T(8,128)(2,1)S(1)}, bf16[1024,128]{1,0:T(8,128)(2,1)S(1)}, bf16[1024,128]{1,0:T(8,128)(2,1)S(1)}, bf16[1024,128]{1,0:T(8,128...) custom-call(bf16[128,4096]{1,0:T(8,128)(2,1)} %bitcast.16, ...), custom_call_target="tpu_custom_call" | custom-call | tf_op jit(solution)/shard_map/pallas_call | solution.py:58
  6.2 1.6 %collective-permute-start.2 = (bf16[1024,128]{1,0:T(8,128)(2,1)S(1)}, bf16[1024,128]{1,0:T(8,128)(2,1)S(1)}, u32[]{:S(2)}, u32[]{:S(2)}) collective-permute-start(bf16[1024,128]{1,0:T(8,128)(2,1)S(1)} %get-tuple-element.21), channel_id=1, source_target_pairs={{0,2},{1,3},{2,0},{3,1},{4,6},{5,7},{6,4},{7,5},{8,10},{9,11},{10,... | collective-permute-start | bytes 786440 | tf_op jit(solution)/shard_map/ppermute | solution.py:36
  7.8 1.5 %collective-permute-start.3 = (bf16[1024,128]{1,0:T(8,128)(2,1)S(1)}, bf16[1024,128]{1,0:T(8,128)(2,1)S(1)}, u32[]{:S(2)}, u32[]{:S(2)}) collective-permute-start(bf16[1024,128]{1,0:T(8,128)(2,1)S(1)} %get-tuple-element.22), channel_id=1, source_target_pairs={{0,16},{1,17},{2,18},{3,19},{4,20},{5,21},{6,22},{7,23},{8,24},{9,... | collective-permute-start | bytes 786440 | tf_op jit(solution)/shard_map/ppermute | solution.py:36
  9.3 2.3 %collective-permute-done.4.refs_3_ = bf16[144,512]{1,0:T(8,128)(2,1)S(1)} collective-permute-done((bf16[144,512]{1,0:T(8,128)(2,1)S(1)}, bf16[144,512]{1,0:T(8,128)(2,1)S(1)}, u32[]{:S(2)}, u32[]{:S(2)}) %collective-permute-start.4) | collective-permute-done | bytes 147488 | tf_op jit(solution)/shard_map/ppermute | solution.py:25
  11.6 1.6 %shard_map.88 = (bf16[4,256,512]{2,1,0:T(8,128)(2,1)S(1)}, bf16[128,512]{1,0:T(8,128)(2,1)S(1)}) custom-call(bf16[128,2048]{1,0:T(8,128)(2,1)S(1)} %get-tuple-element.24.refs_0_, bf16[128,2048]{1,0:T(8,128)(2,1)S(1)} %get-tuple-element.25.refs_1_, bf16[144,512]{1,0:T(8,128)(2,1)S(1)} %shard_map.87.refs_2_, bf16[144,512]{1,0:T(8,128)(2,1)S(1)} %collective-permute-done.4.refs_3_), custom_call_target="tpu_custom_call" | custom-call | flops 99999997952 | tf_op jit(solution)/shard_map/pallas_call | solution.py:58
  13.1 1.7 %collective-permute-start.5 = (bf16[128,512]{1,0:T(8,128)(2,1)S(1)}, bf16[128,512]{1,0:T(8,128)(2,1)S(1)}, u32[]{:S(2)}, u32[]{:S(2)}) collective-permute-start(bf16[128,512]{1,0:T(8,128)(2,1)S(1)} %get-tuple-element.27), channel_id=1, source_target_pairs={{0,7},{1,0},{2,1},{3,2},{4,3},{5,4},{6,5},{7,6},{8,15},{9,8},{10,9... | collective-permute-start | bytes 393224 | tf_op jit(solution)/shard_map/ppermute | solution.py:25
  14.8 2.9 %collective-permute-start = (bf16[128,512]{1,0:T(8,128)(2,1)S(1)}, bf16[128,512]{1,0:T(8,128)(2,1)S(1)}, u32[]{:S(2)}, u32[]{:S(2)}) collective-permute-start(bf16[128,512]{1,0:T(8,128)(2,1)S(1)} %get-tuple-element.19.refs_2_), channel_id=1, source_target_pairs={{0,1},{1,2},{2,3},{3,4},{4,5},{5,6},{6,7},{8,9},{9,10},{10,11},{11... | collective-permute-start | bytes 393224 | tf_op jit(solution)/shard_map/ppermute | solution.py:31
  18.8 1.5 %collective-permute-start.8 = (bf16[128,512]{1,0:T(8,128)(2,1)S(1)}, bf16[128,512]{1,0:T(8,128)(2,1)S(1)}, u32[]{:S(2)}, u32[]{:S(2)}) collective-permute-start(bf16[128,512]{1,0:T(8,128)(2,1)S(1)} %shard_map.90.refs_8_), channel_id=1, source_target_pairs={{0,16},{1,17},{2,18},{3,19},{4,20},{5,21},{6,22},{7,23},{8,24},{9,... | collective-permute-start | bytes 393224 | tf_op jit(solution)/shard_map/ppermute | solution.py:36
  21.0 1.3 %collective-permute-start.6 = (bf16[128,512]{1,0:T(8,128)(2,1)S(1)}, bf16[128,512]{1,0:T(8,128)(2,1)S(1)}, u32[]{:S(2)}, u32[]{:S(2)}) collective-permute-start(bf16[128,512]{1,0:T(8,128)(2,1)S(1)} %shard_map.90.refs_8_), channel_id=1, source_target_pairs={{0,18},{1,19},{2,16},{3,17},{4,22},{5,23},{6,20},{7,21},{8,26},{9,... | collective-permute-start | bytes 393224 | tf_op jit(solution)/shard_map/ppermute | solution.py:36
  22.4 2.7 %collective-permute-done.1.refs_1_ = bf16[1024,128]{1,0:T(8,128)(2,1)S(1)} collective-permute-done((bf16[1024,128]{1,0:T(8,128)(2,1)S(1)}, bf16[1024,128]{1,0:T(8,128)(2,1)S(1)}, u32[]{:S(2)}, u32[]{:S(2)}) %collective-permute-start.1) | collective-permute-done | bytes 262176 | tf_op jit(solution)/shard_map/ppermute | solution.py:36
  25.1 2.5 %collective-permute-done.8.refs_7_ = bf16[128,512]{1,0:T(8,128)(2,1)S(1)} collective-permute-done((bf16[128,512]{1,0:T(8,128)(2,1)S(1)}, bf16[128,512]{1,0:T(8,128)(2,1)S(1)}, u32[]{:S(2)}, u32[]{:S(2)}) %collective-permute-start.8) | collective-permute-done | bytes 131104 | tf_op jit(solution)/shard_map/ppermute | solution.py:36
  27.6 1.4 %collective-permute-done.6.refs_5_ = bf16[128,512]{1,0:T(8,128)(2,1)S(1)} collective-permute-done((bf16[128,512]{1,0:T(8,128)(2,1)S(1)}, bf16[128,512]{1,0:T(8,128)(2,1)S(1)}, u32[]{:S(2)}, u32[]{:S(2)}) %collective-permute-start.6) | collective-permute-done | bytes 131104 | tf_op jit(solution)/shard_map/ppermute | solution.py:36
  29.8 1.2 %collective-permute-done.9.refs_1_ = bf16[512,256]{1,0:T(8,128)(2,1)S(1)} collective-permute-done((bf16[512,256]{1,0:T(8,128)(2,1)S(1)}, bf16[512,256]{1,0:T(8,128)(2,1)S(1)}, u32[]{:S(2)}, u32[]{:S(2)}) %collective-permute-start.9) | collective-permute-done | bytes 262176 | tf_op jit(solution)/shard_map/ppermute | solution.py:36
  31.0 3.0 %collective-permute-start.12 = (bf16[256,256]{1,0:T(8,128)(2,1)S(1)}, bf16[256,256]{1,0:T(8,128)(2,1)S(1)}, u32[]{:S(2)}, u32[]{:S(2)}) collective-permute-start(bf16[256,256]{1,0:T(8,128)(2,1)S(1)} %get-tuple-element.30), channel_id=1, source_target_pairs={{0,5},{1,4},{2,7},{3,6},{4,1},{5,0},{6,3},{7,2},{8,13},{9,12},{10,... | collective-permute-start | bytes 393224 | tf_op jit(solution)/shard_map/ppermute | solution.py:36
  36.2 1.3 %collective-permute-start.13 = (bf16[256,256]{1,0:T(8,128)(2,1)S(1)}, bf16[256,256]{1,0:T(8,128)(2,1)S(1)}, u32[]{:S(2)}, u32[]{:S(2)}) collective-permute-start(bf16[256,256]{1,0:T(8,128)(2,1)S(1)} %get-tuple-element.31), channel_id=1, source_target_pairs={{0,1},{1,0},{2,3},{3,2},{4,5},{5,4},{6,7},{7,6},{8,9},{9,8},{10,11... | collective-permute-start | bytes 393224 | tf_op jit(solution)/shard_map/ppermute | solution.py:36
  38.0 1.3 %collective-permute-start.15 = (bf16[528,128]{1,0:T(8,128)(2,1)S(1)}, bf16[528,128]{1,0:T(8,128)(2,1)S(1)}, u32[]{:S(2)}, u32[]{:S(2)}) collective-permute-start(bf16[528,128]{1,0:T(8,128)(2,1)S(1)} %get-tuple-element.37), channel_id=1, source_target_pairs={{0,16},{8,24},{16,0},{24,8},{1,17},{9,25},{17,1},{25,9},{2,18},{10... | collective-permute-start | bytes 405512 | tf_op jit(solution)/shard_map/ppermute | solution.py:36
  39.3 5.5 %collective-permute-done.12.refs_3_ = bf16[256,256]{1,0:T(8,128)(2,1)S(1)} collective-permute-done((bf16[256,256]{1,0:T(8,128)(2,1)S(1)}, bf16[256,256]{1,0:T(8,128)(2,1)S(1)}, u32[]{:S(2)}, u32[]{:S(2)}) %collective-permute-start.12) | collective-permute-done | bytes 131104 | tf_op jit(solution)/shard_map/ppermute | solution.py:36
  44.8 1.4 %collective-permute-done.11.refs_2_ = bf16[256,256]{1,0:T(8,128)(2,1)S(1)} collective-permute-done((bf16[256,256]{1,0:T(8,128)(2,1)S(1)}, bf16[256,256]{1,0:T(8,128)(2,1)S(1)}, u32[]{:S(2)}, u32[]{:S(2)}) %collective-permute-start.11) | collective-permute-done | bytes 131104 | tf_op jit(solution)/shard_map/ppermute | solution.py:36
  46.9 1.4 %collective-permute-start.21 = (bf16[256,256]{1,0:T(8,128)(2,1)S(1)}, bf16[256,256]{1,0:T(8,128)(2,1)S(1)}, u32[]{:S(2)}, u32[]{:S(2)}) collective-permute-start(bf16[256,256]{1,0:T(8,128)(2,1)S(1)} %shard_map.98.refs_0_), channel_id=1, source_target_pairs={{0,1},{1,0},{2,3},{3,2},{4,5},{5,4},{6,7},{7,6},{8,9},{9,8},{10,11... | collective-permute-start | bytes 393224 | tf_op jit(solution)/shard_map/ppermute | solution.py:36
  48.2 1.6 %collective-permute-start.20 = (bf16[256,256]{1,0:T(8,128)(2,1)S(1)}, bf16[256,256]{1,0:T(8,128)(2,1)S(1)}, u32[]{:S(2)}, u32[]{:S(2)}) collective-permute-start(bf16[256,256]{1,0:T(8,128)(2,1)S(1)} %shard_map.98.refs_0_), channel_id=1, source_target_pairs={{0,17},{1,16},{2,19},{3,18},{4,21},{5,20},{6,23},{7,22},{8,25},{9,... | collective-permute-start | bytes 393224 | tf_op jit(solution)/shard_map/ppermute | solution.py:36
  49.8 2.7 %collective-permute-done.17.refs_1_ = bf16[256,256]{1,0:T(8,128)(2,1)S(1)} collective-permute-done((bf16[256,256]{1,0:T(8,128)(2,1)S(1)}, bf16[256,256]{1,0:T(8,128)(2,1)S(1)}, u32[]{:S(2)}, u32[]{:S(2)}) %collective-permute-start.17) | collective-permute-done | bytes 131104 | tf_op jit(solution)/shard_map/ppermute | solution.py:36
  53.8 1.0 %shard_map.100 = (f32[1024,512]{1,0:T(8,128)}, f32[8,128]{1,0:T(8,128)S(1)}) custom-call(bf16[256,256]{1,0:T(8,128)(2,1)S(1)} %shard_map.98.refs_0_, bf16[256,256]{1,0:T(8,128)(2,1)S(1)} %collective-permute-done.17.refs_1_, bf16[256,256]{1,0:T(8,128)(2,1)S(1)} %collective-permute-done.18.refs_2_, bf16[256,256]{1,0:T(8,128)(2,1)S(1)} %collective-permute-done.19.refs_3_), custom_call_target="tpu_custom_call" | custom-call | flops 2000000000 | tf_op jit(solution)/shard_map/pallas_call | solution.py:58
  56.6 1.0 %shard_map.103 = f32[1024,512]{1,0:T(8,128)} custom-call(bf16[256,256]{1,0:T(8,128)(2,1)S(1)} %shard_map.101.refs_0_, bf16[256,256]{1,0:T(8,128)(2,1)S(1)} %shard_map.102.refs_1_, bf16[256,256]{1,0:T(8,128)(2,1)S(1)} %collective-permute-done.22.refs_2_, bf16[256,256]{1,0:T(8,128)(2,1)S(1)} %collective-permute-done.23.refs_3_, ...), custom_call_target="tpu_custom_call", output_to_operand_aliasing={{}: (4, {})} | custom-call | tf_op jit(solution)/shard_map/pallas_call | solution.py:58
  (45 shorter events, 9.7 us)
Async XLA Ops:
  1.6 10.0 %collective-permute-start.4 = (bf16[144,512]{1,0:T(8,128)(2,1)S(1)}, bf16[144,512]{1,0:T(8,128)(2,1)S(1)}, u32[]{:S(2)}, u32[]{:S(2)}) collective-permute-start(bf16[144,512]{1,0:T(8,128)(2,1)S(1)} %shard_map.87.refs_2_), channel_id=1, source_target_pairs={{0,1},{1,2},{2,3},{3,4},{4,5},{5,6},{6,7},{7,0},{8,9},{9,10},{10,1... | collective-permute-start | bytes 442376 | tf_op jit(solution)/shard_map/ppermute | solution.py:25
  6.2 11.8 %collective-permute-start.2 = (bf16[1024,128]{1,0:T(8,128)(2,1)S(1)}, bf16[1024,128]{1,0:T(8,128)(2,1)S(1)}, u32[]{:S(2)}, u32[]{:S(2)}) collective-permute-start(bf16[1024,128]{1,0:T(8,128)(2,1)S(1)} %get-tuple-element.21), channel_id=1, source_target_pairs={{0,2},{1,3},{2,0},{3,1},{4,6},{5,7},{6,4},{7,5},{8,10},{9,11},{10,... | collective-permute-start | bytes 786440 | tf_op jit(solution)/shard_map/ppermute | solution.py:36
  7.8 10.2 %collective-permute-start.3 = (bf16[1024,128]{1,0:T(8,128)(2,1)S(1)}, bf16[1024,128]{1,0:T(8,128)(2,1)S(1)}, u32[]{:S(2)}, u32[]{:S(2)}) collective-permute-start(bf16[1024,128]{1,0:T(8,128)(2,1)S(1)} %get-tuple-element.22), channel_id=1, source_target_pairs={{0,16},{1,17},{2,18},{3,19},{4,20},{5,21},{6,22},{7,23},{8,24},{9,... | collective-permute-start | bytes 786440 | tf_op jit(solution)/shard_map/ppermute | solution.py:36
  13.1 5.6 %collective-permute-start.5 = (bf16[128,512]{1,0:T(8,128)(2,1)S(1)}, bf16[128,512]{1,0:T(8,128)(2,1)S(1)}, u32[]{:S(2)}, u32[]{:S(2)}) collective-permute-start(bf16[128,512]{1,0:T(8,128)(2,1)S(1)} %get-tuple-element.27), channel_id=1, source_target_pairs={{0,7},{1,0},{2,1},{3,2},{4,3},{5,4},{6,5},{7,6},{8,15},{9,8},{10,9... | collective-permute-start | bytes 393224 | tf_op jit(solution)/shard_map/ppermute | solution.py:25
  14.8 10.2 %collective-permute-start.1 = (bf16[1024,128]{1,0:T(8,128)(2,1)S(1)}, bf16[1024,128]{1,0:T(8,128)(2,1)S(1)}, u32[]{:S(2)}, u32[]{:S(2)}) collective-permute-start(bf16[1024,128]{1,0:T(8,128)(2,1)S(1)} %get-tuple-element.20), channel_id=1, source_target_pairs={{0,18},{1,19},{2,16},{3,17},{4,22},{5,23},{6,20},{7,21},{8,26},{9,... | collective-permute-start | bytes 786440 | tf_op jit(solution)/shard_map/ppermute | solution.py:36
  14.8 7.5 %collective-permute-start = (bf16[128,512]{1,0:T(8,128)(2,1)S(1)}, bf16[128,512]{1,0:T(8,128)(2,1)S(1)}, u32[]{:S(2)}, u32[]{:S(2)}) collective-permute-start(bf16[128,512]{1,0:T(8,128)(2,1)S(1)} %get-tuple-element.19.refs_2_), channel_id=1, source_target_pairs={{0,1},{1,2},{2,3},{3,4},{4,5},{5,6},{6,7},{8,9},{9,10},{10,11},{11... | collective-permute-start | bytes 393224 | tf_op jit(solution)/shard_map/ppermute | solution.py:31
  18.8 8.8 %collective-permute-start.8 = (bf16[128,512]{1,0:T(8,128)(2,1)S(1)}, bf16[128,512]{1,0:T(8,128)(2,1)S(1)}, u32[]{:S(2)}, u32[]{:S(2)}) collective-permute-start(bf16[128,512]{1,0:T(8,128)(2,1)S(1)} %shard_map.90.refs_8_), channel_id=1, source_target_pairs={{0,16},{1,17},{2,18},{3,19},{4,20},{5,21},{6,22},{7,23},{8,24},{9,... | collective-permute-start | bytes 393224 | tf_op jit(solution)/shard_map/ppermute | solution.py:36
  20.4 7.2 %collective-permute-start.7 = (bf16[128,512]{1,0:T(8,128)(2,1)S(1)}, bf16[128,512]{1,0:T(8,128)(2,1)S(1)}, u32[]{:S(2)}, u32[]{:S(2)}) collective-permute-start(bf16[128,512]{1,0:T(8,128)(2,1)S(1)} %shard_map.90.refs_8_), channel_id=1, source_target_pairs={{0,2},{1,3},{2,0},{3,1},{4,6},{5,7},{6,4},{7,5},{8,10},{9,11},{10,... | collective-permute-start | bytes 393224 | tf_op jit(solution)/shard_map/ppermute | solution.py:36
  21.0 8.0 %collective-permute-start.6 = (bf16[128,512]{1,0:T(8,128)(2,1)S(1)}, bf16[128,512]{1,0:T(8,128)(2,1)S(1)}, u32[]{:S(2)}, u32[]{:S(2)}) collective-permute-start(bf16[128,512]{1,0:T(8,128)(2,1)S(1)} %shard_map.90.refs_8_), channel_id=1, source_target_pairs={{0,18},{1,19},{2,16},{3,17},{4,22},{5,23},{6,20},{7,21},{8,26},{9,... | collective-permute-start | bytes 393224 | tf_op jit(solution)/shard_map/ppermute | solution.py:36
  29.3 1.6 %collective-permute-start.9 = (bf16[512,256]{1,0:T(8,128)(2,1)S(1)}, bf16[512,256]{1,0:T(8,128)(2,1)S(1)}, u32[]{:S(2)}, u32[]{:S(2)}) collective-permute-start(bf16[512,256]{1,0:T(8,128)(2,1)S(1)} %shard_map.92), channel_id=1, source_target_pairs={{0,8},{8,0},{16,24},{24,16},{1,9},{9,1},{17,25},{25,17},{2,10},{10... | collective-permute-start | bytes 786440 | tf_op jit(solution)/shard_map/ppermute | solution.py:36
  31.0 13.8 %collective-permute-start.12 = (bf16[256,256]{1,0:T(8,128)(2,1)S(1)}, bf16[256,256]{1,0:T(8,128)(2,1)S(1)}, u32[]{:S(2)}, u32[]{:S(2)}) collective-permute-start(bf16[256,256]{1,0:T(8,128)(2,1)S(1)} %get-tuple-element.30), channel_id=1, source_target_pairs={{0,5},{1,4},{2,7},{3,6},{4,1},{5,0},{6,3},{7,2},{8,13},{9,12},{10,... | collective-permute-start | bytes 393224 | tf_op jit(solution)/shard_map/ppermute | solution.py:36
  34.0 12.2 %collective-permute-start.11 = (bf16[256,256]{1,0:T(8,128)(2,1)S(1)}, bf16[256,256]{1,0:T(8,128)(2,1)S(1)}, u32[]{:S(2)}, u32[]{:S(2)}) collective-permute-start(bf16[256,256]{1,0:T(8,128)(2,1)S(1)} %get-tuple-element.28.refs_0_), channel_id=1, source_target_pairs={{0,4},{1,5},{2,6},{3,7},{4,0},{5,1},{6,2},{7,3},{8,12},{9,13},{10,... | collective-permute-start | bytes 393224 | tf_op jit(solution)/shard_map/ppermute | solution.py:36
  34.6 1.6 %collective-permute-start.10 = (bf16[512,256]{1,0:T(8,128)(2,1)S(1)}, bf16[512,256]{1,0:T(8,128)(2,1)S(1)}, u32[]{:S(2)}, u32[]{:S(2)}) collective-permute-start(bf16[512,256]{1,0:T(8,128)(2,1)S(1)} %shard_map.96), channel_id=1, source_target_pairs={{0,8},{8,0},{16,24},{24,16},{1,9},{9,1},{17,25},{25,17},{2,10},{10... | collective-permute-start | bytes 786440 | tf_op jit(solution)/shard_map/ppermute | solution.py:36
  36.2 10.0 %collective-permute-start.13 = (bf16[256,256]{1,0:T(8,128)(2,1)S(1)}, bf16[256,256]{1,0:T(8,128)(2,1)S(1)}, u32[]{:S(2)}, u32[]{:S(2)}) collective-permute-start(bf16[256,256]{1,0:T(8,128)(2,1)S(1)} %get-tuple-element.31), channel_id=1, source_target_pairs={{0,1},{1,0},{2,3},{3,2},{4,5},{5,4},{6,7},{7,6},{8,9},{9,8},{10,11... | collective-permute-start | bytes 393224 | tf_op jit(solution)/shard_map/ppermute | solution.py:36
  37.5 10.7 %collective-permute-start.16 = (bf16[528,128]{1,0:T(8,128)(2,1)S(1)}, bf16[528,128]{1,0:T(8,128)(2,1)S(1)}, u32[]{:S(2)}, u32[]{:S(2)}) collective-permute-start(bf16[528,128]{1,0:T(8,128)(2,1)S(1)} %get-tuple-element.36), channel_id=1, source_target_pairs={{0,24},{8,16},{16,8},{24,0},{1,25},{9,17},{17,9},{25,1},{2,26},{10... | collective-permute-start | bytes 405512 | tf_op jit(solution)/shard_map/ppermute | solution.py:36
  38.0 11.9 %collective-permute-start.15 = (bf16[528,128]{1,0:T(8,128)(2,1)S(1)}, bf16[528,128]{1,0:T(8,128)(2,1)S(1)}, u32[]{:S(2)}, u32[]{:S(2)}) collective-permute-start(bf16[528,128]{1,0:T(8,128)(2,1)S(1)} %get-tuple-element.37), channel_id=1, source_target_pairs={{0,16},{8,24},{16,0},{24,8},{1,17},{9,25},{17,1},{25,9},{2,18},{10... | collective-permute-start | bytes 405512 | tf_op jit(solution)/shard_map/ppermute | solution.py:36
  44.8 7.7 %collective-permute-start.14 = (bf16[528,128]{1,0:T(8,128)(2,1)S(1)}, bf16[528,128]{1,0:T(8,128)(2,1)S(1)}, u32[]{:S(2)}, u32[]{:S(2)}) collective-permute-start(bf16[528,128]{1,0:T(8,128)(2,1)S(1)} %get-tuple-element.38), channel_id=1, source_target_pairs={{0,8},{8,0},{16,24},{24,16},{1,9},{9,1},{17,25},{25,17},{2,10},{10... | collective-permute-start | bytes 405512 | tf_op jit(solution)/shard_map/ppermute | solution.py:36
  46.3 6.2 %collective-permute-start.17 = (bf16[256,256]{1,0:T(8,128)(2,1)S(1)}, bf16[256,256]{1,0:T(8,128)(2,1)S(1)}, u32[]{:S(2)}, u32[]{:S(2)}) collective-permute-start(bf16[256,256]{1,0:T(8,128)(2,1)S(1)} %shard_map.98.refs_0_), channel_id=1, source_target_pairs={{0,16},{1,17},{2,18},{3,19},{4,20},{5,21},{6,22},{7,23},{8,24},{9,... | collective-permute-start | bytes 393224 | tf_op jit(solution)/shard_map/ppermute | solution.py:36
  46.9 8.3 %collective-permute-start.21 = (bf16[256,256]{1,0:T(8,128)(2,1)S(1)}, bf16[256,256]{1,0:T(8,128)(2,1)S(1)}, u32[]{:S(2)}, u32[]{:S(2)}) collective-permute-start(bf16[256,256]{1,0:T(8,128)(2,1)S(1)} %shard_map.98.refs_0_), channel_id=1, source_target_pairs={{0,1},{1,0},{2,3},{3,2},{4,5},{5,4},{6,7},{7,6},{8,9},{9,8},{10,11... | collective-permute-start | bytes 393224 | tf_op jit(solution)/shard_map/ppermute | solution.py:36
  48.2 6.6 %collective-permute-start.20 = (bf16[256,256]{1,0:T(8,128)(2,1)S(1)}, bf16[256,256]{1,0:T(8,128)(2,1)S(1)}, u32[]{:S(2)}, u32[]{:S(2)}) collective-permute-start(bf16[256,256]{1,0:T(8,128)(2,1)S(1)} %shard_map.98.refs_0_), channel_id=1, source_target_pairs={{0,17},{1,16},{2,19},{3,18},{4,21},{5,20},{6,23},{7,22},{8,25},{9,... | collective-permute-start | bytes 393224 | tf_op jit(solution)/shard_map/ppermute | solution.py:36
  49.8 3.6 %collective-permute-start.18 = (bf16[256,256]{1,0:T(8,128)(2,1)S(1)}, bf16[256,256]{1,0:T(8,128)(2,1)S(1)}, u32[]{:S(2)}, u32[]{:S(2)}) collective-permute-start(bf16[256,256]{1,0:T(8,128)(2,1)S(1)} %shard_map.98.refs_0_), channel_id=1, source_target_pairs={{0,8},{8,0},{16,24},{24,16},{1,9},{9,1},{17,25},{25,17},{2,10},{10... | collective-permute-start | bytes 393224 | tf_op jit(solution)/shard_map/ppermute | solution.py:36
  52.5 1.3 %collective-permute-start.19 = (bf16[256,256]{1,0:T(8,128)(2,1)S(1)}, bf16[256,256]{1,0:T(8,128)(2,1)S(1)}, u32[]{:S(2)}, u32[]{:S(2)}) collective-permute-start(bf16[256,256]{1,0:T(8,128)(2,1)S(1)} %collective-permute-done.17.refs_1_), channel_id=1, source_target_pairs={{0,8},{8,0},{16,24},{24,16},{1,9},{9,1},{17,25},{25,17},{2,10},{10... | collective-permute-start | bytes 393224 | tf_op jit(solution)/shard_map/ppermute | solution.py:36
  54.9 1.4 %collective-permute-start.22 = (bf16[256,256]{1,0:T(8,128)(2,1)S(1)}, bf16[256,256]{1,0:T(8,128)(2,1)S(1)}, u32[]{:S(2)}, u32[]{:S(2)}) collective-permute-start(bf16[256,256]{1,0:T(8,128)(2,1)S(1)} %shard_map.101.refs_0_), channel_id=1, source_target_pairs={{0,8},{8,0},{16,24},{24,16},{1,9},{9,1},{17,25},{25,17},{2,10},{10... | collective-permute-start | bytes 393224 | tf_op jit(solution)/shard_map/ppermute | solution.py:36
  55.2 1.4 %collective-permute-start.23 = (bf16[256,256]{1,0:T(8,128)(2,1)S(1)}, bf16[256,256]{1,0:T(8,128)(2,1)S(1)}, u32[]{:S(2)}, u32[]{:S(2)}) collective-permute-start(bf16[256,256]{1,0:T(8,128)(2,1)S(1)} %shard_map.102.refs_1_), channel_id=1, source_target_pairs={{0,8},{8,0},{16,24},{24,16},{1,9},{9,1},{17,25},{25,17},{2,10},{10... | collective-permute-start | bytes 393224 | tf_op jit(solution)/shard_map/ppermute | solution.py:36
  (1 other events, 4.9 us)

commit v8 on v7

--- a/solution.py
+++ b/solution.py
@@ -76,27 +76,26 @@
 
 
 def message_body(key_hbm, doc_hbm, out_ref, doc_ref, sems):
-    tokens, width = key_hbm.shape
-    copies = [
-        pltpu.make_async_copy(doc_hbm, doc_ref, sems.at[0]),
-        pltpu.make_async_copy(key_hbm, out_ref.at[pl.ds(0, tokens)], sems.at[1]),
-    ]
+    tokens = key_hbm.shape[0]
+    copies = [pltpu.make_async_copy(doc_hbm, doc_ref, sems.at[KV_HEADS])]
+    for g in range(KV_HEADS):
+        head = key_hbm.at[:, pl.ds(g * HEAD_DIM, HEAD_DIM)]
+        copies.append(pltpu.make_async_copy(head, out_ref.at[pl.ds(g * tokens, tokens)], sems.at[g]))
     for copy in copies:
         copy.start()
     copies[0].wait()
     plus = doc_ref[...] + 1
     high = plus // DOC_BASE
-    digits = jnp.concatenate([plus - high * DOC_BASE, high], 1).astype(F32)
-    digits = jnp.broadcast_to(digits, (LABEL_ROWS, 2 * tokens)).astype(BF16)
-    out_ref[tokens:, : 2 * tokens] = digits
-    if width > 2 * tokens:
-        out_ref[tokens:, 2 * tokens :] = jnp.zeros((LABEL_ROWS, width - 2 * tokens), BF16)
-    copies[1].wait()
+    row = lax.broadcasted_iota(jnp.int32, (LABEL_ROWS, tokens), 0)
+    digits = jnp.where(row == 0, plus - high * DOC_BASE, high)
+    out_ref[KV_HEADS * tokens :, :] = digits.astype(F32).astype(BF16)
+    for copy in copies[1:]:
+        copy.wait()
 
 
 def docs_of(message_ref, tokens):
-    codes = message_ref[tokens:, : 2 * tokens].astype(F32)[0:1]
-    return codes[:, :tokens] + DOC_BASE * codes[:, tokens:] - 1.0
+    codes = message_ref[KV_HEADS * tokens :, :].astype(F32)
+    return codes[0:1] + DOC_BASE * codes[1:2] - 1.0
 
 
 def column_of(row, eye):
@@ -119,10 +118,11 @@
     for g in range(KV_HEADS):
         heads = [slice((g * GROUP + r) * HEAD_DIM, (g * GROUP + r + 1) * HEAD_DIM) for r in range(GROUP)]
         col = slice(g * HEAD_DIM, (g + 1) * HEAD_DIM)
+        below = slice(g * tokens, (g + 1) * tokens)
         q4 = jnp.concatenate([q_ref[:, h] for h in heads], 0)
         g4 = jnp.concatenate([g_ref[:, h] for h in heads], 0)
-        sp = jnp.where(prior_ok, dot(prior_ref[:tokens, col], q4, ((1,), (1,))), MASKED)
-        so = jnp.where(own_ok, dot(k_ref[:tokens, col], q4, ((1,), (1,))), MASKED)
+        sp = jnp.where(prior_ok, dot(prior_ref[below, :], q4, ((1,), (1,))), MASKED)
+        so = jnp.where(own_ok, dot(k_ref[below, :], q4, ((1,), (1,))), MASKED)
         top = jnp.maximum(jnp.max(sp, 0, keepdims=True), jnp.max(so, 0, keepdims=True))
         ep = jnp.exp2((sp - top) * scale)
         eo = jnp.exp2((so - top) * scale)
@@ -304,10 +304,10 @@
 
     (message,) = call(
         message_body,
-        [shape(tokens + LABEL_ROWS, kv_width)],
+        [shape(KV_HEADS * tokens + LABEL_ROWS, HEAD_DIM)],
         [keys[0], doc_ids],
         hbm_in=(0, 1),
-        scratch=[pltpu.VMEM(doc_ids.shape, jnp.int32), pltpu.SemaphoreType.DMA((2,))],
+        scratch=[pltpu.VMEM(doc_ids.shape, jnp.int32), pltpu.SemaphoreType.DMA((KV_HEADS + 1,))],
     )
     prior = from_behind(message, shards, 1)
 

time: 57.8 us -> 57.7 us (level)
  no operation moved by 1% of the time
where the time goes in v8:
time: 57.7 us; the launch traced here: 57.4 us
  starting transfers between devices  24.8 us (43%)
  waiting for transfers between devices  21.9 us (38%)
  Pallas kernels  9.82 us (17%)
  between operations  0.83 us (1%)
    ppermute x21, waiting for transfers between devices, swap(): return lax.ppermute(value, axis, [(i, i ^ mask) for i in range(devices)])  19.1 us
    ppermute x21, starting transfers between devices, swap(): return lax.ppermute(value, axis, [(i, i ^ mask) for i in range(devices)])  17.3 us
    pallas_call x18, Pallas kernels, call(): pl.pallas_call(lambda *refs: body(*refs[skip:]), out_shape=[pltpu.HBM(o.s...  9.82 us
    ppermute x2, starting transfers between devices, from_behind(): lax.ppermute(value, axis, [(i, (i + by) % devices) for i in range(devices)])  4.71 us
    ppermute x2, waiting for transfers between devices, from_behind(): lax.ppermute(value, axis, [(i, (i + by) % devices) for i in range(devices)])  2.86 us
    ppermute x1, starting transfers between devices, open_ended(): return lax.ppermute(value, axis, pairs)  2.77 us
  transfers between devices with their start and end apart: 24, of which 13 were waited for; matrix products, arithmetic and copies ran while one was open for 0% of the time, Pallas kernels for 13%

profile of v8, /device:TPU:0, one launch (start us, length us, event | category | flops | bytes accessed | tf_op | source)
XLA Modules:
  0.0 57.4 jit_solution(15852757526299958294)
XLA Ops:
  1.5 3.0 %collective-permute-start.4 = (bf16[528,128]{1,0:T(8,128)(2,1)S(1)}, bf16[528,128]{1,0:T(8,128)(2,1)S(1)}, u32[]{:S(2)}, u32[]{:S(2)}) collective-permute-start(bf16[528,128]{1,0:T(8,128)(2,1)S(1)} %shard_map.87.refs_2_), channel_id=1, source_target_pairs={{0,1},{1,2},{2,3},{3,4},{4,5},{5,6},{6,7},{7,0},{8,9},{9,10},{10,1... | collective-permute-start | bytes 405512 | tf_op jit(solution)/shard_map/ppermute | solution.py:25
  4.5 1.6 %shard_map.86 = (bf16[1024,128]{1,0:T(8,128)(2,1)S(1)}, bf16[1024,128]{1,0:T(8,128)(2,1)S(1)}, bf16[1024,128]{1,0:T(8,128)(2,1)S(1)}, bf16[1024,128]{1,0:T(8,128...) custom-call(bf16[128,4096]{1,0:T(8,128)(2,1)} %bitcast.16, ...), custom_call_target="tpu_custom_call" | custom-call | tf_op jit(solution)/shard_map/pallas_call | solution.py:58
  6.1 1.6 %collective-permute-start.2 = (bf16[1024,128]{1,0:T(8,128)(2,1)S(1)}, bf16[1024,128]{1,0:T(8,128)(2,1)S(1)}, u32[]{:S(2)}, u32[]{:S(2)}) collective-permute-start(bf16[1024,128]{1,0:T(8,128)(2,1)S(1)} %get-tuple-element.21), channel_id=1, source_target_pairs={{0,2},{1,3},{2,0},{3,1},{4,6},{5,7},{6,4},{7,5},{8,10},{9,11},{10,... | collective-permute-start | bytes 786440 | tf_op jit(solution)/shard_map/ppermute | solution.py:36
  7.8 1.5 %collective-permute-start.3 = (bf16[1024,128]{1,0:T(8,128)(2,1)S(1)}, bf16[1024,128]{1,0:T(8,128)(2,1)S(1)}, u32[]{:S(2)}, u32[]{:S(2)}) collective-permute-start(bf16[1024,128]{1,0:T(8,128)(2,1)S(1)} %get-tuple-element.22), channel_id=1, source_target_pairs={{0,16},{1,17},{2,18},{3,19},{4,20},{5,21},{6,22},{7,23},{8,24},{9,... | collective-permute-start | bytes 786440 | tf_op jit(solution)/shard_map/ppermute | solution.py:36
  9.3 2.0 %collective-permute-done.4.refs_3_ = bf16[528,128]{1,0:T(8,128)(2,1)S(1)} collective-permute-done((bf16[528,128]{1,0:T(8,128)(2,1)S(1)}, bf16[528,128]{1,0:T(8,128)(2,1)S(1)}, u32[]{:S(2)}, u32[]{:S(2)}) %collective-permute-start.4) | collective-permute-done | bytes 135200 | tf_op jit(solution)/shard_map/ppermute | solution.py:25
  11.3 1.6 %shard_map.88 = (bf16[4,256,512]{2,1,0:T(8,128)(2,1)S(1)}, bf16[128,512]{1,0:T(8,128)(2,1)S(1)}) custom-call(bf16[128,2048]{1,0:T(8,128)(2,1)S(1)} %get-tuple-element.24.refs_0_, bf16[128,2048]{1,0:T(8,128)(2,1)S(1)} %get-tuple-element.25.refs_1_, bf16[528,128]{1,0:T(8,128)(2,1)S(1)} %shard_map.87.refs_2_, bf16[528,128]{1,0:T(8,128)(2,1)S(1)} %collective-permute-done.4.refs_3_), custom_call_target="tpu_custom_call" | custom-call | flops 99999997952 | tf_op jit(solution)/shard_map/pallas_call | solution.py:58
  12.8 1.7 %collective-permute-start.5 = (bf16[128,512]{1,0:T(8,128)(2,1)S(1)}, bf16[128,512]{1,0:T(8,128)(2,1)S(1)}, u32[]{:S(2)}, u32[]{:S(2)}) collective-permute-start(bf16[128,512]{1,0:T(8,128)(2,1)S(1)} %get-tuple-element.27), channel_id=1, source_target_pairs={{0,7},{1,0},{2,1},{3,2},{4,3},{5,4},{6,5},{7,6},{8,15},{9,8},{10,9... | collective-permute-start | bytes 393224 | tf_op jit(solution)/shard_map/ppermute | solution.py:25
  14.5 2.8 %collective-permute-start = (bf16[128,512]{1,0:T(8,128)(2,1)S(1)}, bf16[128,512]{1,0:T(8,128)(2,1)S(1)}, u32[]{:S(2)}, u32[]{:S(2)}) collective-permute-start(bf16[128,512]{1,0:T(8,128)(2,1)S(1)} %get-tuple-element.19.refs_2_), channel_id=1, source_target_pairs={{0,1},{1,2},{2,3},{3,4},{4,5},{5,6},{6,7},{8,9},{9,10},{10,11},{11... | collective-permute-start | bytes 393224 | tf_op jit(solution)/shard_map/ppermute | solution.py:31
  18.5 1.6 %collective-permute-start.8 = (bf16[128,512]{1,0:T(8,128)(2,1)S(1)}, bf16[128,512]{1,0:T(8,128)(2,1)S(1)}, u32[]{:S(2)}, u32[]{:S(2)}) collective-permute-start(bf16[128,512]{1,0:T(8,128)(2,1)S(1)} %shard_map.90.refs_8_), channel_id=1, source_target_pairs={{0,16},{1,17},{2,18},{3,19},{4,20},{5,21},{6,22},{7,23},{8,24},{9,... | collective-permute-start | bytes 393224 | tf_op jit(solution)/shard_map/ppermute | solution.py:36
  20.7 1.3 %collective-permute-start.6 = (bf16[128,512]{1,0:T(8,128)(2,1)S(1)}, bf16[128,512]{1,0:T(8,128)(2,1)S(1)}, u32[]{:S(2)}, u32[]{:S(2)}) collective-permute-start(bf16[128,512]{1,0:T(8,128)(2,1)S(1)} %shard_map.90.refs_8_), channel_id=1, source_target_pairs={{0,18},{1,19},{2,16},{3,17},{4,22},{5,23},{6,20},{7,21},{8,26},{9,... | collective-permute-start | bytes 393224 | tf_op jit(solution)/shard_map/ppermute | solution.py:36
  22.1 2.6 %collective-permute-done.1.refs_1_ = bf16[1024,128]{1,0:T(8,128)(2,1)S(1)} collective-permute-done((bf16[1024,128]{1,0:T(8,128)(2,1)S(1)}, bf16[1024,128]{1,0:T(8,128)(2,1)S(1)}, u32[]{:S(2)}, u32[]{:S(2)}) %collective-permute-start.1) | collective-permute-done | bytes 262176 | tf_op jit(solution)/shard_map/ppermute | solution.py:36
  24.7 2.7 %collective-permute-done.8.refs_7_ = bf16[128,512]{1,0:T(8,128)(2,1)S(1)} collective-permute-done((bf16[128,512]{1,0:T(8,128)(2,1)S(1)}, bf16[128,512]{1,0:T(8,128)(2,1)S(1)}, u32[]{:S(2)}, u32[]{:S(2)}) %collective-permute-start.8) | collective-permute-done | bytes 131104 | tf_op jit(solution)/shard_map/ppermute | solution.py:36
  27.4 1.6 %collective-permute-done.6.refs_5_ = bf16[128,512]{1,0:T(8,128)(2,1)S(1)} collective-permute-done((bf16[128,512]{1,0:T(8,128)(2,1)S(1)}, bf16[128,512]{1,0:T(8,128)(2,1)S(1)}, u32[]{:S(2)}, u32[]{:S(2)}) %collective-permute-start.6) | collective-permute-done | bytes 131104 | tf_op jit(solution)/shard_map/ppermute | solution.py:36
  29.7 1.2 %collective-permute-done.9.refs_1_ = bf16[512,256]{1,0:T(8,128)(2,1)S(1)} collective-permute-done((bf16[512,256]{1,0:T(8,128)(2,1)S(1)}, bf16[512,256]{1,0:T(8,128)(2,1)S(1)}, u32[]{:S(2)}, u32[]{:S(2)}) %collective-permute-start.9) | collective-permute-done | bytes 262176 | tf_op jit(solution)/shard_map/ppermute | solution.py:36
  30.9 2.8 %collective-permute-start.12 = (bf16[256,256]{1,0:T(8,128)(2,1)S(1)}, bf16[256,256]{1,0:T(8,128)(2,1)S(1)}, u32[]{:S(2)}, u32[]{:S(2)}) collective-permute-start(bf16[256,256]{1,0:T(8,128)(2,1)S(1)} %get-tuple-element.30), channel_id=1, source_target_pairs={{0,5},{1,4},{2,7},{3,6},{4,1},{5,0},{6,3},{7,2},{8,13},{9,12},{10,... | collective-permute-start | bytes 393224 | tf_op jit(solution)/shard_map/ppermute | solution.py:36
  36.1 1.4 %collective-permute-start.13 = (bf16[256,256]{1,0:T(8,128)(2,1)S(1)}, bf16[256,256]{1,0:T(8,128)(2,1)S(1)}, u32[]{:S(2)}, u32[]{:S(2)}) collective-permute-start(bf16[256,256]{1,0:T(8,128)(2,1)S(1)} %get-tuple-element.31), channel_id=1, source_target_pairs={{0,1},{1,0},{2,3},{3,2},{4,5},{5,4},{6,7},{7,6},{8,9},{9,8},{10,11... | collective-permute-start | bytes 393224 | tf_op jit(solution)/shard_map/ppermute | solution.py:36
  37.8 1.5 %collective-permute-start.15 = (bf16[528,128]{1,0:T(8,128)(2,1)S(1)}, bf16[528,128]{1,0:T(8,128)(2,1)S(1)}, u32[]{:S(2)}, u32[]{:S(2)}) collective-permute-start(bf16[528,128]{1,0:T(8,128)(2,1)S(1)} %get-tuple-element.37), channel_id=1, source_target_pairs={{0,16},{8,24},{16,0},{24,8},{1,17},{9,25},{17,1},{25,9},{2,18},{10... | collective-permute-start | bytes 405512 | tf_op jit(solution)/shard_map/ppermute | solution.py:36
  39.2 5.5 %collective-permute-done.12.refs_3_ = bf16[256,256]{1,0:T(8,128)(2,1)S(1)} collective-permute-done((bf16[256,256]{1,0:T(8,128)(2,1)S(1)}, bf16[256,256]{1,0:T(8,128)(2,1)S(1)}, u32[]{:S(2)}, u32[]{:S(2)}) %collective-permute-start.12) | collective-permute-done | bytes 131104 | tf_op jit(solution)/shard_map/ppermute | solution.py:36
  44.8 1.3 %collective-permute-done.11.refs_2_ = bf16[256,256]{1,0:T(8,128)(2,1)S(1)} collective-permute-done((bf16[256,256]{1,0:T(8,128)(2,1)S(1)}, bf16[256,256]{1,0:T(8,128)(2,1)S(1)}, u32[]{:S(2)}, u32[]{:S(2)}) %collective-permute-start.11) | collective-permute-done | bytes 131104 | tf_op jit(solution)/shard_map/ppermute | solution.py:36
  46.6 1.5 %collective-permute-start.21 = (bf16[256,256]{1,0:T(8,128)(2,1)S(1)}, bf16[256,256]{1,0:T(8,128)(2,1)S(1)}, u32[]{:S(2)}, u32[]{:S(2)}) collective-permute-start(bf16[256,256]{1,0:T(8,128)(2,1)S(1)} %shard_map.98.refs_0_), channel_id=1, source_target_pairs={{0,1},{1,0},{2,3},{3,2},{4,5},{5,4},{6,7},{7,6},{8,9},{9,8},{10,11... | collective-permute-start | bytes 393224 | tf_op jit(solution)/shard_map/ppermute | solution.py:36
  48.1 1.6 %collective-permute-start.20 = (bf16[256,256]{1,0:T(8,128)(2,1)S(1)}, bf16[256,256]{1,0:T(8,128)(2,1)S(1)}, u32[]{:S(2)}, u32[]{:S(2)}) collective-permute-start(bf16[256,256]{1,0:T(8,128)(2,1)S(1)} %shard_map.98.refs_0_), channel_id=1, source_target_pairs={{0,17},{1,16},{2,19},{3,18},{4,21},{5,20},{6,23},{7,22},{8,25},{9,... | collective-permute-start | bytes 393224 | tf_op jit(solution)/shard_map/ppermute | solution.py:36
  49.7 2.6 %collective-permute-done.17.refs_1_ = bf16[256,256]{1,0:T(8,128)(2,1)S(1)} collective-permute-done((bf16[256,256]{1,0:T(8,128)(2,1)S(1)}, bf16[256,256]{1,0:T(8,128)(2,1)S(1)}, u32[]{:S(2)}, u32[]{:S(2)}) %collective-permute-start.17) | collective-permute-done | bytes 131104 | tf_op jit(solution)/shard_map/ppermute | solution.py:36
  53.7 1.0 %shard_map.100 = (f32[1024,512]{1,0:T(8,128)}, f32[8,128]{1,0:T(8,128)S(1)}) custom-call(bf16[256,256]{1,0:T(8,128)(2,1)S(1)} %shard_map.98.refs_0_, bf16[256,256]{1,0:T(8,128)(2,1)S(1)} %collective-permute-done.17.refs_1_, bf16[256,256]{1,0:T(8,128)(2,1)S(1)} %collective-permute-done.18.refs_2_, bf16[256,256]{1,0:T(8,128)(2,1)S(1)} %collective-permute-done.19.refs_3_), custom_call_target="tpu_custom_call" | custom-call | flops 2000000000 | tf_op jit(solution)/shard_map/pallas_call | solution.py:58
  56.4 1.0 %shard_map.103 = f32[1024,512]{1,0:T(8,128)} custom-call(bf16[256,256]{1,0:T(8,128)(2,1)S(1)} %shard_map.101.refs_0_, bf16[256,256]{1,0:T(8,128)(2,1)S(1)} %shard_map.102.refs_1_, bf16[256,256]{1,0:T(8,128)(2,1)S(1)} %collective-permute-done.22.refs_2_, bf16[256,256]{1,0:T(8,128)(2,1)S(1)} %collective-permute-done.23.refs_3_, ...), custom_call_target="tpu_custom_call", output_to_operand_aliasing={{}: (4, {})} | custom-call | tf_op jit(solution)/shard_map/pallas_call | solution.py:58
  (45 shorter events, 9.7 us)
Async XLA Ops:
  1.5 9.7 %collective-permute-start.4 = (bf16[528,128]{1,0:T(8,128)(2,1)S(1)}, bf16[528,128]{1,0:T(8,128)(2,1)S(1)}, u32[]{:S(2)}, u32[]{:S(2)}) collective-permute-start(bf16[528,128]{1,0:T(8,128)(2,1)S(1)} %shard_map.87.refs_2_), channel_id=1, source_target_pairs={{0,1},{1,2},{2,3},{3,4},{4,5},{5,6},{6,7},{7,0},{8,9},{9,10},{10,1... | collective-permute-start | bytes 405512 | tf_op jit(solution)/shard_map/ppermute | solution.py:25
  6.1 11.5 %collective-permute-start.2 = (bf16[1024,128]{1,0:T(8,128)(2,1)S(1)}, bf16[1024,128]{1,0:T(8,128)(2,1)S(1)}, u32[]{:S(2)}, u32[]{:S(2)}) collective-permute-start(bf16[1024,128]{1,0:T(8,128)(2,1)S(1)} %get-tuple-element.21), channel_id=1, source_target_pairs={{0,2},{1,3},{2,0},{3,1},{4,6},{5,7},{6,4},{7,5},{8,10},{9,11},{10,... | collective-permute-start | bytes 786440 | tf_op jit(solution)/shard_map/ppermute | solution.py:36
  7.8 9.8 %collective-permute-start.3 = (bf16[1024,128]{1,0:T(8,128)(2,1)S(1)}, bf16[1024,128]{1,0:T(8,128)(2,1)S(1)}, u32[]{:S(2)}, u32[]{:S(2)}) collective-permute-start(bf16[1024,128]{1,0:T(8,128)(2,1)S(1)} %get-tuple-element.22), channel_id=1, source_target_pairs={{0,16},{1,17},{2,18},{3,19},{4,20},{5,21},{6,22},{7,23},{8,24},{9,... | collective-permute-start | bytes 786440 | tf_op jit(solution)/shard_map/ppermute | solution.py:36
  12.8 5.6 %collective-permute-start.5 = (bf16[128,512]{1,0:T(8,128)(2,1)S(1)}, bf16[128,512]{1,0:T(8,128)(2,1)S(1)}, u32[]{:S(2)}, u32[]{:S(2)}) collective-permute-start(bf16[128,512]{1,0:T(8,128)(2,1)S(1)} %get-tuple-element.27), channel_id=1, source_target_pairs={{0,7},{1,0},{2,1},{3,2},{4,3},{5,4},{6,5},{7,6},{8,15},{9,8},{10,9... | collective-permute-start | bytes 393224 | tf_op jit(solution)/shard_map/ppermute | solution.py:25
  14.5 10.2 %collective-permute-start.1 = (bf16[1024,128]{1,0:T(8,128)(2,1)S(1)}, bf16[1024,128]{1,0:T(8,128)(2,1)S(1)}, u32[]{:S(2)}, u32[]{:S(2)}) collective-permute-start(bf16[1024,128]{1,0:T(8,128)(2,1)S(1)} %get-tuple-element.20), channel_id=1, source_target_pairs={{0,18},{1,19},{2,16},{3,17},{4,22},{5,23},{6,20},{7,21},{8,26},{9,... | collective-permute-start | bytes 786440 | tf_op jit(solution)/shard_map/ppermute | solution.py:36
  14.5 7.5 %collective-permute-start = (bf16[128,512]{1,0:T(8,128)(2,1)S(1)}, bf16[128,512]{1,0:T(8,128)(2,1)S(1)}, u32[]{:S(2)}, u32[]{:S(2)}) collective-permute-start(bf16[128,512]{1,0:T(8,128)(2,1)S(1)} %get-tuple-element.19.refs_2_), channel_id=1, source_target_pairs={{0,1},{1,2},{2,3},{3,4},{4,5},{5,6},{6,7},{8,9},{9,10},{10,11},{11... | collective-permute-start | bytes 393224 | tf_op jit(solution)/shard_map/ppermute | solution.py:31
  18.5 8.9 %collective-permute-start.8 = (bf16[128,512]{1,0:T(8,128)(2,1)S(1)}, bf16[128,512]{1,0:T(8,128)(2,1)S(1)}, u32[]{:S(2)}, u32[]{:S(2)}) collective-permute-start(bf16[128,512]{1,0:T(8,128)(2,1)S(1)} %shard_map.90.refs_8_), channel_id=1, source_target_pairs={{0,16},{1,17},{2,18},{3,19},{4,20},{5,21},{6,22},{7,23},{8,24},{9,... | collective-permute-start | bytes 393224 | tf_op jit(solution)/shard_map/ppermute | solution.py:36
  20.1 7.3 %collective-permute-start.7 = (bf16[128,512]{1,0:T(8,128)(2,1)S(1)}, bf16[128,512]{1,0:T(8,128)(2,1)S(1)}, u32[]{:S(2)}, u32[]{:S(2)}) collective-permute-start(bf16[128,512]{1,0:T(8,128)(2,1)S(1)} %shard_map.90.refs_8_), channel_id=1, source_target_pairs={{0,2},{1,3},{2,0},{3,1},{4,6},{5,7},{6,4},{7,5},{8,10},{9,11},{10,... | collective-permute-start | bytes 393224 | tf_op jit(solution)/shard_map/ppermute | solution.py:36
  20.7 8.2 %collective-permute-start.6 = (bf16[128,512]{1,0:T(8,128)(2,1)S(1)}, bf16[128,512]{1,0:T(8,128)(2,1)S(1)}, u32[]{:S(2)}, u32[]{:S(2)}) collective-permute-start(bf16[128,512]{1,0:T(8,128)(2,1)S(1)} %shard_map.90.refs_8_), channel_id=1, source_target_pairs={{0,18},{1,19},{2,16},{3,17},{4,22},{5,23},{6,20},{7,21},{8,26},{9,... | collective-permute-start | bytes 393224 | tf_op jit(solution)/shard_map/ppermute | solution.py:36
  29.3 1.6 %collective-permute-start.9 = (bf16[512,256]{1,0:T(8,128)(2,1)S(1)}, bf16[512,256]{1,0:T(8,128)(2,1)S(1)}, u32[]{:S(2)}, u32[]{:S(2)}) collective-permute-start(bf16[512,256]{1,0:T(8,128)(2,1)S(1)} %shard_map.92), channel_id=1, source_target_pairs={{0,8},{8,0},{16,24},{24,16},{1,9},{9,1},{17,25},{25,17},{2,10},{10... | collective-permute-start | bytes 786440 | tf_op jit(solution)/shard_map/ppermute | solution.py:36
  30.9 13.8 %collective-permute-start.12 = (bf16[256,256]{1,0:T(8,128)(2,1)S(1)}, bf16[256,256]{1,0:T(8,128)(2,1)S(1)}, u32[]{:S(2)}, u32[]{:S(2)}) collective-permute-start(bf16[256,256]{1,0:T(8,128)(2,1)S(1)} %get-tuple-element.30), channel_id=1, source_target_pairs={{0,5},{1,4},{2,7},{3,6},{4,1},{5,0},{6,3},{7,2},{8,13},{9,12},{10,... | collective-permute-start | bytes 393224 | tf_op jit(solution)/shard_map/ppermute | solution.py:36
  33.7 12.3 %collective-permute-start.11 = (bf16[256,256]{1,0:T(8,128)(2,1)S(1)}, bf16[256,256]{1,0:T(8,128)(2,1)S(1)}, u32[]{:S(2)}, u32[]{:S(2)}) collective-permute-start(bf16[256,256]{1,0:T(8,128)(2,1)S(1)} %get-tuple-element.28.refs_0_), channel_id=1, source_target_pairs={{0,4},{1,5},{2,6},{3,7},{4,0},{5,1},{6,2},{7,3},{8,12},{9,13},{10,... | collective-permute-start | bytes 393224 | tf_op jit(solution)/shard_map/ppermute | solution.py:36
  34.4 1.6 %collective-permute-start.10 = (bf16[512,256]{1,0:T(8,128)(2,1)S(1)}, bf16[512,256]{1,0:T(8,128)(2,1)S(1)}, u32[]{:S(2)}, u32[]{:S(2)}) collective-permute-start(bf16[512,256]{1,0:T(8,128)(2,1)S(1)} %shard_map.96), channel_id=1, source_target_pairs={{0,8},{8,0},{16,24},{24,16},{1,9},{9,1},{17,25},{25,17},{2,10},{10... | collective-permute-start | bytes 786440 | tf_op jit(solution)/shard_map/ppermute | solution.py:36
  36.1 10.0 %collective-permute-start.13 = (bf16[256,256]{1,0:T(8,128)(2,1)S(1)}, bf16[256,256]{1,0:T(8,128)(2,1)S(1)}, u32[]{:S(2)}, u32[]{:S(2)}) collective-permute-start(bf16[256,256]{1,0:T(8,128)(2,1)S(1)} %get-tuple-element.31), channel_id=1, source_target_pairs={{0,1},{1,0},{2,3},{3,2},{4,5},{5,4},{6,7},{7,6},{8,9},{9,8},{10,11... | collective-permute-start | bytes 393224 | tf_op jit(solution)/shard_map/ppermute | solution.py:36
  37.5 10.6 %collective-permute-start.16 = (bf16[528,128]{1,0:T(8,128)(2,1)S(1)}, bf16[528,128]{1,0:T(8,128)(2,1)S(1)}, u32[]{:S(2)}, u32[]{:S(2)}) collective-permute-start(bf16[528,128]{1,0:T(8,128)(2,1)S(1)} %get-tuple-element.36), channel_id=1, source_target_pairs={{0,24},{8,16},{16,8},{24,0},{1,25},{9,17},{17,9},{25,1},{2,26},{10... | collective-permute-start | bytes 405512 | tf_op jit(solution)/shard_map/ppermute | solution.py:36
  37.8 11.9 %collective-permute-start.15 = (bf16[528,128]{1,0:T(8,128)(2,1)S(1)}, bf16[528,128]{1,0:T(8,128)(2,1)S(1)}, u32[]{:S(2)}, u32[]{:S(2)}) collective-permute-start(bf16[528,128]{1,0:T(8,128)(2,1)S(1)} %get-tuple-element.37), channel_id=1, source_target_pairs={{0,16},{8,24},{16,0},{24,8},{1,17},{9,25},{17,1},{25,9},{2,18},{10... | collective-permute-start | bytes 405512 | tf_op jit(solution)/shard_map/ppermute | solution.py:36
  44.8 7.5 %collective-permute-start.14 = (bf16[528,128]{1,0:T(8,128)(2,1)S(1)}, bf16[528,128]{1,0:T(8,128)(2,1)S(1)}, u32[]{:S(2)}, u32[]{:S(2)}) collective-permute-start(bf16[528,128]{1,0:T(8,128)(2,1)S(1)} %get-tuple-element.38), channel_id=1, source_target_pairs={{0,8},{8,0},{16,24},{24,16},{1,9},{9,1},{17,25},{25,17},{2,10},{10... | collective-permute-start | bytes 405512 | tf_op jit(solution)/shard_map/ppermute | solution.py:36
  46.1 6.2 %collective-permute-start.17 = (bf16[256,256]{1,0:T(8,128)(2,1)S(1)}, bf16[256,256]{1,0:T(8,128)(2,1)S(1)}, u32[]{:S(2)}, u32[]{:S(2)}) collective-permute-start(bf16[256,256]{1,0:T(8,128)(2,1)S(1)} %shard_map.98.refs_0_), channel_id=1, source_target_pairs={{0,16},{1,17},{2,18},{3,19},{4,20},{5,21},{6,22},{7,23},{8,24},{9,... | collective-permute-start | bytes 393224 | tf_op jit(solution)/shard_map/ppermute | solution.py:36
  46.6 8.4 %collective-permute-start.21 = (bf16[256,256]{1,0:T(8,128)(2,1)S(1)}, bf16[256,256]{1,0:T(8,128)(2,1)S(1)}, u32[]{:S(2)}, u32[]{:S(2)}) collective-permute-start(bf16[256,256]{1,0:T(8,128)(2,1)S(1)} %shard_map.98.refs_0_), channel_id=1, source_target_pairs={{0,1},{1,0},{2,3},{3,2},{4,5},{5,4},{6,7},{7,6},{8,9},{9,8},{10,11... | collective-permute-start | bytes 393224 | tf_op jit(solution)/shard_map/ppermute | solution.py:36
  48.1 6.6 %collective-permute-start.20 = (bf16[256,256]{1,0:T(8,128)(2,1)S(1)}, bf16[256,256]{1,0:T(8,128)(2,1)S(1)}, u32[]{:S(2)}, u32[]{:S(2)}) collective-permute-start(bf16[256,256]{1,0:T(8,128)(2,1)S(1)} %shard_map.98.refs_0_), channel_id=1, source_target_pairs={{0,17},{1,16},{2,19},{3,18},{4,21},{5,20},{6,23},{7,22},{8,25},{9,... | collective-permute-start | bytes 393224 | tf_op jit(solution)/shard_map/ppermute | solution.py:36
  49.7 3.6 %collective-permute-start.18 = (bf16[256,256]{1,0:T(8,128)(2,1)S(1)}, bf16[256,256]{1,0:T(8,128)(2,1)S(1)}, u32[]{:S(2)}, u32[]{:S(2)}) collective-permute-start(bf16[256,256]{1,0:T(8,128)(2,1)S(1)} %shard_map.98.refs_0_), channel_id=1, source_target_pairs={{0,8},{8,0},{16,24},{24,16},{1,9},{9,1},{17,25},{25,17},{2,10},{10... | collective-permute-start | bytes 393224 | tf_op jit(solution)/shard_map/ppermute | solution.py:36
  52.3 1.3 %collective-permute-start.19 = (bf16[256,256]{1,0:T(8,128)(2,1)S(1)}, bf16[256,256]{1,0:T(8,128)(2,1)S(1)}, u32[]{:S(2)}, u32[]{:S(2)}) collective-permute-start(bf16[256,256]{1,0:T(8,128)(2,1)S(1)} %collective-permute-done.17.refs_1_), channel_id=1, source_target_pairs={{0,8},{8,0},{16,24},{24,16},{1,9},{9,1},{17,25},{25,17},{2,10},{10... | collective-permute-start | bytes 393224 | tf_op jit(solution)/shard_map/ppermute | solution.py:36
  54.7 1.4 %collective-permute-start.22 = (bf16[256,256]{1,0:T(8,128)(2,1)S(1)}, bf16[256,256]{1,0:T(8,128)(2,1)S(1)}, u32[]{:S(2)}, u32[]{:S(2)}) collective-permute-start(bf16[256,256]{1,0:T(8,128)(2,1)S(1)} %shard_map.101.refs_0_), channel_id=1, source_target_pairs={{0,8},{8,0},{16,24},{24,16},{1,9},{9,1},{17,25},{25,17},{2,10},{10... | collective-permute-start | bytes 393224 | tf_op jit(solution)/shard_map/ppermute | solution.py:36
  55.0 1.4 %collective-permute-start.23 = (bf16[256,256]{1,0:T(8,128)(2,1)S(1)}, bf16[256,256]{1,0:T(8,128)(2,1)S(1)}, u32[]{:S(2)}, u32[]{:S(2)}) collective-permute-start(bf16[256,256]{1,0:T(8,128)(2,1)S(1)} %shard_map.102.refs_1_), channel_id=1, source_target_pairs={{0,8},{8,0},{16,24},{24,16},{1,9},{9,1},{17,25},{25,17},{2,10},{10... | collective-permute-start | bytes 393224 | tf_op jit(solution)/shard_map/ppermute | solution.py:36
  (1 other events, 4.8 us)
